TPU v7x, 32 devices: a whole 2x2x4 slice. The times are simulated.
32 devices in a mesh: ctx: 8 (over y, x, core), head: 4 (over z).
Axes of the slice: x: 2, y: 2, z: 4, core: 2. Of those that a mesh axis runs over, the one named last changes fastest.
Arguments:
- queries: bfloat16 [4096, 2048], P(('ctx', 'head')), may hold values from -5.5 to 5.5
- key_vecs: bfloat16 [4096, 2048], P(('ctx', 'head')), may hold values from -5.5 to 5.5
- value_vecs: bfloat16 [4096, 2048], P(('ctx', 'head')), may hold values from -6 to 6
- out_grads: bfloat16 [4096, 2048], P(('ctx', 'head')), may hold values from -6 to 6
- local_offsets: int32 [32, 2], P('ctx'), may hold values from 0 to 3, as said below
- partner_pool: int32 [8, 2, 3], replicated, may hold values from 0 to 3, as said below
- partner_picks: int32 [32, 2, 2], P('ctx'), may hold values from 0 to 2, as said below
Outputs:
- query_grads: bfloat16 [4096, 2048], P(('ctx', 'head'))
- key_grads: bfloat16 [4096, 2048], P(('ctx', 'head'))
- value_grads: bfloat16 [4096, 2048], P(('ctx', 'head'))
Inputs may be any that keep to these rules, and one draw needn't show every extreme that they name: `local_offsets`: each row holds 2 distinct offsets. `partner_pool`: each row of 3 entries names distinct blocks. `partner_picks`: each row of 2 entries holds distinct positions.
All inputs are finite; a program needn't handle non-finite values.
Results may differ from a plain program's by a relative error of at most 0.0069.
Values may be sent and summed in bfloat16 or wider, within the bound.
No kernel may reach another device: no remote copies, remote signals or barrier semaphores. Data moves between devices by JAX's collectives and lax.ppermute only.
A program may use at most 64 MiB of HBM per device.

v0:
```python
import jax
import jax.numpy as jnp
from jax import lax
from jax.sharding import PartitionSpec as P

DH = 128
BLK = 128


def swapped(value, axis, distance):
    return lax.ppermute(value, axis, [(i, i ^ 1 << distance) for i in range(lax.axis_size(axis))])


def per_device(
    queries, key_vecs, value_vecs, out_grads, local_offsets, partner_pool, partner_picks
):
    query_heads, key_heads, value_heads, grad_heads = (
        lax.all_to_all(queries, "head", split_axis=1, concat_axis=0, tiled=True),
        lax.all_to_all(key_vecs, "head", split_axis=1, concat_axis=0, tiled=True),
        lax.all_to_all(value_vecs, "head", split_axis=1, concat_axis=0, tiled=True),
        lax.all_to_all(out_grads, "head", split_axis=1, concat_axis=0, tiled=True),
    )
    feat_width = query_heads.shape[1]
    heads_local = feat_width // DH
    blocks = query_heads.shape[0] // BLK
    bit_count = partner_pool.shape[1]
    pool_size = partner_pool.shape[2]
    group_id = lax.axis_index("ctx")
    key_blocks = key_heads.reshape(blocks, BLK, feat_width)
    value_blocks = value_heads.reshape(blocks, BLK, feat_width)
    bit_order = list(range(bit_count))
    remote_keys = [None] * bit_count
    remote_values = [None] * bit_count
    for bit_num in bit_order:
        asked_idx = partner_pool[jnp.bitwise_xor(group_id, 1 << bit_num), bit_num]
        far_keys, far_values = swapped(
            (key_blocks[asked_idx], value_blocks[asked_idx]), "ctx", bit_num
        )
        remote_keys[bit_num] = far_keys
        remote_values[bit_num] = far_values
    key_table = jnp.concatenate([key_blocks] + remote_keys, axis=0)
    value_table = jnp.concatenate([value_blocks] + remote_values, axis=0)
    table_rows = key_table.shape[0]
    inner_idx = jnp.arange(blocks, dtype=jnp.int32)
    local_idx = (inner_idx[:, None] + local_offsets) % blocks
    remote_idx = (
        blocks + jnp.arange(bit_count, dtype=jnp.int32)[None, :, None] * pool_size + partner_picks
    )
    key_index = jnp.concatenate([local_idx, remote_idx.reshape(blocks, -1)], axis=1)
    key_count = key_index.shape[1]
    group_size = min(2, blocks)
    steps_total = blocks // group_size
    softmax_scale = DH ** (-0.5)
    query_blocks = query_heads.reshape(blocks, BLK, heads_local, DH)
    grad_blocks = grad_heads.reshape(blocks, BLK, heads_local, DH)

    def attend(carry_in, step_id):
        acc_key, acc_value = carry_in
        first_row = step_id * group_size
        query_part = lax.dynamic_slice_in_dim(query_blocks, first_row, group_size)
        grad_part = lax.dynamic_slice_in_dim(grad_blocks, first_row, group_size)
        chosen = lax.dynamic_slice_in_dim(key_index, first_row, group_size)
        key_part = key_table[chosen].reshape(group_size, key_count * BLK, heads_local, DH)
        value_part = value_table[chosen].reshape(group_size, key_count * BLK, heads_local, DH)
        scores = (
            jnp.einsum("gqhd,gkhd->ghqk", query_part, key_part, preferred_element_type=jnp.float32)
            * softmax_scale
        )
        row_max = jnp.max(scores, axis=-1, keepdims=True)
        exp_scores = jnp.exp(scores - row_max)
        weights = exp_scores / jnp.sum(exp_scores, axis=-1, keepdims=True)
        prob_grad = jnp.einsum(
            "gqhd,gkhd->ghqk", grad_part, value_part, preferred_element_type=jnp.float32
        )
        row_delta = jnp.sum(weights * prob_grad, axis=-1, keepdims=True)
        score_grad = (softmax_scale * weights * (prob_grad - row_delta)).astype(jnp.bfloat16)
        weights_half = weights.astype(jnp.bfloat16)
        query_out = jnp.einsum(
            "ghqk,gkhd->gqhd", score_grad, key_part, preferred_element_type=jnp.float32
        )
        key_out = jnp.einsum(
            "ghqk,gqhd->gkhd", score_grad, query_part, preferred_element_type=jnp.float32
        )
        value_out = jnp.einsum(
            "ghqk,gqhd->gkhd", weights_half, grad_part, preferred_element_type=jnp.float32
        )
        flat_index = chosen.reshape(-1)
        acc_key = acc_key.at[flat_index].add(
            key_out.reshape(group_size * key_count, BLK, feat_width)
        )
        acc_value = acc_value.at[flat_index].add(
            value_out.reshape(group_size * key_count, BLK, feat_width)
        )
        return ((acc_key, acc_value), query_out.astype(jnp.bfloat16))

    zeros_init = jnp.zeros((table_rows, BLK, feat_width), jnp.float32)
    step_ids = jnp.arange(steps_total, dtype=jnp.int32)
    (acc_key, acc_value), query_rows = lax.scan(attend, (zeros_init, zeros_init), step_ids)
    own_key = acc_key[:blocks]
    own_value = acc_value[:blocks]
    for bit_num in bit_order:
        lower = blocks + bit_num * pool_size
        sent_key = acc_key[lower : lower + pool_size]
        sent_value = acc_value[lower : lower + pool_size]
        asked_idx = partner_pool[jnp.bitwise_xor(group_id, 1 << bit_num), bit_num]
        back_key, back_value = swapped((sent_key, sent_value), "ctx", bit_num)
        own_key = own_key.at[asked_idx].add(back_key)
        own_value = own_value.at[asked_idx].add(back_value)
    query_local = query_rows.reshape(blocks * BLK, feat_width)
    key_local = own_key.reshape(blocks * BLK, feat_width).astype(jnp.bfloat16)
    value_local = own_value.reshape(blocks * BLK, feat_width).astype(jnp.bfloat16)
    query_grads, key_grads, value_grads = (
        lax.all_to_all(query_local, "head", split_axis=0, concat_axis=1, tiled=True),
        lax.all_to_all(key_local, "head", split_axis=0, concat_axis=1, tiled=True),
        lax.all_to_all(value_local, "head", split_axis=0, concat_axis=1, tiled=True),
    )
    return (query_grads, key_grads, value_grads)


def solution(mesh):
    return jax.shard_map(
        per_device,
        mesh=mesh,
        in_specs=(
            P(("ctx", "head"), None),
            P(("ctx", "head"), None),
            P(("ctx", "head"), None),
            P(("ctx", "head"), None),
            P("ctx", None),
            P(),
            P("ctx", None, None),
        ),
        out_specs=(P(("ctx", "head"), None), P(("ctx", "head"), None), P(("ctx", "head"), None)),
        check_vma=False,
    )
```

profile of v0, /device:TPU:0, one launch (start us, length us, event | category | flops | bytes accessed | tf_op | source)
XLA Modules:
  0.0 282.1 jit_solution(7600545536483731016)
XLA Ops:
  0.6 2.1 copy.65
  2.7 6.4 %all-to-all-start.1 = ((bf16[128,4,512]{0,2,1:T(8,128)(2,1)}), bf16[128,4,512]{0,2,1:T(8,128)(2,1)S(1)}, u32[]{:S(2)}, u32[]{:S(2)}) async-start(bf16[128,4,512]{0,2,1:T(8,128)(2,1)} %bitcast.10), calls=%async_computation.1 | async-start | bytes 1048576 | tf_op jit(solution)/shard_map/all_to_all | solution.py:19
  9.2 2.1 copy.67
  11.2 12.4 %all-to-all-done.1 = bf16[128,4,512]{0,2,1:T(8,128)(2,1)S(1)} async-done(((bf16[128,4,512]{0,2,1:T(8,128)(2,1)}), bf16[128,4,512]{0,2,1:T(8,128)(2,1)S(1)}, u32[]{:S(2)}, u32[]{:S(2)}) %all-to-all-start.1) | async-done | bytes 524320 | tf_op jit(solution)/shard_map/all_to_all | solution.py:19
  23.7 3.5 %all-to-all-start.3 = ((bf16[128,4,512]{0,2,1:T(8,128)(2,1)}), bf16[128,4,512]{0,2,1:T(8,128)(2,1)S(1)}, u32[]{:S(2)}, u32[]{:S(2)}) async-start(bf16[128,4,512]{0,2,1:T(8,128)(2,1)} %bitcast.17), calls=%async_computation.3 | async-start | bytes 1048576 | tf_op jit(solution)/shard_map/all_to_all | solution.py:20
  28.2 12.9 %all-to-all-done.3 = bf16[128,4,512]{0,2,1:T(8,128)(2,1)S(1)} async-done(((bf16[128,4,512]{0,2,1:T(8,128)(2,1)}), bf16[128,4,512]{0,2,1:T(8,128)(2,1)S(1)}, u32[]{:S(2)}, u32[]{:S(2)}) %all-to-all-start.3) | async-done | bytes 524320 | tf_op jit(solution)/shard_map/all_to_all | solution.py:20
  41.1 4.1 %all-to-all-start.2 = ((bf16[128,4,512]{0,2,1:T(8,128)(2,1)}), bf16[128,4,512]{0,2,1:T(8,128)(2,1)}, u32[]{:S(2)}, u32[]{:S(2)}) async-start(bf16[128,4,512]{0,2,1:T(8,128)(2,1)} %bitcast.14), calls=%async_computation.2 | async-start | bytes 1048576 | tf_op jit(solution)/shard_map/all_to_all | solution.py:21
  50.1 9.2 %all-to-all-done.2 = bf16[128,4,512]{0,2,1:T(8,128)(2,1)} async-done(((bf16[128,4,512]{0,2,1:T(8,128)(2,1)}), bf16[128,4,512]{0,2,1:T(8,128)(2,1)}, u32[]{:S(2)}, u32[]{:S(2)}) %all-to-all-start.2) | async-done | bytes 524320 | tf_op jit(solution)/shard_map/all_to_all | solution.py:21
  59.3 4.1 %all-to-all-start = ((bf16[128,4,512]{0,2,1:T(8,128)(2,1)}), bf16[128,4,512]{0,2,1:T(8,128)(2,1)}, u32[]{:S(2)}, u32[]{:S(2)}) async-start(bf16[128,4,512]{0,2,1:T(8,128)(2,1)} %bitcast.7), calls=%async_computation | async-start | bytes 1048576 | tf_op jit(solution)/shard_map/all_to_all | solution.py:18
  69.5 8.6 %collective-permute-done.3 = bf16[3,128,512]{1,2,0:T(8,128)(2,1)} collective-permute-done((bf16[3,128,512]{1,2,0:T(8,128)(2,1)}, bf16[3,128,512]{1,2,0:T(8,128)(2,1)}, u32[]{:S(2)}, u32[]{:S(2)}) %collective-permute-start.3) | collective-permute-done | bytes 393248 | tf_op jit(solution)/shard_map/ppermute | solution.py:11
  84.3 131.6 %while.14 = (s32[]{:T(128)}, f32[10,128,512]{2,1,0:T(8,128)}, f32[10,128,512]{2,1,0:T(8,128)}, bf16[2,2,128,4,128]{2,4,3,1,0:T(8,128)(2,1)}, s32[2]{0:T(128)S(1)...) while((s32[]{:T(128)}, f32[10,128,512]{2,1,0:T(8,128)}, ...), condition=%wide.region_6.7_spmd, body=%wide.region_0.6_spmd.sunk | while | flops 1021708864 | bytes 130315688 | solution.py:98
  85.6 2.0 gather_fusion
  90.4 2.6 fusion.59
  93.0 6.7 %convolution_bitcast_fusion.5 = f32[2,768,4,128]{1,3,2,0:T(8,128)} fusion(bf16[4,128,4,128]{1,3,2,0:T(8,128)(2,1)} %get-tuple-element.246, s32[]{:T(128)S(6)} %select_n.82, f32[2,4,128]{2,1,0:T(4,128)S(1)} %get-tuple-element.207, f32[2,4,128,768]{3,2,1,0:T(8,128)} %copy-done.1), kind=kOutput, calls=%fused_computation.18.clone.1 | convolution fusion | flops 205260544 | bytes 9703428 | tf_op jit(solution)/shard_map/while/body/eval_jaxpr/ghqk,gqhd->gkhd/dot_general | solution.py:84
  99.8 4.9 %copy.96 = f32[2,768,4,128]{3,2,1,0:T(4,128)} copy(f32[2,768,4,128]{1,3,2,0:T(8,128)} %convolution_bitcast_fusion.5) | data formatting | bytes 6291456 | tf_op jit(solution)/shard_map/while/body/eval_jaxpr/ghqk,gqhd->gkhd/transpose | solution.py:84
  104.6 5.1 %reshape.291 = f32[12,128,512]{2,1,0:T(8,128)} reshape(f32[2,768,4,128]{3,2,1,0:T(4,128)} %copy.96) | data formatting | bytes 6291456 | tf_op jit(solution)/shard_map/while/body/eval_jaxpr/reshape | solution.py:92
  109.8 9.1 %scatter_fusion.1 = f32[10,128,512]{2,1,0:T(8,128)} fusion(f32[10,128,512]{2,1,0:T(8,128)} %get-tuple-element.226, s32[12]{0:T(128)S(1)} %fusion.57, f32[12,128,512]{2,1,0:T(8,128)} %reshape.291), kind=kCustom, calls=%fused_computation.7.clone.1 | custom fusion | flops 786432 | bytes 9437232 | tf_op jit(solution)/shard_map/while/body/eval_jaxpr/scatter-add | solution.py:91
  118.9 2.0 gather_fusion.1
  122.8 3.5 %multiply_reduce_fusion.3 = (f32[2,4,128]{2,1,0:T(4,128)S(1)}, f32[2,4,128,768]{3,2,1,0:T(8,128)S(1)}) fusion(f32[2,4,128,768]{3,2,1,0:T(8,128)} %get-tuple-element.206, f32[2,4,128]{2,1,0:T(4,128)S(1)} %get-tuple-element.207, bf16[2,768,4,128]{3,2,1,0:T(4,128)(2,1)} %reshape.289, bf16[4,128,4,128]{1,3,2,0:T(8,128)(2,1)} %get-tuple-element.246, ...), kind=kOutput, calls=%fused_computation.14.clone.1 | convolution fusion | flops 203684864 | bytes 8134660 | tf_op jit(solution)/shard_map/while/body/eval_jaxpr/gqhd,gkhd->ghqk/dot_general | solution.py:72
  126.9 3.2 %convolution_bitcast_fusion.4 = f32[2,768,4,128]{1,3,2,0:T(8,128)} fusion(bf16[2,4,128,768]{3,2,1,0:T(8,128)(2,1)S(1)} %multiply_convert_fusion.2, bf16[4,128,4,128]{1,3,2,0:T(8,128)(2,1)} %get-tuple-element.244, s32[]{:T(128)S(6)} %select_n.82), kind=kOutput, calls=%fused_computation.19.clone.1 | convolution fusion | flops 201326592 | bytes 4980740 | tf_op jit(solution)/shard_map/while/body/eval_jaxpr/ghqk,gqhd->gkhd/dot_general | solution.py:81
  130.1 4.9 %copy.95 = f32[2,768,4,128]{3,2,1,0:T(4,128)} copy(f32[2,768,4,128]{1,3,2,0:T(8,128)} %convolution_bitcast_fusion.4) | data formatting | bytes 6291456 | tf_op jit(solution)/shard_map/while/body/eval_jaxpr/ghqk,gqhd->gkhd/transpose | solution.py:81
  134.9 5.0 %reshape.290 = f32[12,128,512]{2,1,0:T(8,128)} reshape(f32[2,768,4,128]{3,2,1,0:T(4,128)} %copy.95) | data formatting | bytes 6291456 | tf_op jit(solution)/shard_map/while/body/eval_jaxpr/reshape | solution.py:89
  140.0 9.0 %scatter_fusion = f32[10,128,512]{2,1,0:T(8,128)} fusion(f32[10,128,512]{2,1,0:T(8,128)} %get-tuple-element.225, s32[12]{0:T(128)S(1)} %fusion.57, f32[12,128,512]{2,1,0:T(8,128)} %reshape.290), kind=kCustom, calls=%fused_computation.6.clone.1 | custom fusion | flops 786432 | bytes 9437232 | tf_op jit(solution)/shard_map/while/body/eval_jaxpr/scatter-add | solution.py:88
  151.6 2.0 gather_fusion
  156.4 2.6 fusion.59
  159.0 6.8 %convolution_bitcast_fusion.5 = f32[2,768,4,128]{1,3,2,0:T(8,128)} fusion(bf16[4,128,4,128]{1,3,2,0:T(8,128)(2,1)} %get-tuple-element.246, s32[]{:T(128)S(6)} %select_n.82, f32[2,4,128]{2,1,0:T(4,128)S(1)} %get-tuple-element.207, f32[2,4,128,768]{3,2,1,0:T(8,128)} %copy-done.1), kind=kOutput, calls=%fused_computation.18.clone.1 | convolution fusion | flops 205260544 | bytes 9703428 | tf_op jit(solution)/shard_map/while/body/eval_jaxpr/ghqk,gqhd->gkhd/dot_general | solution.py:84
  165.8 4.9 %copy.96 = f32[2,768,4,128]{3,2,1,0:T(4,128)} copy(f32[2,768,4,128]{1,3,2,0:T(8,128)} %convolution_bitcast_fusion.5) | data formatting | bytes 6291456 | tf_op jit(solution)/shard_map/while/body/eval_jaxpr/ghqk,gqhd->gkhd/transpose | solution.py:84
  170.7 5.1 %reshape.291 = f32[12,128,512]{2,1,0:T(8,128)} reshape(f32[2,768,4,128]{3,2,1,0:T(4,128)} %copy.96) | data formatting | bytes 6291456 | tf_op jit(solution)/shard_map/while/body/eval_jaxpr/reshape | solution.py:92
  175.8 8.9 %scatter_fusion.1 = f32[10,128,512]{2,1,0:T(8,128)} fusion(f32[10,128,512]{2,1,0:T(8,128)} %get-tuple-element.226, s32[12]{0:T(128)S(1)} %fusion.57, f32[12,128,512]{2,1,0:T(8,128)} %reshape.291), kind=kCustom, calls=%fused_computation.7.clone.1 | custom fusion | flops 786432 | bytes 9437232 | tf_op jit(solution)/shard_map/while/body/eval_jaxpr/scatter-add | solution.py:91
  188.5 3.5 %multiply_reduce_fusion.3 = (f32[2,4,128]{2,1,0:T(4,128)S(1)}, f32[2,4,128,768]{3,2,1,0:T(8,128)S(1)}) fusion(f32[2,4,128,768]{3,2,1,0:T(8,128)} %get-tuple-element.206, f32[2,4,128]{2,1,0:T(4,128)S(1)} %get-tuple-element.207, bf16[2,768,4,128]{3,2,1,0:T(4,128)(2,1)} %reshape.289, bf16[4,128,4,128]{1,3,2,0:T(8,128)(2,1)} %get-tuple-element.246, ...), kind=kOutput, calls=%fused_computation.14.clone.1 | convolution fusion | flops 203684864 | bytes 8134660 | tf_op jit(solution)/shard_map/while/body/eval_jaxpr/gqhd,gkhd->ghqk/dot_general | solution.py:72
  192.7 3.2 %convolution_bitcast_fusion.4 = f32[2,768,4,128]{1,3,2,0:T(8,128)} fusion(bf16[2,4,128,768]{3,2,1,0:T(8,128)(2,1)S(1)} %multiply_convert_fusion.2, bf16[4,128,4,128]{1,3,2,0:T(8,128)(2,1)} %get-tuple-element.244, s32[]{:T(128)S(6)} %select_n.82), kind=kOutput, calls=%fused_computation.19.clone.1 | convolution fusion | flops 201326592 | bytes 4980740 | tf_op jit(solution)/shard_map/while/body/eval_jaxpr/ghqk,gqhd->gkhd/dot_general | solution.py:81
  195.8 4.9 %copy.95 = f32[2,768,4,128]{3,2,1,0:T(4,128)} copy(f32[2,768,4,128]{1,3,2,0:T(8,128)} %convolution_bitcast_fusion.4) | data formatting | bytes 6291456 | tf_op jit(solution)/shard_map/while/body/eval_jaxpr/ghqk,gqhd->gkhd/transpose | solution.py:81
  200.7 5.0 %reshape.290 = f32[12,128,512]{2,1,0:T(8,128)} reshape(f32[2,768,4,128]{3,2,1,0:T(4,128)} %copy.95) | data formatting | bytes 6291456 | tf_op jit(solution)/shard_map/while/body/eval_jaxpr/reshape | solution.py:89
  205.7 8.9 %scatter_fusion = f32[10,128,512]{2,1,0:T(8,128)} fusion(f32[10,128,512]{2,1,0:T(8,128)} %get-tuple-element.225, s32[12]{0:T(128)S(1)} %fusion.57, f32[12,128,512]{2,1,0:T(8,128)} %reshape.290), kind=kCustom, calls=%fused_computation.6.clone.1 | custom fusion | flops 786432 | bytes 9437232 | tf_op jit(solution)/shard_map/while/body/eval_jaxpr/scatter-add | solution.py:88
  215.9 2.8 fusion.29
  221.2 5.0 %all-to-all-start.4 = ((bf16[4,128,512]{2,1,0:T(8,128)(2,1)}), bf16[4,128,512]{2,1,0:T(8,128)(2,1)S(1)}, u32[]{:S(2)}, u32[]{:S(2)}) async-start(bf16[4,128,512]{2,1,0:T(8,128)(2,1)} %copy.80), calls=%async_computation.4 | async-start | bytes 1048576 | tf_op jit(solution)/shard_map/all_to_all | solution.py:113
  226.2 2.3 slice.21
  230.3 3.2 %scatter_fusion.4 = f32[4,128,512]{2,1,0:T(8,128)} fusion(f32[4,128,512]{2,1,0:T(8,128)} %slice.21, s32[3]{0:T(128)S(1)} %copy-done.9, f32[3,128,512]{2,1,0:T(8,128)} %collective-permute-done.6), kind=kCustom, calls=%fused_computation.10 | custom fusion | flops 196608 | bytes 2359308 | tf_op jit(solution)/shard_map/scatter-add | solution.py:108
  233.5 5.8 %collective-permute-done.7 = f32[3,128,512]{2,1,0:T(8,128)} collective-permute-done((f32[3,128,512]{2,1,0:T(8,128)}, f32[3,128,512]{2,1,0:T(8,128)}, u32[]{:S(2)}, u32[]{:S(2)}) %collective-permute-start.7) | collective-permute-done | bytes 786464 | tf_op jit(solution)/shard_map/ppermute | solution.py:11
  239.4 3.2 %scatter_fusion.5 = f32[4,128,512]{2,1,0:T(8,128)} fusion(f32[4,128,512]{2,1,0:T(8,128)} %scatter_fusion.4, s32[3]{0:T(128)S(1)} %copy-done.7, f32[3,128,512]{2,1,0:T(8,128)} %collective-permute-done.7), kind=kCustom, calls=%fused_computation.11 | custom fusion | flops 196608 | bytes 2359308 | tf_op jit(solution)/shard_map/scatter-add | solution.py:108
  242.6 2.1 convert_element_type.21
  244.7 5.0 %all-to-all-start.6 = ((bf16[4,128,512]{2,1,0:T(8,128)(2,1)}), bf16[4,128,512]{2,1,0:T(8,128)(2,1)}, u32[]{:S(2)}, u32[]{:S(2)}) async-start(bf16[4,128,512]{2,1,0:T(8,128)(2,1)} %convert_element_type.21), calls=%async_computation.6 | async-start | bytes 1048576 | tf_op jit(solution)/shard_map/all_to_all | solution.py:115
  250.7 3.2 %scatter_fusion.2 = f32[4,128,512]{2,1,0:T(8,128)} fusion(f32[4,128,512]{2,1,0:T(8,128)} %slice.18, s32[3]{0:T(128)S(1)} %copy-done.9, f32[3,128,512]{2,1,0:T(8,128)} %collective-permute-done.4), kind=kCustom, calls=%fused_computation.8 | custom fusion | flops 196608 | bytes 2359308 | tf_op jit(solution)/shard_map/scatter-add | solution.py:107
  255.8 3.2 %scatter_fusion.3 = f32[4,128,512]{2,1,0:T(8,128)} fusion(f32[4,128,512]{2,1,0:T(8,128)} %scatter_fusion.2, s32[3]{0:T(128)S(1)} %copy-done.7, f32[3,128,512]{2,1,0:T(8,128)} %collective-permute-done.5), kind=kCustom, calls=%fused_computation.9 | custom fusion | flops 196608 | bytes 2359308 | tf_op jit(solution)/shard_map/scatter-add | solution.py:107
  259.0 2.1 convert_element_type.20
  261.1 2.7 all-to-all-done.6
  263.8 3.5 %all-to-all-start.5 = ((bf16[4,128,512]{2,1,0:T(8,128)(2,1)}), bf16[4,128,512]{2,1,0:T(8,128)(2,1)S(1)}, u32[]{:S(2)}, u32[]{:S(2)}) async-start(bf16[4,128,512]{2,1,0:T(8,128)(2,1)} %convert_element_type.20), calls=%async_computation.5 | async-start | bytes 1048576 | tf_op jit(solution)/shard_map/all_to_all | solution.py:114
  270.5 10.8 %all-to-all-done.5 = bf16[4,128,512]{2,1,0:T(8,128)(2,1)S(1)} async-done(((bf16[4,128,512]{2,1,0:T(8,128)(2,1)}), bf16[4,128,512]{2,1,0:T(8,128)(2,1)S(1)}, u32[]{:S(2)}, u32[]{:S(2)}) %all-to-all-start.5) | async-done | bytes 524320 | tf_op jit(solution)/shard_map/all_to_all | solution.py:114
  (101 shorter events, 45.9 us)
Async XLA Ops:
  0.6 26.5 %copy-start.3 = (bf16[128,2048]{1,0:T(8,128)(2,1)S(1)}, bf16[128,2048]{1,0:T(8,128)(2,1)}, u32[]{:S(2)}) copy-start(bf16[128,2048]{1,0:T(8,128)(2,1)} %param.12) | copy-start | bytes 1572868
  2.7 42.5 %copy-start.4 = (bf16[128,2048]{1,0:T(8,128)(2,1)S(1)}, bf16[128,2048]{1,0:T(8,128)(2,1)}, u32[]{:S(2)}) copy-start(bf16[128,2048]{1,0:T(8,128)(2,1)} %param.9) | copy-start | bytes 1572868
  2.7 20.9 %all-to-all-start.1 = ((bf16[128,4,512]{0,2,1:T(8,128)(2,1)}), bf16[128,4,512]{0,2,1:T(8,128)(2,1)S(1)}, u32[]{:S(2)}, u32[]{:S(2)}) async-start(bf16[128,4,512]{0,2,1:T(8,128)(2,1)} %bitcast.10), calls=%async_computation.1 | async-start | bytes 1048576 | tf_op jit(solution)/shard_map/all_to_all | solution.py:19
  9.2 37.1 %copy-start.10 = (s32[8,2,3]{0,1,2:T(2,128)S(1)}, s32[8,2,3]{0,1,2:T(2,128)}, u32[]{:S(2)}) copy-start(s32[8,2,3]{0,1,2:T(2,128)} %param.14) | copy-start | bytes 580
  23.7 17.4 %all-to-all-start.3 = ((bf16[128,4,512]{0,2,1:T(8,128)(2,1)}), bf16[128,4,512]{0,2,1:T(8,128)(2,1)S(1)}, u32[]{:S(2)}, u32[]{:S(2)}) async-start(bf16[128,4,512]{0,2,1:T(8,128)(2,1)} %bitcast.17), calls=%async_computation.3 | async-start | bytes 1048576 | tf_op jit(solution)/shard_map/all_to_all | solution.py:20
  28.2 35.3 %copy-start.11 = (s32[4,2,2]{0,2,1:T(2,128)S(1)}, s32[4,2,2]{0,2,1:T(2,128)}, u32[]{:S(2)}) copy-start(s32[4,2,2]{0,2,1:T(2,128)} %param.15) | copy-start | bytes 196
  41.1 18.2 %all-to-all-start.2 = ((bf16[128,4,512]{0,2,1:T(8,128)(2,1)}), bf16[128,4,512]{0,2,1:T(8,128)(2,1)}, u32[]{:S(2)}, u32[]{:S(2)}) async-start(bf16[128,4,512]{0,2,1:T(8,128)(2,1)} %bitcast.14), calls=%async_computation.2 | async-start | bytes 1048576 | tf_op jit(solution)/shard_map/all_to_all | solution.py:21
  45.3 22.4 %copy-start.12 = (s32[4,2]{0,1:T(2,128)S(1)}, s32[4,2]{0,1:T(2,128)}, u32[]{:S(2)}) copy-start(s32[4,2]{0,1:T(2,128)} %param.13) | copy-start | bytes 100
  46.6 0.6 copy-start.6
  46.6 0.6 copy-start.8
  47.8 20.0 %collective-permute-start = (bf16[3,128,512]{1,2,0:T(8,128)(2,1)S(1)}, bf16[3,128,512]{1,2,0:T(8,128)(2,1)S(1)}, u32[]{:S(2)}, u32[]{:S(2)}) collective-permute-start(bf16[3,128,512]{1,2,0:T(8,128)(2,1)S(1)} %gather_fusion.2), channel_id=1, source_target_pairs={{0,4},{4,0},{8,12},{12,8},{16,20},{20,16},{24,28},{28,24},{1,5},{5... | collective-permute-start | bytes 1179656 | tf_op jit(solution)/shard_map/ppermute | solution.py:11
  48.5 19.3 %collective-permute-start.1 = (bf16[3,128,512]{1,2,0:T(8,128)(2,1)S(1)}, bf16[3,128,512]{1,2,0:T(8,128)(2,1)S(1)}, u32[]{:S(2)}, u32[]{:S(2)}) collective-permute-start(bf16[3,128,512]{1,2,0:T(8,128)(2,1)S(1)} %gather_fusion.3), channel_id=1, source_target_pairs={{0,8},{4,12},{8,0},{12,4},{16,24},{20,28},{24,16},{28,20},{1,9},{5... | collective-permute-start | bytes 1179656 | tf_op jit(solution)/shard_map/ppermute | solution.py:11
  59.3 21.4 %all-to-all-start = ((bf16[128,4,512]{0,2,1:T(8,128)(2,1)}), bf16[128,4,512]{0,2,1:T(8,128)(2,1)}, u32[]{:S(2)}, u32[]{:S(2)}) async-start(bf16[128,4,512]{0,2,1:T(8,128)(2,1)} %bitcast.7), calls=%async_computation | async-start | bytes 1048576 | tf_op jit(solution)/shard_map/all_to_all | solution.py:18
  66.2 3.2 %collective-permute-start.2 = (bf16[3,128,512]{1,2,0:T(8,128)(2,1)}, bf16[3,128,512]{1,2,0:T(8,128)(2,1)S(1)}, u32[]{:S(2)}, u32[]{:S(2)}) collective-permute-start(bf16[3,128,512]{1,2,0:T(8,128)(2,1)} %gather_fusion.4), channel_id=1, source_target_pairs={{0,4},{4,0},{8,12},{12,8},{16,20},{20,16},{24,28},{28,24},{1,5},{5... | collective-permute-start | bytes 1179656 | tf_op jit(solution)/shard_map/ppermute | solution.py:11
  66.2 11.8 %collective-permute-start.3 = (bf16[3,128,512]{1,2,0:T(8,128)(2,1)}, bf16[3,128,512]{1,2,0:T(8,128)(2,1)}, u32[]{:S(2)}, u32[]{:S(2)}) collective-permute-start(bf16[3,128,512]{1,2,0:T(8,128)(2,1)} %gather_fusion.5), channel_id=1, source_target_pairs={{0,8},{4,12},{8,0},{12,4},{16,24},{20,28},{24,16},{28,20},{1,9},{5... | collective-permute-start | bytes 1179656 | tf_op jit(solution)/shard_map/ppermute | solution.py:11
  90.4 2.6 copy-start.1
  122.8 3.5 %copy-start = (f32[2,4,128,768]{3,2,1,0:T(8,128)S(1)}, f32[2,4,128,768]{3,2,1,0:T(8,128)}, u32[]{:S(2)}) copy-start(f32[2,4,128,768]{3,2,1,0:T(8,128)} %get-tuple-element.206) | copy-start | bytes 9437188 | tf_op jit(solution)/shard_map/while
  156.4 2.6 copy-start.1
  188.5 3.5 %copy-start = (f32[2,4,128,768]{3,2,1,0:T(8,128)S(1)}, f32[2,4,128,768]{3,2,1,0:T(8,128)}, u32[]{:S(2)}) copy-start(f32[2,4,128,768]{3,2,1,0:T(8,128)} %get-tuple-element.206) | copy-start | bytes 9437188 | tf_op jit(solution)/shard_map/while
  215.9 4.2 %copy-start.5 = (bf16[2,2,128,4,128]{2,4,3,1,0:T(8,128)(2,1)S(1)}, bf16[2,2,128,4,128]{2,4,3,1,0:T(8,128)(2,1)}, u32[]{:S(2)}) copy-start(bf16[2,2,128,4,128]{2,4,3,1,0:T(8,128)(2,1)} %get-tuple-element.57) | copy-start | bytes 1572868
  218.7 9.8 %copy-start.2 = (f32[10,128,512]{2,1,0:T(8,128)S(1)}, f32[10,128,512]{2,1,0:T(8,128)}, u32[]{:S(2)}) copy-start(f32[10,128,512]{2,1,0:T(8,128)} %get-tuple-element.58) | copy-start | bytes 7864324
  218.7 11.6 %collective-permute-start.6 = (f32[3,128,512]{2,1,0:T(8,128)}, f32[3,128,512]{2,1,0:T(8,128)}, u32[]{:S(2)}, u32[]{:S(2)}) collective-permute-start(f32[3,128,512]{2,1,0:T(8,128)} %get-tuple-element.132), channel_id=1, source_target_pairs={{0,4},{4,0},{8,12},{12,8},{16,20},{20,16},{24,28},{28,24},{1,5},{5... | collective-permute-start | bytes 2359304 | tf_op jit(solution)/shard_map/ppermute | solution.py:11
  218.7 20.7 %collective-permute-start.7 = (f32[3,128,512]{2,1,0:T(8,128)}, f32[3,128,512]{2,1,0:T(8,128)}, u32[]{:S(2)}, u32[]{:S(2)}) collective-permute-start(f32[3,128,512]{2,1,0:T(8,128)} %get-tuple-element.131), channel_id=1, source_target_pairs={{0,8},{4,12},{8,0},{12,4},{16,24},{20,28},{24,16},{28,20},{1,9},{5... | collective-permute-start | bytes 2359304 | tf_op jit(solution)/shard_map/ppermute | solution.py:11
  221.2 23.5 %all-to-all-start.4 = ((bf16[4,128,512]{2,1,0:T(8,128)(2,1)}), bf16[4,128,512]{2,1,0:T(8,128)(2,1)S(1)}, u32[]{:S(2)}, u32[]{:S(2)}) async-start(bf16[4,128,512]{2,1,0:T(8,128)(2,1)} %copy.80), calls=%async_computation.4 | async-start | bytes 1048576 | tf_op jit(solution)/shard_map/all_to_all | solution.py:113
  226.2 4.1 %copy-start.9 = (s32[3]{0:T(128)S(1)}, s32[3]{0:T(128)}, u32[]{:S(2)}) copy-start(s32[3]{0:T(128)} %copy-done.8) | copy-start | bytes 40
  228.5 10.9 %copy-start.7 = (s32[3]{0:T(128)S(1)}, s32[3]{0:T(128)}, u32[]{:S(2)}) copy-start(s32[3]{0:T(128)} %copy-done.6) | copy-start | bytes 40
  229.7 21.0 %collective-permute-start.4 = (f32[3,128,512]{2,1,0:T(8,128)}, f32[3,128,512]{2,1,0:T(8,128)}, u32[]{:S(2)}, u32[]{:S(2)}) collective-permute-start(f32[3,128,512]{2,1,0:T(8,128)} %get-tuple-element.134), channel_id=1, source_target_pairs={{0,4},{4,0},{8,12},{12,8},{16,20},{20,16},{24,28},{28,24},{1,5},{5... | collective-permute-start | bytes 2359304 | tf_op jit(solution)/shard_map/ppermute | solution.py:11
  229.8 26.1 %collective-permute-start.5 = (f32[3,128,512]{2,1,0:T(8,128)}, f32[3,128,512]{2,1,0:T(8,128)}, u32[]{:S(2)}, u32[]{:S(2)}) collective-permute-start(f32[3,128,512]{2,1,0:T(8,128)} %get-tuple-element.133), channel_id=1, source_target_pairs={{0,8},{4,12},{8,0},{12,4},{16,24},{20,28},{24,16},{28,20},{1,9},{5... | collective-permute-start | bytes 2359304 | tf_op jit(solution)/shard_map/ppermute | solution.py:11
  244.7 19.1 %all-to-all-start.6 = ((bf16[4,128,512]{2,1,0:T(8,128)(2,1)}), bf16[4,128,512]{2,1,0:T(8,128)(2,1)}, u32[]{:S(2)}, u32[]{:S(2)}) async-start(bf16[4,128,512]{2,1,0:T(8,128)(2,1)} %convert_element_type.21), calls=%async_computation.6 | async-start | bytes 1048576 | tf_op jit(solution)/shard_map/all_to_all | solution.py:115
  263.8 17.4 %all-to-all-start.5 = ((bf16[4,128,512]{2,1,0:T(8,128)(2,1)}), bf16[4,128,512]{2,1,0:T(8,128)(2,1)S(1)}, u32[]{:S(2)}, u32[]{:S(2)}) async-start(bf16[4,128,512]{2,1,0:T(8,128)(2,1)} %convert_element_type.20), calls=%async_computation.5 | async-start | bytes 1048576 | tf_op jit(solution)/shard_map/all_to_all | solution.py:114
where the time goes:
time: 284 us; the launch traced here: 282 us
  local copies, waits for them, and re-layouts  85.1 us (30%)
  waiting for transfers between devices  64.5 us (23%)
  other arithmetic  60.7 us (21%)
  starting transfers between devices  36.9 us (13%)
  matrix products  32.6 us (11%)
    scatter-add x2, other arithmetic, attend(): acc_value.at[flat_index]  18 us
    scatter-add x2, other arithmetic, attend(): acc_key.at[flat_index]  17.9 us
    ppermute x8, waiting for transfers between devices, swapped(): lax.ppermute(value, axis, [(i, i ^ 1 << distance) for i in range(lax.axis...  16.4 us
    dot_general x2, matrix products, attend(): jnp.einsum('ghqk,gqhd->gkhd', weights_half, grad_part, preferred_element_...  13.5 us
    all_to_all x1, waiting for transfers between devices, per_device(): lax.all_to_all(value_vecs, 'head', split_axis=1, concat_axis=0, tiled=True)  12.9 us
    all_to_all x1, waiting for transfers between devices, per_device(): lax.all_to_all(key_vecs, 'head', split_axis=1, concat_axis=0, tiled=True)  12.4 us
    all_to_all x1, waiting for transfers between devices, per_device(): lax.all_to_all(key_local, 'head', split_axis=0, concat_axis=1, tiled=True)  10.8 us
    reshape x2, local copies, waits for them, and re-layouts, attend(): value_out.reshape(group_size * key_count, BLK, feat_width)  10.1 us
  transfers between devices with their start and end apart: 15, of which 8 were waited for; matrix products, arithmetic and copies ran while one was open for 14% of the time, Pallas kernels for 0%

commit v1 on v0

v1 whole, which is shorter than its diff:
```python
import functools

import jax
import jax.numpy as jnp
from jax import lax
from jax.experimental import pallas as pl
from jax.experimental.pallas import tpu as pltpu
from jax.sharding import PartitionSpec as P

DH = 128
BLK = 128
LOG2_E = 1.4426950408889634
NT = (((1,), (1,)), ((), ()))


def swapped(value, axis, distance):
    return lax.ppermute(value, axis, [(i, i ^ 1 << distance) for i in range(lax.axis_size(axis))])


def rows(block):
    return pl.ds(pl.multiple_of(block * BLK, BLK), BLK)


def attend_kernel(
    index_ref, q_ref, k_ref, v_ref, g_ref, dq_ref, dk_ref, dv_ref, acc_k, acc_v, k_turned, k_cat, v_cat, kt_cat
):
    query_blocks = q_ref.shape[0] // BLK
    table_blocks = k_ref.shape[0] // BLK
    key_count = k_cat.shape[0] // BLK
    scale = DH**-0.5

    acc_k[...] = jnp.zeros_like(acc_k)
    acc_v[...] = jnp.zeros_like(acc_v)
    for block in range(table_blocks):
        k_turned[block] = k_ref[block * BLK : (block + 1) * BLK, :].T

    def step(block, _):
        query = q_ref[rows(block), :]
        grad = g_ref[rows(block), :]
        chosen = [index_ref[block * key_count + j] for j in range(key_count)]
        for j in range(key_count):
            part = slice(j * BLK, (j + 1) * BLK)
            k_cat[part, :] = k_ref[rows(chosen[j]), :]
            v_cat[part, :] = v_ref[rows(chosen[j]), :]
            kt_cat[:, part] = k_turned[chosen[j]]
        scores = lax.dot_general(k_cat[...], query, NT, preferred_element_type=jnp.float32)
        row_max = jnp.max(scores, axis=0, keepdims=True)
        exp_scores = jnp.exp2((scores - row_max) * (scale * LOG2_E))
        weights = exp_scores * (1.0 / jnp.sum(exp_scores, axis=0, keepdims=True))
        prob_grad = lax.dot_general(v_cat[...], grad, NT, preferred_element_type=jnp.float32)
        row_delta = jnp.sum(weights * prob_grad, axis=0, keepdims=True)
        score_grad = (scale * weights * (prob_grad - row_delta)).astype(jnp.bfloat16)
        weights_half = weights.astype(jnp.bfloat16)
        query_turned = jnp.dot(kt_cat[...], score_grad, preferred_element_type=jnp.float32)
        dq_ref[rows(block), :] = query_turned.T.astype(jnp.bfloat16)
        key_out = jnp.dot(score_grad, query, preferred_element_type=jnp.float32)
        value_out = jnp.dot(weights_half, grad, preferred_element_type=jnp.float32)
        for j in range(key_count):
            part = slice(j * BLK, (j + 1) * BLK)
            acc_k[rows(chosen[j]), :] += key_out[part]
            acc_v[rows(chosen[j]), :] += value_out[part]
        return 0

    lax.fori_loop(0, query_blocks, step, 0)
    dk_ref[...] = acc_k[...].astype(dk_ref.dtype)
    dv_ref[...] = acc_v[...].astype(dv_ref.dtype)


def attend(index, query, key, value, grad, table_type):
    heads = query.shape[1] // DH
    key_count = index.shape[1]
    tokens, table = query.shape[0], key.shape[0]
    token_spec = pl.BlockSpec((tokens, DH), lambda h, *_: (0, h))
    table_spec = pl.BlockSpec((table, DH), lambda h, *_: (0, h))
    return pl.pallas_call(
        attend_kernel,
        grid_spec=pltpu.PrefetchScalarGridSpec(
            num_scalar_prefetch=1,
            grid=(heads,),
            in_specs=[token_spec, table_spec, table_spec, token_spec],
            out_specs=[token_spec, table_spec, table_spec],
            scratch_shapes=[
                pltpu.VMEM((table, DH), jnp.float32),
                pltpu.VMEM((table, DH), jnp.float32),
                pltpu.VMEM((table // BLK, DH, BLK), jnp.bfloat16),
                pltpu.VMEM((key_count * BLK, DH), jnp.bfloat16),
                pltpu.VMEM((key_count * BLK, DH), jnp.bfloat16),
                pltpu.VMEM((DH, key_count * BLK), jnp.bfloat16),
            ],
        ),
        out_shape=[
            jax.ShapeDtypeStruct(query.shape, jnp.bfloat16),
            jax.ShapeDtypeStruct(key.shape, table_type),
            jax.ShapeDtypeStruct(key.shape, table_type),
        ],
        compiler_params=pltpu.CompilerParams(vmem_limit_bytes=40 << 20),
        name="attend",
    )(index.reshape(-1), query, key, value, grad)


def to_heads_kernel(*refs):
    *ins, out = refs
    for place, ref in enumerate(ins):
        for head in range(out.shape[0]):
            out[head, place] = ref[:, head * DH : (head + 1) * DH]


def from_heads_kernel(ref, *outs):
    for place, out in enumerate(outs):
        for head in range(ref.shape[0]):
            out[:, head * DH : (head + 1) * DH] = ref[head, place]


def whole_cluster(
    queries, key_vecs, value_vecs, out_grads, local_offsets, partner_pool, partner_picks
):
    bits = partner_pool.shape[1]
    groups, parts = lax.axis_size("ctx"), lax.axis_size("head")
    tokens, features = queries.shape
    cluster = (parts << bits)
    heads = features // DH // cluster
    members = [
        [group * parts + part for group in range(first, first + (1 << bits)) for part in range(parts)]
        for first in range(0, groups, 1 << bits)
    ]
    exchange = functools.partial(
        lax.all_to_all, axis_name=("ctx", "head"), split_axis=0, concat_axis=0, tiled=True, axis_index_groups=members
    )
    group = lax.axis_index("ctx")
    blocks = parts * (tokens // BLK)
    inner = jnp.arange(blocks, dtype=jnp.int32)
    place = jnp.bitwise_and(group, (1 << bits) - 1)
    own = place * blocks + (inner[:, None] + local_offsets) % blocks
    far = []
    for bit in range(bits):
        pool = partner_pool[group, bit]
        far.append(jnp.bitwise_xor(place, 1 << bit) * blocks + pool[partner_picks[:, bit]])
    index = jnp.concatenate([own] + far, axis=1).astype(jnp.int32)
    near = [list(range(first, first + (1 << bits))) for first in range(0, groups, 1 << bits)]
    index = lax.all_gather(index, "ctx", axis_index_groups=near, tiled=True)

    arrays = (queries, key_vecs, value_vecs, out_grads)
    packed = pl.pallas_call(
        to_heads_kernel,
        out_shape=jax.ShapeDtypeStruct((features // DH, len(arrays), tokens, DH), queries.dtype),
        name="to_heads",
    )(*arrays)
    packed = exchange(packed)
    query, key, value, grad = (packed[:, n].reshape(cluster * tokens, DH) for n in range(4))
    results = attend(index, query, key, value, grad, jnp.bfloat16)
    packed = jnp.stack([r.reshape(cluster, tokens, DH) for r in results], axis=1)
    packed = exchange(packed)
    return pl.pallas_call(
        from_heads_kernel,
        out_shape=[jax.ShapeDtypeStruct(queries.shape, queries.dtype)] * 3,
        name="from_heads",
    )(packed)


def by_pools(
    queries, key_vecs, value_vecs, out_grads, local_offsets, partner_pool, partner_picks
):
    to_heads = functools.partial(lax.all_to_all, axis_name="head", split_axis=1, concat_axis=0, tiled=True)
    to_tokens = functools.partial(lax.all_to_all, axis_name="head", split_axis=0, concat_axis=1, tiled=True)
    query, key, value, grad = (to_heads(x) for x in (queries, key_vecs, value_vecs, out_grads))
    width = query.shape[1]
    blocks = query.shape[0] // BLK
    bits, pool_size = partner_pool.shape[1:]
    group = lax.axis_index("ctx")
    asked = [partner_pool[jnp.bitwise_xor(group, 1 << bit), bit] for bit in range(bits)]

    def table(array):
        by_block = array.reshape(blocks, BLK, width)
        far = [swapped(by_block[asked[bit]], "ctx", bit) for bit in range(bits)]
        return jnp.concatenate([by_block] + far).reshape(-1, width)

    inner = jnp.arange(blocks, dtype=jnp.int32)
    own = (inner[:, None] + local_offsets) % blocks
    far = blocks + jnp.arange(bits, dtype=jnp.int32)[None, :, None] * pool_size + partner_picks
    index = jnp.concatenate([own, far.reshape(blocks, -1)], axis=1).astype(jnp.int32)
    dq, *tables = attend(index, query, table(key), table(value), grad, jnp.float32)
    grads = [dq]
    for array in tables:
        by_block = array.reshape(-1, BLK, width)
        total = by_block[:blocks]
        for bit in range(bits):
            lower = blocks + bit * pool_size
            back = swapped(by_block[lower : lower + pool_size], "ctx", bit)
            total = total.at[asked[bit]].add(back)
        grads.append(total.reshape(blocks * BLK, width).astype(jnp.bfloat16))
    return tuple(to_tokens(x) for x in grads)


def per_device(*args):
    partner_pool = args[5]
    cluster = lax.axis_size("head") << partner_pool.shape[1]
    if args[0].shape[1] // DH == cluster and args[0].shape[0] == BLK:
        return tuple(whole_cluster(*args))
    return by_pools(*args)


def solution(mesh):
    return jax.shard_map(
        per_device,
        mesh=mesh,
        in_specs=(
            P(("ctx", "head"), None),
            P(("ctx", "head"), None),
            P(("ctx", "head"), None),
            P(("ctx", "head"), None),
            P("ctx", None),
            P(),
            P("ctx", None, None),
        ),
        out_specs=(P(("ctx", "head"), None), P(("ctx", "head"), None), P(("ctx", "head"), None)),
        check_vma=False,
    )
```

time: 284 us -> 121 us (0.43)
  local copies, waits for them, and re-layouts: 85.1 us -> 2.52 us
  other arithmetic: 60.7 us -> 0.28 us
  blocking collectives: 0 us -> 56.9 us
  waiting for transfers between devices: 64.5 us -> 31.6 us
  matrix products: 32.6 us -> 0 us
  starting transfers between devices: 36.9 us -> 7.5 us
  Pallas kernels: 0 us -> 21.3 us
    scatter-add x8 -> x0, other arithmetic: 48.7 us -> none  [the longest x2 18 us: attend(): acc_value.at[flat_index]]
    all_to_all x0 -> x1, blocking collectives: none -> 41.5 us  [whole_cluster(): packed = exchange(packed)]
    dot_general x10 -> x0, matrix products: 32.6 us -> none  [the longest x2 13.5 us: attend(): jnp.einsum('ghqk,gqhd->gkhd', weights_half, grad_part, preferred_element_...]
    reshape x12 -> x1, local copies, waits for them, and re-layouts: 26.6 us -> 0.09 us  [attend(): index.reshape(-1)]
    all_to_all x7 -> x1, starting transfers between devices: 31.7 us -> 7.5 us  [whole_cluster(): packed = exchange(packed)]
    pallas_call x0 -> x3, Pallas kernels: none -> 21.3 us  [the longest x1 15.1 us: attend(): pl.pallas_call(attend_kernel, grid_spec=pltpu.PrefetchScalarGridSpec(num_...]
    transpose x4 -> x0, local copies, waits for them, and re-layouts: 19.4 us -> none  [the longest x2 9.73 us: attend(): jnp.einsum('ghqk,gqhd->gkhd', weights_half, grad_part, preferred_element_...]
    all_to_all x7 -> x1, waiting for transfers between devices: 48.1 us -> 31.6 us  [whole_cluster(): packed = exchange(packed)]
  transfers between devices with their start and end apart: 15 -> 1, of which waited for: 8 -> 1; matrix products, arithmetic and copies ran while one was open for 14% -> 2% of each run, Pallas kernels for 0% -> 0%
where the time goes in v1:
time: 121 us
  blocking collectives  56.9 us (47%)
  waiting for transfers between devices  31.6 us (26%)
  Pallas kernels  21.3 us (18%)
  starting transfers between devices  7.5 us (6%)
  local copies, waits for them, and re-layouts  2.52 us (2%)
    all_to_all x1, blocking collectives, whole_cluster(): packed = exchange(packed)  41.5 us
    all_to_all x1, waiting for transfers between devices, whole_cluster(): packed = exchange(packed)  31.6 us
    all_gather x1, blocking collectives, whole_cluster(): index = lax.all_gather(index, 'ctx', axis_index_groups=near, tiled=True)  15.4 us
    pallas_call x1, Pallas kernels, attend(): pl.pallas_call(attend_kernel, grid_spec=pltpu.PrefetchScalarGridSpec(num_...  15.1 us
    all_to_all x1, starting transfers between devices, whole_cluster(): packed = exchange(packed)  7.5 us
    pallas_call x1, Pallas kernels, whole_cluster(): pl.pallas_call(to_heads_kernel, out_shape=jax.ShapeDtypeStruct((features...  3.21 us
    pallas_call x1, Pallas kernels, whole_cluster(): pl.pallas_call(from_heads_kernel, out_shape=[jax.ShapeDtypeStruct(queries...  2.95 us
  transfers between devices with their start and end apart: 1, of which 1 were waited for; matrix products, arithmetic and copies ran while one was open for 2% of the time, Pallas kernels for 0%

profile of v1, /device:TPU:0, one launch (start us, length us, event | category | flops | bytes accessed | tf_op | source)
XLA Modules:
  0.0 120.7 jit_solution(9441915794078314698)
XLA Ops:
  0.6 3.2 %to_heads.1 = bf16[16,4,128,128]{3,2,1,0:T(8,128)(2,1)} custom-call(bf16[128,2048]{1,0:T(8,128)(2,1)} %refs_0_.1, bf16[128,2048]{1,0:T(8,128)(2,1)} %refs_1_.1, bf16[128,2048]{1,0:T(8,128)(2,1)} %refs_2_.1, bf16[128,2048]{1,0:T(8,128)(2,1)} %refs_3_.1), custom_call_target="tpu_custom_call" | custom-call | tf_op jit(solution)/shard_map/to_heads/pallas_call | solution.py:143
  3.8 0.0 copy-start.2
  3.8 0.0 copy-start.1
  3.8 0.0 copy-start
  3.8 7.5 %all-to-all-start = ((bf16[16,4,128,128]{3,2,1,0:T(8,128)(2,1)}), bf16[16,4,128,128]{3,2,1,0:T(8,128)(2,1)S(1)}, u32[]{:S(2)}, u32[]{:S(2)}) async-start(bf16[16,4,128,128]{3,2,1,0:T(8,128)(2,1)} %to_heads.1), calls=%async_computation | async-start | bytes 4194304 | tf_op jit(solution)/shard_map/all_to_all | solution.py:148
  11.4 0.0 copy-done.2
  11.4 0.1 copy.16
  11.5 0.0 copy-done.1
  11.5 0.1 copy.17
  11.6 0.1 reshape.68
  11.7 0.1 copy.18
  11.7 0.1 reshape.76
  11.8 0.0 copy-done
  11.8 0.3 dynamic-slice_reduce_fusion.1
  12.1 0.6 gather_fusion.1
  12.8 0.1 reshape.87
  12.9 0.6 gather_fusion
  13.5 0.1 reshape.85
  13.6 0.1 add_bitcast_fusion
  13.7 15.4 %all-gather = s32[4,4,6]{2,1,0:T(4,128)S(1)} all-gather(s32[1,4,6]{2,1,0:T(4,128)S(1)} %add_bitcast_fusion), channel_id=1, replica_groups={{0,4,8,12},{16,20,24,28},{1,5,9,13},{17,21,25,29},{2,6,10,14},{18,22,26..., dimensions={0}, use_global_device_ids=true | all-gather | bytes 480 | tf_op jit(solution)/shard_map/all_gather | solution.py:140
  29.1 0.1 reshape.65.index_ref
  29.2 31.6 %all-to-all-done = bf16[16,4,128,128]{3,2,1,0:T(8,128)(2,1)S(1)} async-done(((bf16[16,4,128,128]{3,2,1,0:T(8,128)(2,1)}), bf16[16,4,128,128]{3,2,1,0:T(8,128)(2,1)S(1)}, u32[]{:S(2)}, u32[]{:S(2)}) %all-to-all-start) | async-done | bytes 2097184 | tf_op jit(solution)/shard_map/all_to_all | solution.py:148
  60.8 0.2 fusion.2
  61.0 15.1 %attend.1 = (bf16[2048,128]{1,0:T(8,128)(2,1)S(1)}, bf16[2048,128]{1,0:T(8,128)(2,1)S(1)}, bf16[2048,128]{1,0:T(8,128)(2,1)S(1)}) custom-call(s32[96]{0:T(128)S(1)} %reshape.65.index_ref, bf16[2048,128]{1,0:T(8,128)(2,1)S(1)} %bitcast.20, bf16[2048,128]{1,0:T(8,128)(2,1)S(1)} %bitcast.19, bf16[2048,128]{1,0:T(8,128)(2,1)S(1)} %bitcast.18, ...), custom_call_target="tpu_custom_call" | custom-call | tf_op jit(solution)/shard_map/attend/pallas_call | solution.py:75
  76.1 0.2 pad_maximum_fusion
  76.3 41.5 %all_to_all.10.ref = bf16[16,3,128,128]{3,2,1,0:T(8,128)(2,1)} all-to-all(bf16[16,3,128,128]{3,2,1,0:T(8,128)(2,1)S(1)} %pad_maximum_fusion), channel_id=1, replica_groups={{0,1,2,3,4,5,6,7,8,9,10,11,12,13,14,15},{16,17,18,19,20,21,22,23,24,25,..., dimensions={0} | all-to-all | bytes 3145728 | tf_op jit(solution)/shard_map/all_to_all | solution.py:152
  117.8 3.0 %from_heads.1 = (bf16[128,2048]{1,0:T(8,128)(2,1)}, bf16[128,2048]{1,0:T(8,128)(2,1)}, bf16[128,2048]{1,0:T(8,128)(2,1)}) custom-call(bf16[16,3,128,128]{3,2,1,0:T(8,128)(2,1)} %all_to_all.10.ref), custom_call_target="tpu_custom_call" | custom-call | tf_op jit(solution)/shard_map/from_heads/pallas_call | solution.py:153
  (6 shorter events, 0.0 us)
Async XLA Ops:
  3.8 7.5 %copy-start.2 = (s32[4,2]{0,1:T(2,128)S(1)}, s32[4,2]{0,1:T(2,128)}, u32[]{:S(2)}) copy-start(s32[4,2]{0,1:T(2,128)} %param.11) | copy-start | bytes 100
  3.8 7.6 %copy-start.1 = (s32[4,2,2]{0,2,1:T(2,128)S(1)}, s32[4,2,2]{0,2,1:T(2,128)}, u32[]{:S(2)}) copy-start(s32[4,2,2]{0,2,1:T(2,128)} %param.13) | copy-start | bytes 196
  3.8 8.0 %copy-start = (s32[8,2,3]{0,1,2:T(2,128)S(1)}, s32[8,2,3]{0,1,2:T(2,128)}, u32[]{:S(2)}) copy-start(s32[8,2,3]{0,1,2:T(2,128)} %param.12) | copy-start | bytes 580
  3.8 56.9 %all-to-all-start = ((bf16[16,4,128,128]{3,2,1,0:T(8,128)(2,1)}), bf16[16,4,128,128]{3,2,1,0:T(8,128)(2,1)S(1)}, u32[]{:S(2)}, u32[]{:S(2)}) async-start(bf16[16,4,128,128]{3,2,1,0:T(8,128)(2,1)} %to_heads.1), calls=%async_computation | async-start | bytes 4194304 | tf_op jit(solution)/shard_map/all_to_all | solution.py:148

commit v2 on v1

--- a/solution.py
+++ b/solution.py
@@ -9,16 +9,316 @@
 
 DH = 128
 BLK = 128
+SCALE = DH**-0.5
 LOG2_E = 1.4426950408889634
 NT = (((1,), (1,)), ((), ()))
+VMEM_BYTES = 16 << 20
+IN_VMEM = pl.BlockSpec(memory_space=pltpu.VMEM)
+IN_SMEM = pl.BlockSpec(memory_space=pltpu.SMEM)
+INDEX_ROWS = 16
 
 
 def swapped(value, axis, distance):
-    return lax.ppermute(value, axis, [(i, i ^ 1 << distance) for i in range(lax.axis_size(axis))])
+    return lax.ppermute(value, axis, [(i, i ^ distance) for i in range(lax.axis_size(axis))])
 
 
 def rows(block):
-    return pl.ds(pl.multiple_of(block * BLK, BLK), BLK)
+    return pl.ds(block * BLK if isinstance(block, int) else pl.multiple_of(block * BLK, BLK), BLK)
+
+
+def head_lanes(head):
+    return pl.ds(pl.multiple_of(head * DH, DH), DH)
+
+
+def local_call(kernel, out_shape, scalars, arrays, scratch=(), flops=0):
+    moved = sum(x.size * x.dtype.itemsize for x in (*arrays, *jax.tree.leaves(out_shape)))
+    return pl.pallas_call(
+        kernel,
+        out_shape=out_shape,
+        in_specs=[IN_SMEM] * len(scalars) + [IN_VMEM] * len(arrays),
+        out_specs=jax.tree.map(lambda _: IN_VMEM, out_shape),
+        scratch_shapes=list(scratch),
+        compiler_params=pltpu.CompilerParams(vmem_limit_bytes=VMEM_BYTES),
+        cost_estimate=pl.CostEstimate(flops=flops, bytes_accessed=moved, transcendentals=0),
+        name=getattr(kernel, "func", kernel).__name__,
+    )(*scalars, *arrays)
+
+
+def parts_of(blocks, count, extra=0):
+    return [jax.ShapeDtypeStruct((blocks * BLK + extra, DH), jnp.bfloat16)] * count
+
+
+def natural(me_ref, i, n, by, parts):
+    k, j = (i, n) if by == "ctx" else (n, i)
+    return jnp.bitwise_xor(me_ref[0], k) * parts + jnp.bitwise_xor(me_ref[1], j)
+
+
+def pack(me_ref, *refs, arrays, others, by, parts):
+    ins, outs = refs[:arrays], refs[arrays:]
+    for i, out in enumerate(outs):
+        for n in range(others):
+            lanes = head_lanes(natural(me_ref, i, n, by, parts))
+            for place, ref in enumerate(ins):
+                out[rows(place * others + n), :] = ref[:, lanes]
+
+
+def pack_with_index(me_ref, offsets_ref, pool_ref, picks_ref, *refs, parts, **kwargs):
+    pack(me_ref, *refs, by="ctx", parts=parts, **kwargs)
+    row = lax.broadcasted_iota(jnp.int32, (INDEX_ROWS, DH), 0)
+    lane = lax.broadcasted_iota(jnp.int32, (INDEX_ROWS, DH), 1)
+    tile = jnp.zeros((INDEX_ROWS, DH), jnp.int32)
+    for block in range(parts):
+        local = [offsets_ref[block, n] for n in range(offsets_ref.shape[1])]
+        chosen = [me_ref[0] * parts + jnp.bitwise_and(block + offset, parts - 1) for offset in local]
+        for bit in range(picks_ref.shape[1]):
+            far = jnp.bitwise_xor(me_ref[0], 1 << bit) * parts
+            for n in range(picks_ref.shape[2]):
+                chosen.append(far + pool_ref[me_ref[2], bit, picks_ref[block, bit, n]])
+        for n, value in enumerate(chosen):
+            tile = jnp.where((row == block) & (lane == n), value, tile)
+    for out in refs[kwargs["arrays"] :]:
+        out[out.shape[0] - INDEX_ROWS :, :] = tile.astype(jnp.float32).astype(out.dtype)
+
+
+def unpack(me_ref, *refs, by, parts):
+    *ins, out = refs
+    for i, ref in enumerate(ins):
+        for n in range(ref.shape[0] // BLK):
+            out[:, head_lanes(natural(me_ref, i, n, by, parts))] = ref[rows(n), :]
+
+
+def pack_natural(*refs):
+    *ins, out = refs
+    for head in range(ins[0].shape[1] // DH):
+        for place, ref in enumerate(ins):
+            out[rows(head * len(ins) + place), :] = ref[:, head * DH : (head + 1) * DH]
+
+
+def unpack_natural(ref, *outs):
+    for head in range(outs[0].shape[1] // DH):
+        for place, out in enumerate(outs):
+            out[:, head * DH : (head + 1) * DH] = ref[rows(head * len(outs) + place), :]
+
+
+def regroup(*refs, count, places):
+    ins, outs = refs[:count], refs[count:]
+    for i, out in enumerate(outs):
+        for n, place in enumerate(places):
+            for k, ref in enumerate(ins):
+                out[rows(n * count + k), :] = ref[rows(place * len(outs) + i), :]
+
+
+def regroup_with_index(*refs, count, places):
+    *refs, index_ref = refs
+    regroup(*refs, count=count, places=places)
+    for k, ref in enumerate(refs[:count]):
+        tile = ref[ref.shape[0] - INDEX_ROWS :, :]
+        index_ref[k * INDEX_ROWS : (k + 1) * INDEX_ROWS, :] = tile.astype(jnp.float32).astype(jnp.int32)
+
+
+def gather(me_ref, table, refs, by, parts, place=0):
+    others = table.shape[0] // len(refs)
+    for i, ref in enumerate(refs):
+        for n in range(others):
+            table[natural(me_ref, i, n, by, parts)] = ref[rows(place * others + n), :]
+
+
+def spread(me_ref, table, refs, by, parts):
+    others = table.shape[0] // len(refs)
+    for i, ref in enumerate(refs):
+        for n in range(others):
+            ref[rows(n), :] = table[natural(me_ref, i, n, by, parts)].astype(ref.dtype)
+
+
+def chosen_blocks(me_ref, index_ref, block, parts, key_count):
+    group = jnp.bitwise_xor(lax.div(block, parts), me_ref[0])
+    row = group * INDEX_ROWS + lax.rem(block, parts)
+    return [index_ref[row, j] for j in range(key_count)]
+
+
+def pair_of(block_of, first, second):
+    return jnp.concatenate(
+        [jnp.concatenate([block_of(a), block_of(b)], axis=1) for a, b in zip(first, second, strict=True)], axis=0
+    )
+
+
+def set_diagonal(ref, first, second):
+    ref[:BLK, :DH] = first
+    ref[BLK:, DH:] = second
+
+
+def add_pair(acc, chosen, values):
+    for half, blocks in enumerate(chosen):
+        for j, block in enumerate(blocks):
+            acc[block] += values[j * BLK : (j + 1) * BLK, half * DH : (half + 1) * DH]
+
+
+def for_pairs(me_ref, index_ref, count, parts, key_count, unroll, one):
+    def step(i, _):
+        for slot in range(unroll):
+            pair = i * unroll + slot
+            blocks = (2 * pair, 2 * pair + 1)
+            one(pair, slot, blocks, [chosen_blocks(me_ref, index_ref, b, parts, key_count) for b in blocks])
+        return 0
+
+    lax.fori_loop(0, count // unroll, step, 0)
+
+
+def joined_block(ref, blocks, place):
+    arrays = ref.shape[0] // (blocks * BLK)
+    return lambda b: ref[rows(b * arrays + place), :]
+
+
+def softmax_weights(me_ref, index_ref, joined_ref, w_ref, half_ref, q_diag, *, parts, near, key_count, unroll):
+    query, key = (joined_block(joined_ref, near * parts, place) for place in range(2))
+    q_diag[...] = jnp.zeros_like(q_diag)
+
+    def one(pair, slot, blocks, chosen):
+        set_diagonal(q_diag.at[slot], *map(query, blocks))
+        keys = pair_of(key, *chosen)
+        scores = lax.dot_general(keys, q_diag[slot], NT, preferred_element_type=jnp.float32)
+        row_max = jnp.max(scores, axis=0, keepdims=True)
+        exp_scores = jnp.exp2((scores - row_max) * (SCALE * LOG2_E))
+        weights = exp_scores * (1.0 / jnp.sum(exp_scores, axis=0, keepdims=True))
+        w_ref[pair] = weights
+        half_ref[pair] = weights.astype(half_ref.dtype)
+
+    for_pairs(me_ref, index_ref, w_ref.shape[0], parts, key_count, unroll, one)
+
+
+def dv_parts(me_ref, index_ref, half_ref, *refs, parts, near, key_count, unroll):
+    g_refs, dv_refs, (acc, g_table, g_diag) = refs[:parts], refs[parts : 2 * parts], refs[2 * parts :]
+    gather(me_ref, g_table, g_refs, "head", parts)
+    for ref in (acc, g_diag):
+        ref[...] = jnp.zeros_like(ref)
+
+    def one(pair, slot, blocks, chosen):
+        set_diagonal(g_diag.at[slot], *(g_table[b] for b in blocks))
+        add_pair(acc, chosen, jnp.dot(half_ref[pair], g_diag[slot], preferred_element_type=jnp.float32))
+
+    for_pairs(me_ref, index_ref, half_ref.shape[0], parts, key_count, unroll, one)
+    spread(me_ref, acc, dv_refs, "head", parts)
+
+
+def dq_and_dk(me_ref, index_ref, joined_ref, *refs, parts, near, key_count, unroll):
+    g_refs, v_refs, refs = refs[:parts], refs[parts : 2 * parts], refs[2 * parts :]
+    w_ref, out_ref, acc, k_table, g_table, v_table, q_diag, g_diag = refs
+    gather(me_ref, g_table, g_refs, "head", parts)
+    gather(me_ref, v_table, v_refs, "head", parts)
+    for ref in (acc, q_diag, g_diag):
+        ref[...] = jnp.zeros_like(ref)
+    query, key = (joined_block(joined_ref, near * parts, place) for place in range(2))
+    for block in range(k_table.shape[0]):
+        k_table[block] = key(block).T
+
+    def one(pair, slot, blocks, chosen):
+        set_diagonal(q_diag.at[slot], *map(query, blocks))
+        set_diagonal(g_diag.at[slot], *(g_table[b] for b in blocks))
+        values = pair_of(lambda b: v_table[b], *chosen)
+        prob_grad = lax.dot_general(values, g_diag[slot], NT, preferred_element_type=jnp.float32)
+        weights = w_ref[pair]
+        row_delta = jnp.sum(weights * prob_grad, axis=0, keepdims=True)
+        score_grad = (SCALE * (weights * (prob_grad - row_delta))).astype(jnp.bfloat16)
+        add_pair(acc, chosen, jnp.dot(score_grad, q_diag[slot], preferred_element_type=jnp.float32))
+        for half, block in enumerate(blocks):
+            turned = jnp.concatenate([k_table[b] for b in chosen[half]], axis=1)
+            own = score_grad[:, half * BLK : (half + 1) * BLK]
+            grad = jnp.dot(turned, own, preferred_element_type=jnp.float32).T
+            out_ref[rows(2 * block), :] = grad.astype(out_ref.dtype)
+
+    for_pairs(me_ref, index_ref, w_ref.shape[0], parts, key_count, unroll, one)
+    for block in range(acc.shape[0]):
+        out_ref[rows(2 * block + 1), :] = acc[block].astype(out_ref.dtype)
+
+
+def whole_cluster(
+    queries, key_vecs, value_vecs, out_grads, local_offsets, partner_pool, partner_picks
+):
+    bits = partner_pool.shape[1]
+    parts = lax.axis_size("head")
+    near = 1 << bits
+    cluster = near * parts
+    key_count = local_offsets.shape[1] + bits * partner_picks.shape[2]
+    group = lax.axis_index("ctx")
+    me = jnp.stack([jnp.bitwise_and(group, near - 1), lax.axis_index("head"), group]).astype(jnp.int32)
+
+    def over_ctx(by_part):
+        return [x if k == 0 else swapped(x, "ctx", k) for k, x in enumerate(by_part)]
+
+    def over_head(by_part):
+        return [x if j == 0 else swapped(x, "head", j) for j, x in enumerate(by_part)]
+
+    members = [
+        [member * parts + part for member in range(first, first + near) for part in range(parts)]
+        for first in range(0, lax.axis_size("ctx"), near)
+    ]
+    exchange = functools.partial(
+        lax.all_to_all, axis_name=("ctx", "head"), split_axis=0, concat_axis=0, tiled=True, axis_index_groups=members
+    )
+    joined = local_call(pack_natural, parts_of(2 * cluster, 1)[0], (), (queries, key_vecs))
+    later = (out_grads, value_vecs, local_offsets, partner_pool, partner_picks)
+    joined, later = lax.optimization_barrier((joined, later))
+    out_grads, value_vecs, local_offsets, partner_pool, partner_picks = later
+    joined = exchange(joined)
+    grad = local_call(
+        functools.partial(pack, arrays=1, others=parts, by="ctx", parts=parts), parts_of(parts, near), (me,), (out_grads,)
+    )
+    grad = local_call(functools.partial(regroup, count=near, places=[0]), parts_of(near, parts), (), over_ctx(grad))
+    grad = over_head(grad)
+    value = local_call(
+        functools.partial(pack_with_index, arrays=1, others=parts, parts=parts),
+        parts_of(parts, near, INDEX_ROWS),
+        (me, local_offsets, partner_pool, partner_picks),
+        (value_vecs,),
+    )
+    *value, index = local_call(
+        functools.partial(regroup_with_index, count=near, places=[0]),
+        parts_of(near, parts) + [jax.ShapeDtypeStruct((near * INDEX_ROWS, DH), jnp.int32)],
+        (),
+        over_ctx(value),
+    )
+    joined, value = lax.optimization_barrier((joined, value))
+    value = over_head(value)
+
+    pairs, keys = cluster // 2, key_count * BLK
+    unroll = 4 if pairs % 4 == 0 else 1
+    kwargs = dict(parts=parts, near=near, key_count=key_count, unroll=unroll)
+    flops = 4 * cluster * keys * BLK * DH
+    acc, table = (pltpu.VMEM((cluster, BLK, DH), dtype) for dtype in (jnp.float32, jnp.bfloat16))
+    diagonal = pltpu.VMEM((unroll, 2 * BLK, 2 * DH), jnp.bfloat16)
+    weights, half = local_call(
+        functools.partial(softmax_weights, **kwargs),
+        [jax.ShapeDtypeStruct((pairs, keys, 2 * BLK), dtype) for dtype in (jnp.float32, jnp.bfloat16)],
+        (me, index),
+        (joined,),
+        [diagonal],
+        flops // 2,
+    )
+    dv = local_call(
+        functools.partial(dv_parts, **kwargs),
+        parts_of(near, parts),
+        (me, index),
+        (half, *grad),
+        [acc, table, diagonal],
+        flops // 2,
+    )
+    dv = over_head(dv)
+    joined = local_call(
+        functools.partial(dq_and_dk, **kwargs),
+        parts_of(2 * cluster, 1)[0],
+        (me, index),
+        (joined, *grad, *value, weights),
+        [acc] + [table] * 3 + [diagonal] * 2,
+        flops * 3 // 2,
+    )
+    joined, dv = lax.optimization_barrier((joined, dv))
+    joined = exchange(joined)
+    dv = local_call(functools.partial(regroup, count=parts, places=[0]), parts_of(parts, near), (), dv)
+    dv = over_ctx(dv)
+    out = jax.ShapeDtypeStruct(queries.shape, queries.dtype)
+    value_grads = local_call(functools.partial(unpack, by="ctx", parts=parts), out, (me,), dv)
+    query_grads, key_grads = local_call(unpack_natural, [out] * 2, (), (joined,))
+    return query_grads, key_grads, value_grads
 
 
 def attend_kernel(
@@ -27,7 +327,6 @@
     query_blocks = q_ref.shape[0] // BLK
     table_blocks = k_ref.shape[0] // BLK
     key_count = k_cat.shape[0] // BLK
-    scale = DH**-0.5
 
     acc_k[...] = jnp.zeros_like(acc_k)
     acc_v[...] = jnp.zeros_like(acc_v)
@@ -45,11 +344,11 @@
             kt_cat[:, part] = k_turned[chosen[j]]
         scores = lax.dot_general(k_cat[...], query, NT, preferred_element_type=jnp.float32)
         row_max = jnp.max(scores, axis=0, keepdims=True)
-        exp_scores = jnp.exp2((scores - row_max) * (scale * LOG2_E))
+        exp_scores = jnp.exp2((scores - row_max) * (SCALE * LOG2_E))
         weights = exp_scores * (1.0 / jnp.sum(exp_scores, axis=0, keepdims=True))
         prob_grad = lax.dot_general(v_cat[...], grad, NT, preferred_element_type=jnp.float32)
         row_delta = jnp.sum(weights * prob_grad, axis=0, keepdims=True)
-        score_grad = (scale * weights * (prob_grad - row_delta)).astype(jnp.bfloat16)
+        score_grad = (SCALE * weights * (prob_grad - row_delta)).astype(jnp.bfloat16)
         weights_half = weights.astype(jnp.bfloat16)
         query_turned = jnp.dot(kt_cat[...], score_grad, preferred_element_type=jnp.float32)
         dq_ref[rows(block), :] = query_turned.T.astype(jnp.bfloat16)
@@ -93,68 +392,9 @@
             jax.ShapeDtypeStruct(key.shape, table_type),
             jax.ShapeDtypeStruct(key.shape, table_type),
         ],
-        compiler_params=pltpu.CompilerParams(vmem_limit_bytes=40 << 20),
+        compiler_params=pltpu.CompilerParams(vmem_limit_bytes=VMEM_BYTES),
         name="attend",
     )(index.reshape(-1), query, key, value, grad)
-
-
-def to_heads_kernel(*refs):
-    *ins, out = refs
-    for place, ref in enumerate(ins):
-        for head in range(out.shape[0]):
-            out[head, place] = ref[:, head * DH : (head + 1) * DH]
-
-
-def from_heads_kernel(ref, *outs):
-    for place, out in enumerate(outs):
-        for head in range(ref.shape[0]):
-            out[:, head * DH : (head + 1) * DH] = ref[head, place]
-
-
-def whole_cluster(
-    queries, key_vecs, value_vecs, out_grads, local_offsets, partner_pool, partner_picks
-):
-    bits = partner_pool.shape[1]
-    groups, parts = lax.axis_size("ctx"), lax.axis_size("head")
-    tokens, features = queries.shape
-    cluster = (parts << bits)
-    heads = features // DH // cluster
-    members = [
-        [group * parts + part for group in range(first, first + (1 << bits)) for part in range(parts)]
-        for first in range(0, groups, 1 << bits)
-    ]
-    exchange = functools.partial(
-        lax.all_to_all, axis_name=("ctx", "head"), split_axis=0, concat_axis=0, tiled=True, axis_index_groups=members
-    )
-    group = lax.axis_index("ctx")
-    blocks = parts * (tokens // BLK)
-    inner = jnp.arange(blocks, dtype=jnp.int32)
-    place = jnp.bitwise_and(group, (1 << bits) - 1)
-    own = place * blocks + (inner[:, None] + local_offsets) % blocks
-    far = []
-    for bit in range(bits):
-        pool = partner_pool[group, bit]
-        far.append(jnp.bitwise_xor(place, 1 << bit) * blocks + pool[partner_picks[:, bit]])
-    index = jnp.concatenate([own] + far, axis=1).astype(jnp.int32)
-    near = [list(range(first, first + (1 << bits))) for first in range(0, groups, 1 << bits)]
-    index = lax.all_gather(index, "ctx", axis_index_groups=near, tiled=True)
-
-    arrays = (queries, key_vecs, value_vecs, out_grads)
-    packed = pl.pallas_call(
-        to_heads_kernel,
-        out_shape=jax.ShapeDtypeStruct((features // DH, len(arrays), tokens, DH), queries.dtype),
-        name="to_heads",
-    )(*arrays)
-    packed = exchange(packed)
-    query, key, value, grad = (packed[:, n].reshape(cluster * tokens, DH) for n in range(4))
-    results = attend(index, query, key, value, grad, jnp.bfloat16)
-    packed = jnp.stack([r.reshape(cluster, tokens, DH) for r in results], axis=1)
-    packed = exchange(packed)
-    return pl.pallas_call(
-        from_heads_kernel,
-        out_shape=[jax.ShapeDtypeStruct(queries.shape, queries.dtype)] * 3,
-        name="from_heads",
-    )(packed)
 
 
 def by_pools(
@@ -171,7 +411,7 @@
 
     def table(array):
         by_block = array.reshape(blocks, BLK, width)
-        far = [swapped(by_block[asked[bit]], "ctx", bit) for bit in range(bits)]
+        far = [swapped(by_block[asked[bit]], "ctx", 1 << bit) for bit in range(bits)]
         return jnp.concatenate([by_block] + far).reshape(-1, width)
 
     inner = jnp.arange(blocks, dtype=jnp.int32)
@@ -185,17 +425,18 @@
         total = by_block[:blocks]
         for bit in range(bits):
             lower = blocks + bit * pool_size
-            back = swapped(by_block[lower : lower + pool_size], "ctx", bit)
+            back = swapped(by_block[lower : lower + pool_size], "ctx", 1 << bit)
             total = total.at[asked[bit]].add(back)
         grads.append(total.reshape(blocks * BLK, width).astype(jnp.bfloat16))
     return tuple(to_tokens(x) for x in grads)
 
 
 def per_device(*args):
-    partner_pool = args[5]
-    cluster = lax.axis_size("head") << partner_pool.shape[1]
-    if args[0].shape[1] // DH == cluster and args[0].shape[0] == BLK:
-        return tuple(whole_cluster(*args))
+    tokens, features = args[0].shape
+    parts = lax.axis_size("head")
+    cluster = parts << args[5].shape[1]
+    if features // DH == cluster and tokens == BLK and parts & (parts - 1) == 0 and 1 < parts <= INDEX_ROWS:
+        return whole_cluster(*args)
     return by_pools(*args)
 
 

time: 121 us -> 104 us (0.86)
  blocking collectives: 56.9 us -> 0 us
  starting transfers between devices: 7.5 us -> 32.6 us
  waiting for transfers between devices: 31.6 us -> 42.2 us
  local copies, waits for them, and re-layouts: 2.52 us -> 6.47 us
    all_to_all x1 -> x0, blocking collectives: 41.5 us -> none  [whole_cluster(): packed = exchange(packed)]
    ppermute x0 -> x18, waiting for transfers between devices: none -> 33.2 us  [swapped(): lax.ppermute(value, axis, [(i, i ^ distance) for i in range(lax.axis_size...]
    all_to_all x1 -> x2, waiting for transfers between devices: 31.6 us -> 9.03 us  [whole_cluster(): joined = exchange(joined)]
    ppermute x0 -> x18, starting transfers between devices: none -> 20.6 us  [swapped(): lax.ppermute(value, axis, [(i, i ^ distance) for i in range(lax.axis_size...]
    all_gather x1 -> x0, blocking collectives: 15.4 us -> none  [whole_cluster(): index = lax.all_gather(index, 'ctx', axis_index_groups=near, tiled=True)]
    all_to_all x1 -> x2, starting transfers between devices: 7.5 us -> 12.1 us  [whole_cluster(): joined = exchange(joined)]
    unnamed x7 -> x8, local copies, waits for them, and re-layouts: 0.1 us -> 4.16 us
    optimization_barrier x0 -> x3, local copies, waits for them, and re-layouts: none -> 2.31 us  [whole_cluster(): joined, later = lax.optimization_barrier((joined, later))]
  transfers between devices with their start and end apart: 1 -> 20, of which waited for: 1 -> 9; matrix products, arithmetic and copies ran while one was open for 2% -> 2% of each run, Pallas kernels for 0% -> 19%
where the time goes in v2:
time: 104 us
  waiting for transfers between devices  42.2 us (41%)
  starting transfers between devices  32.6 us (31%)
  Pallas kernels  21.7 us (21%)
  local copies, waits for them, and re-layouts  6.47 us (6%)
    ppermute x18, waiting for transfers between devices, swapped(): lax.ppermute(value, axis, [(i, i ^ distance) for i in range(lax.axis_size...  33.2 us
    pallas_call x11, Pallas kernels, local_call(): pl.pallas_call(kernel, out_shape=out_shape, in_specs=[IN_SMEM] * len(scal...  21.7 us
    ppermute x18, starting transfers between devices, swapped(): lax.ppermute(value, axis, [(i, i ^ distance) for i in range(lax.axis_size...  20.6 us
    all_to_all x2, starting transfers between devices, whole_cluster(): joined = exchange(joined)  12.1 us
    all_to_all x2, waiting for transfers between devices, whole_cluster(): joined = exchange(joined)  9.03 us
    unnamed x8, local copies, waits for them, and re-layouts  4.16 us
    optimization_barrier x3, local copies, waits for them, and re-layouts, whole_cluster(): joined, later = lax.optimization_barrier((joined, later))  2.31 us
  transfers between devices with their start and end apart: 20, of which 9 were waited for; matrix products, arithmetic and copies ran while one was open for 2% of the time, Pallas kernels for 19%

profile of v2, /device:TPU:0, one launch (start us, length us, event | category | flops | bytes accessed | tf_op | source)
XLA Modules:
  0.0 103.8 jit_solution(6447270706819006116)
XLA Ops:
  0.6 1.0 copy-done.2
  1.7 1.0 %copy-done.3 = bf16[128,2048]{1,0:T(8,128)(2,1)S(1)} copy-done((bf16[128,2048]{1,0:T(8,128)(2,1)S(1)}, bf16[128,2048]{1,0:T(8,128)(2,1)}, u32[]{:S(2)}) %copy-start.3) | copy-done | bytes 524312
  2.7 1.2 %pack_natural.1 = bf16[4096,128]{1,0:T(8,128)(2,1)} custom-call(bf16[128,2048]{1,0:T(8,128)(2,1)S(1)} %copy-done.2, bf16[128,2048]{1,0:T(8,128)(2,1)S(1)} %copy-done.3), custom_call_target="tpu_custom_call" | custom-call | bytes 2097152 | tf_op jit(solution)/shard_map/pack_natural/pallas_call | solution.py:35
  3.9 7.4 %all-to-all-start = ((bf16[16,256,128]{2,1,0:T(8,128)(2,1)}), bf16[16,256,128]{2,1,0:T(8,128)(2,1)S(1)}, u32[]{:S(2)}, u32[]{:S(2)}) async-start(bf16[16,256,128]{2,1,0:T(8,128)(2,1)} %bitcast.3), calls=%async_computation | async-start | bytes 2097152 | tf_op jit(solution)/shard_map/all_to_all | solution.py:262
  11.2 0.1 pad_add_fusion.me_ref
  11.3 1.0 %copy-done = bf16[128,2048]{1,0:T(8,128)(2,1)S(1)} copy-done((bf16[128,2048]{1,0:T(8,128)(2,1)S(1)}, bf16[128,2048]{1,0:T(8,128)(2,1)}, u32[]{:S(2)}) %copy-start) | copy-done | bytes 524312
  12.4 0.7 pack.1
  13.1 0.5 collective-permute-start.3
  13.5 1.7 %collective-permute-start.4 = (bf16[512,128]{1,0:T(8,128)(2,1)S(1)}, bf16[512,128]{1,0:T(8,128)(2,1)S(1)}, u32[]{:S(2)}, u32[]{:S(2)}) collective-permute-start(bf16[512,128]{1,0:T(8,128)(2,1)S(1)} %get-tuple-element.66), channel_id=1, source_target_pairs={{0,8},{4,12},{8,0},{12,4},{16,24},{20,28},{24,16},{28,20},{1,9},{5... | collective-permute-start | bytes 393224 | tf_op jit(solution)/shard_map/ppermute | solution.py:22
  15.2 0.8 copy.11.pool_ref
  16.0 0.8 copy.12.picks_ref
  16.8 0.8 copy.10.offsets_ref
  17.5 1.0 %copy-done.1 = bf16[128,2048]{1,0:T(8,128)(2,1)S(1)} copy-done((bf16[128,2048]{1,0:T(8,128)(2,1)S(1)}, bf16[128,2048]{1,0:T(8,128)(2,1)}, u32[]{:S(2)}) %copy-start.1) | copy-done | bytes 524312
  18.6 1.0 pack_with_index.1
  19.5 0.5 collective-permute-start
  20.0 1.7 %collective-permute-start.1 = (bf16[528,128]{1,0:T(8,128)(2,1)S(1)}, bf16[528,128]{1,0:T(8,128)(2,1)S(1)}, u32[]{:S(2)}, u32[]{:S(2)}) collective-permute-start(bf16[528,128]{1,0:T(8,128)(2,1)S(1)} %get-tuple-element.54), channel_id=1, source_target_pairs={{0,8},{4,12},{8,0},{12,4},{16,24},{20,28},{24,16},{28,20},{1,9},{5... | collective-permute-start | bytes 405512 | tf_op jit(solution)/shard_map/ppermute | solution.py:22
  21.7 0.0 collective-permute-done.3.refs_1_
  21.7 0.0 collective-permute-start.2
  21.7 5.7 %collective-permute-done.4.refs_2_ = bf16[512,128]{1,0:T(8,128)(2,1)S(1)} collective-permute-done((bf16[512,128]{1,0:T(8,128)(2,1)S(1)}, bf16[512,128]{1,0:T(8,128)(2,1)S(1)}, u32[]{:S(2)}, u32[]{:S(2)}) %collective-permute-start.4) | collective-permute-done | bytes 131104 | tf_op jit(solution)/shard_map/ppermute | solution.py:22
  27.5 2.6 %collective-permute-done.5.refs_3_ = bf16[512,128]{1,0:T(8,128)(2,1)S(1)} collective-permute-done((bf16[512,128]{1,0:T(8,128)(2,1)S(1)}, bf16[512,128]{1,0:T(8,128)(2,1)S(1)}, u32[]{:S(2)}, u32[]{:S(2)}) %collective-permute-start.5) | collective-permute-done | bytes 131104 | tf_op jit(solution)/shard_map/ppermute | solution.py:22
  30.1 0.1 collective-permute-start.6
  30.2 4.6 %collective-permute-start.7 = (bf16[512,128]{1,0:T(8,128)(2,1)S(1)}, bf16[512,128]{1,0:T(8,128)(2,1)S(1)}, u32[]{:S(2)}, u32[]{:S(2)}) collective-permute-start(bf16[512,128]{1,0:T(8,128)(2,1)S(1)} %get-tuple-element.70), channel_id=1, source_target_pairs={{0,2},{1,3},{2,0},{3,1},{4,6},{5,7},{6,4},{7,5},{8,10},{9,11},{10,... | collective-permute-start | bytes 393224 | tf_op jit(solution)/shard_map/ppermute | solution.py:22
  34.8 0.0 collective-permute-done.refs_1_
  34.8 0.0 collective-permute-start.8
  34.8 0.0 collective-permute-done.1.refs_2_
  34.8 1.1 %collective-permute-done.2.refs_3_ = bf16[528,128]{1,0:T(8,128)(2,1)S(1)} collective-permute-done((bf16[528,128]{1,0:T(8,128)(2,1)S(1)}, bf16[528,128]{1,0:T(8,128)(2,1)S(1)}, u32[]{:S(2)}, u32[]{:S(2)}) %collective-permute-start.2) | collective-permute-done | bytes 135200 | tf_op jit(solution)/shard_map/ppermute | solution.py:22
  35.9 2.3 %all-to-all-done = bf16[16,256,128]{2,1,0:T(8,128)(2,1)S(1)} async-done(((bf16[16,256,128]{2,1,0:T(8,128)(2,1)}), bf16[16,256,128]{2,1,0:T(8,128)(2,1)S(1)}, u32[]{:S(2)}, u32[]{:S(2)}) %all-to-all-start) | async-done | bytes 1048608 | tf_op jit(solution)/shard_map/all_to_all | solution.py:262
  38.2 1.2 %collective-permute-start.10 = (bf16[512,128]{1,0:T(8,128)(2,1)S(1)}, bf16[512,128]{1,0:T(8,128)(2,1)S(1)}, u32[]{:S(2)}, u32[]{:S(2)}) collective-permute-start(bf16[512,128]{1,0:T(8,128)(2,1)S(1)} %get-tuple-element.74), channel_id=1, source_target_pairs={{0,2},{1,3},{2,0},{3,1},{4,6},{5,7},{6,4},{7,5},{8,10},{9,11},{10,... | collective-permute-start | bytes 393224 | tf_op jit(solution)/shard_map/ppermute | solution.py:22
  39.4 1.0 collective-permute-start.11
  40.5 0.0 collective-permute-done.6.refs_1_
  40.5 1.2 %collective-permute-start.9 = (bf16[512,128]{1,0:T(8,128)(2,1)S(1)}, bf16[512,128]{1,0:T(8,128)(2,1)S(1)}, u32[]{:S(2)}, u32[]{:S(2)}) collective-permute-start(bf16[512,128]{1,0:T(8,128)(2,1)S(1)} %get-tuple-element.73), channel_id=1, source_target_pairs={{0,1},{1,0},{2,3},{3,2},{4,5},{5,4},{6,7},{7,6},{8,9},{9,8},{10,11... | collective-permute-start | bytes 393224 | tf_op jit(solution)/shard_map/ppermute | solution.py:22
  41.7 4.1 %softmax_weights.1 = (f32[8,768,256]{2,1,0:T(8,128)S(1)}, bf16[8,768,256]{2,1,0:T(8,128)(2,1)S(1)}) custom-call(s32[3]{0:T(128)S(1)} %pad_add_fusion.me_ref, s32[64,128]{1,0:T(8,128)S(1)} %get-tuple-element.56.index_ref, bf16[4096,128]{1,0:T(8,128)(2,1)S(1)} %bitcast.7), custom_call_target="tpu_custom_call" | custom-call | flops 402653184 | bytes 10485760 | tf_op jit(solution)/shard_map/softmax_weights/pallas_call | solution.py:35
  45.8 6.5 %collective-permute-done.7.refs_2_ = bf16[512,128]{1,0:T(8,128)(2,1)S(1)} collective-permute-done((bf16[512,128]{1,0:T(8,128)(2,1)S(1)}, bf16[512,128]{1,0:T(8,128)(2,1)S(1)}, u32[]{:S(2)}, u32[]{:S(2)}) %collective-permute-start.7) | collective-permute-done | bytes 131104 | tf_op jit(solution)/shard_map/ppermute | solution.py:22
  52.3 2.9 %dv_parts.1 = (bf16[512,128]{1,0:T(8,128)(2,1)S(1)}, bf16[512,128]{1,0:T(8,128)(2,1)S(1)}, bf16[512,128]{1,0:T(8,128)(2,1)S(1)}, bf16[512,128]{1,0:T(8,128)(2,1)S(1)}) custom-call(s32[3]{0:T(128)S(1)} %pad_add_fusion.me_ref, s32[64,128]{1,0:T(8,128)S(1)} %get-tuple-element.56.index_ref, bf16[8,768,256]{2,1,0:T(8,128)(2,1)S(1)} %get-tuple-element.77.half_ref, ...), custom_call_target="tpu_custom_call" | custom-call | flops 402653184 | bytes 4194304 | tf_op jit(solution)/shard_map/dv_parts/pallas_call | solution.py:35
  55.2 3.4 %collective-permute-start.12 = (bf16[512,128]{1,0:T(8,128)(2,1)S(1)}, bf16[512,128]{1,0:T(8,128)(2,1)S(1)}, u32[]{:S(2)}, u32[]{:S(2)}) collective-permute-start(bf16[512,128]{1,0:T(8,128)(2,1)S(1)} %get-tuple-element.79), channel_id=1, source_target_pairs={{0,1},{1,0},{2,3},{3,2},{4,5},{5,4},{6,7},{7,6},{8,9},{9,8},{10,11... | collective-permute-start | bytes 393224 | tf_op jit(solution)/shard_map/ppermute | solution.py:22
  58.6 2.4 %collective-permute-start.14 = (bf16[512,128]{1,0:T(8,128)(2,1)S(1)}, bf16[512,128]{1,0:T(8,128)(2,1)S(1)}, u32[]{:S(2)}, u32[]{:S(2)}) collective-permute-start(bf16[512,128]{1,0:T(8,128)(2,1)S(1)} %get-tuple-element.81), channel_id=1, source_target_pairs={{0,3},{1,2},{2,1},{3,0},{4,7},{5,6},{6,5},{7,4},{8,11},{9,10},{10,... | collective-permute-start | bytes 393224 | tf_op jit(solution)/shard_map/ppermute | solution.py:22
  61.1 0.0 collective-permute-done.11.refs_7_
  61.1 0.0 collective-permute-done.9.refs_5_
  61.1 9.1 %dq_and_dk.1 = bf16[4096,128]{1,0:T(8,128)(2,1)} custom-call(s32[3]{0:T(128)S(1)} %pad_add_fusion.me_ref, s32[64,128]{1,0:T(8,128)S(1)} %get-tuple-element.56.index_ref, bf16[4096,128]{1,0:T(8,128)(2,1)S(1)} %bitcast.8, bf16[512,128]{1,0:T(8,128)(2,1)S(1)} %get-tuple-element.68.refs_0_, bf16[512,128]{1,0:T(8,128)(2,1)S(1)} %collective-permute-done.6.refs_1_, ...), custom_call_target="tpu_custom_call" | custom-call | flops 1207959552 | bytes 9437184 | tf_op jit(solution)/shard_map/dq_and_dk/pallas_call | solution.py:35
  70.2 0.7 collective-permute-done.13.refs_2_
  70.9 4.7 %all-to-all-start.1 = ((bf16[16,256,128]{2,1,0:T(8,128)(2,1)}), bf16[16,256,128]{2,1,0:T(8,128)(2,1)S(1)}, u32[]{:S(2)}, u32[]{:S(2)}) async-start(bf16[16,256,128]{2,1,0:T(8,128)(2,1)} %bitcast.5), calls=%async_computation.1 | async-start | bytes 2097152 | tf_op jit(solution)/shard_map/all_to_all | solution.py:315
  75.6 0.5 collective-permute-start.15
  76.1 1.7 %collective-permute-start.16 = (bf16[512,128]{1,0:T(8,128)(2,1)S(1)}, bf16[512,128]{1,0:T(8,128)(2,1)S(1)}, u32[]{:S(2)}, u32[]{:S(2)}) collective-permute-start(bf16[512,128]{1,0:T(8,128)(2,1)S(1)} %get-tuple-element.91), channel_id=1, source_target_pairs={{0,8},{4,12},{8,0},{12,4},{16,24},{20,28},{24,16},{28,20},{1,9},{5... | collective-permute-start | bytes 393224 | tf_op jit(solution)/shard_map/ppermute | solution.py:22
  77.8 14.0 %collective-permute-done.16.refs_2_ = bf16[512,128]{1,0:T(8,128)(2,1)S(1)} collective-permute-done((bf16[512,128]{1,0:T(8,128)(2,1)S(1)}, bf16[512,128]{1,0:T(8,128)(2,1)S(1)}, u32[]{:S(2)}, u32[]{:S(2)}) %collective-permute-start.16) | collective-permute-done | bytes 131104 | tf_op jit(solution)/shard_map/ppermute | solution.py:22
  91.8 2.6 %collective-permute-done.17.refs_3_ = bf16[512,128]{1,0:T(8,128)(2,1)S(1)} collective-permute-done((bf16[512,128]{1,0:T(8,128)(2,1)S(1)}, bf16[512,128]{1,0:T(8,128)(2,1)S(1)}, u32[]{:S(2)}, u32[]{:S(2)}) %collective-permute-start.17) | collective-permute-done | bytes 131104 | tf_op jit(solution)/shard_map/ppermute | solution.py:22
  94.4 1.5 %unpack.1 = bf16[128,2048]{1,0:T(8,128)(2,1)} custom-call(s32[3]{0:T(128)S(1)} %pad_add_fusion.me_ref, bf16[512,128]{1,0:T(8,128)(2,1)S(1)} %get-tuple-element.89.refs_0_, bf16[512,128]{1,0:T(8,128)(2,1)S(1)} %collective-permute-done.15.refs_1_, bf16[512,128]{1,0:T(8,128)(2,1)S(1)} %collective-permute-done.16.refs_2_, ...), custom_call_target="tpu_custom_call" | custom-call | bytes 1048576 | tf_op jit(solution)/shard_map/unpack/pallas_call | solution.py:35
  95.9 6.7 %all-to-all-done.1 = bf16[16,256,128]{2,1,0:T(8,128)(2,1)S(1)} async-done(((bf16[16,256,128]{2,1,0:T(8,128)(2,1)}), bf16[16,256,128]{2,1,0:T(8,128)(2,1)S(1)}, u32[]{:S(2)}, u32[]{:S(2)}) %all-to-all-start.1) | async-done | bytes 1048608 | tf_op jit(solution)/shard_map/all_to_all | solution.py:315
  102.6 1.3 %unpack_natural.1 = (bf16[128,2048]{1,0:T(8,128)(2,1)}, bf16[128,2048]{1,0:T(8,128)(2,1)}) custom-call(bf16[4096,128]{1,0:T(8,128)(2,1)S(1)} %bitcast.9), custom_call_target="tpu_custom_call" | custom-call | bytes 2097152 | tf_op jit(solution)/shard_map/unpack_natural/pallas_call | solution.py:35
  (15 shorter events, 0.1 us)
Async XLA Ops:
  0.6 1.0 %copy-start.2 = (bf16[128,2048]{1,0:T(8,128)(2,1)S(1)}, bf16[128,2048]{1,0:T(8,128)(2,1)}, u32[]{:S(2)}) copy-start(bf16[128,2048]{1,0:T(8,128)(2,1)} %refs_0_.1) | copy-start | bytes 1572868
  1.7 1.0 %copy-start.3 = (bf16[128,2048]{1,0:T(8,128)(2,1)S(1)}, bf16[128,2048]{1,0:T(8,128)(2,1)}, u32[]{:S(2)}) copy-start(bf16[128,2048]{1,0:T(8,128)(2,1)} %refs_1_.1) | copy-start | bytes 1572868
  3.9 34.3 %all-to-all-start = ((bf16[16,256,128]{2,1,0:T(8,128)(2,1)}), bf16[16,256,128]{2,1,0:T(8,128)(2,1)S(1)}, u32[]{:S(2)}, u32[]{:S(2)}) async-start(bf16[16,256,128]{2,1,0:T(8,128)(2,1)} %bitcast.3), calls=%async_computation | async-start | bytes 2097152 | tf_op jit(solution)/shard_map/all_to_all | solution.py:262
  11.3 1.0 %copy-start = (bf16[128,2048]{1,0:T(8,128)(2,1)S(1)}, bf16[128,2048]{1,0:T(8,128)(2,1)}, u32[]{:S(2)}) copy-start(bf16[128,2048]{1,0:T(8,128)(2,1)} %refs_0_.3) | copy-start | bytes 1572868
  13.1 8.7 %collective-permute-start.3 = (bf16[512,128]{1,0:T(8,128)(2,1)S(1)}, bf16[512,128]{1,0:T(8,128)(2,1)S(1)}, u32[]{:S(2)}, u32[]{:S(2)}) collective-permute-start(bf16[512,128]{1,0:T(8,128)(2,1)S(1)} %get-tuple-element.65), channel_id=1, source_target_pairs={{0,4},{4,0},{8,12},{12,8},{16,20},{20,16},{24,28},{28,24},{1,5},{5... | collective-permute-start | bytes 393224 | tf_op jit(solution)/shard_map/ppermute | solution.py:22
  13.5 14.0 %collective-permute-start.4 = (bf16[512,128]{1,0:T(8,128)(2,1)S(1)}, bf16[512,128]{1,0:T(8,128)(2,1)S(1)}, u32[]{:S(2)}, u32[]{:S(2)}) collective-permute-start(bf16[512,128]{1,0:T(8,128)(2,1)S(1)} %get-tuple-element.66), channel_id=1, source_target_pairs={{0,8},{4,12},{8,0},{12,4},{16,24},{20,28},{24,16},{28,20},{1,9},{5... | collective-permute-start | bytes 393224 | tf_op jit(solution)/shard_map/ppermute | solution.py:22
  15.2 14.8 %collective-permute-start.5 = (bf16[512,128]{1,0:T(8,128)(2,1)S(1)}, bf16[512,128]{1,0:T(8,128)(2,1)S(1)}, u32[]{:S(2)}, u32[]{:S(2)}) collective-permute-start(bf16[512,128]{1,0:T(8,128)(2,1)S(1)} %get-tuple-element.67), channel_id=1, source_target_pairs={{0,12},{4,8},{8,4},{12,0},{16,28},{20,24},{24,20},{28,16},{1,13},{... | collective-permute-start | bytes 393224 | tf_op jit(solution)/shard_map/ppermute | solution.py:22
  17.5 1.0 %copy-start.1 = (bf16[128,2048]{1,0:T(8,128)(2,1)S(1)}, bf16[128,2048]{1,0:T(8,128)(2,1)}, u32[]{:S(2)}) copy-start(bf16[128,2048]{1,0:T(8,128)(2,1)} %refs_0_.2) | copy-start | bytes 1572868
  19.5 15.2 %collective-permute-start = (bf16[528,128]{1,0:T(8,128)(2,1)S(1)}, bf16[528,128]{1,0:T(8,128)(2,1)S(1)}, u32[]{:S(2)}, u32[]{:S(2)}) collective-permute-start(bf16[528,128]{1,0:T(8,128)(2,1)S(1)} %get-tuple-element.53), channel_id=1, source_target_pairs={{0,4},{4,0},{8,12},{12,8},{16,20},{20,16},{24,28},{28,24},{1,5},{5... | collective-permute-start | bytes 405512 | tf_op jit(solution)/shard_map/ppermute | solution.py:22
  20.0 14.7 %collective-permute-start.1 = (bf16[528,128]{1,0:T(8,128)(2,1)S(1)}, bf16[528,128]{1,0:T(8,128)(2,1)S(1)}, u32[]{:S(2)}, u32[]{:S(2)}) collective-permute-start(bf16[528,128]{1,0:T(8,128)(2,1)S(1)} %get-tuple-element.54), channel_id=1, source_target_pairs={{0,8},{4,12},{8,0},{12,4},{16,24},{20,28},{24,16},{28,20},{1,9},{5... | collective-permute-start | bytes 405512 | tf_op jit(solution)/shard_map/ppermute | solution.py:22
  21.7 14.1 %collective-permute-start.2 = (bf16[528,128]{1,0:T(8,128)(2,1)S(1)}, bf16[528,128]{1,0:T(8,128)(2,1)S(1)}, u32[]{:S(2)}, u32[]{:S(2)}) collective-permute-start(bf16[528,128]{1,0:T(8,128)(2,1)S(1)} %get-tuple-element.55), channel_id=1, source_target_pairs={{0,12},{4,8},{8,4},{12,0},{16,28},{20,24},{24,20},{28,16},{1,13},{... | collective-permute-start | bytes 405512 | tf_op jit(solution)/shard_map/ppermute | solution.py:22
  30.1 10.4 %collective-permute-start.6 = (bf16[512,128]{1,0:T(8,128)(2,1)S(1)}, bf16[512,128]{1,0:T(8,128)(2,1)S(1)}, u32[]{:S(2)}, u32[]{:S(2)}) collective-permute-start(bf16[512,128]{1,0:T(8,128)(2,1)S(1)} %get-tuple-element.69), channel_id=1, source_target_pairs={{0,1},{1,0},{2,3},{3,2},{4,5},{5,4},{6,7},{7,6},{8,9},{9,8},{10,11... | collective-permute-start | bytes 393224 | tf_op jit(solution)/shard_map/ppermute | solution.py:22
  30.2 22.1 %collective-permute-start.7 = (bf16[512,128]{1,0:T(8,128)(2,1)S(1)}, bf16[512,128]{1,0:T(8,128)(2,1)S(1)}, u32[]{:S(2)}, u32[]{:S(2)}) collective-permute-start(bf16[512,128]{1,0:T(8,128)(2,1)S(1)} %get-tuple-element.70), channel_id=1, source_target_pairs={{0,2},{1,3},{2,0},{3,1},{4,6},{5,7},{6,4},{7,5},{8,10},{9,11},{10,... | collective-permute-start | bytes 393224 | tf_op jit(solution)/shard_map/ppermute | solution.py:22
  34.8 17.6 %collective-permute-start.8 = (bf16[512,128]{1,0:T(8,128)(2,1)S(1)}, bf16[512,128]{1,0:T(8,128)(2,1)S(1)}, u32[]{:S(2)}, u32[]{:S(2)}) collective-permute-start(bf16[512,128]{1,0:T(8,128)(2,1)S(1)} %get-tuple-element.71), channel_id=1, source_target_pairs={{0,3},{1,2},{2,1},{3,0},{4,7},{5,6},{6,5},{7,4},{8,11},{9,10},{10,... | collective-permute-start | bytes 393224 | tf_op jit(solution)/shard_map/ppermute | solution.py:22
  38.2 20.4 %collective-permute-start.10 = (bf16[512,128]{1,0:T(8,128)(2,1)S(1)}, bf16[512,128]{1,0:T(8,128)(2,1)S(1)}, u32[]{:S(2)}, u32[]{:S(2)}) collective-permute-start(bf16[512,128]{1,0:T(8,128)(2,1)S(1)} %get-tuple-element.74), channel_id=1, source_target_pairs={{0,2},{1,3},{2,0},{3,1},{4,6},{5,7},{6,4},{7,5},{8,10},{9,11},{10,... | collective-permute-start | bytes 393224 | tf_op jit(solution)/shard_map/ppermute | solution.py:22
  39.4 21.6 %collective-permute-start.11 = (bf16[512,128]{1,0:T(8,128)(2,1)S(1)}, bf16[512,128]{1,0:T(8,128)(2,1)S(1)}, u32[]{:S(2)}, u32[]{:S(2)}) collective-permute-start(bf16[512,128]{1,0:T(8,128)(2,1)S(1)} %get-tuple-element.75), channel_id=1, source_target_pairs={{0,3},{1,2},{2,1},{3,0},{4,7},{5,6},{6,5},{7,4},{8,11},{9,10},{10,... | collective-permute-start | bytes 393224 | tf_op jit(solution)/shard_map/ppermute | solution.py:22
  40.5 20.6 %collective-permute-start.9 = (bf16[512,128]{1,0:T(8,128)(2,1)S(1)}, bf16[512,128]{1,0:T(8,128)(2,1)S(1)}, u32[]{:S(2)}, u32[]{:S(2)}) collective-permute-start(bf16[512,128]{1,0:T(8,128)(2,1)S(1)} %get-tuple-element.73), channel_id=1, source_target_pairs={{0,1},{1,0},{2,3},{3,2},{4,5},{5,4},{6,7},{7,6},{8,9},{9,8},{10,11... | collective-permute-start | bytes 393224 | tf_op jit(solution)/shard_map/ppermute | solution.py:22
  55.2 15.0 %collective-permute-start.12 = (bf16[512,128]{1,0:T(8,128)(2,1)S(1)}, bf16[512,128]{1,0:T(8,128)(2,1)S(1)}, u32[]{:S(2)}, u32[]{:S(2)}) collective-permute-start(bf16[512,128]{1,0:T(8,128)(2,1)S(1)} %get-tuple-element.79), channel_id=1, source_target_pairs={{0,1},{1,0},{2,3},{3,2},{4,5},{5,4},{6,7},{7,6},{8,9},{9,8},{10,11... | collective-permute-start | bytes 393224 | tf_op jit(solution)/shard_map/ppermute | solution.py:22
  58.6 12.3 %collective-permute-start.13 = (bf16[512,128]{1,0:T(8,128)(2,1)S(1)}, bf16[512,128]{1,0:T(8,128)(2,1)S(1)}, u32[]{:S(2)}, u32[]{:S(2)}) collective-permute-start(bf16[512,128]{1,0:T(8,128)(2,1)S(1)} %get-tuple-element.80), channel_id=1, source_target_pairs={{0,2},{1,3},{2,0},{3,1},{4,6},{5,7},{6,4},{7,5},{8,10},{9,11},{10,... | collective-permute-start | bytes 393224 | tf_op jit(solution)/shard_map/ppermute | solution.py:22
  58.6 12.3 %collective-permute-start.14 = (bf16[512,128]{1,0:T(8,128)(2,1)S(1)}, bf16[512,128]{1,0:T(8,128)(2,1)S(1)}, u32[]{:S(2)}, u32[]{:S(2)}) collective-permute-start(bf16[512,128]{1,0:T(8,128)(2,1)S(1)} %get-tuple-element.81), channel_id=1, source_target_pairs={{0,3},{1,2},{2,1},{3,0},{4,7},{5,6},{6,5},{7,4},{8,11},{9,10},{10,... | collective-permute-start | bytes 393224 | tf_op jit(solution)/shard_map/ppermute | solution.py:22
  70.9 31.7 %all-to-all-start.1 = ((bf16[16,256,128]{2,1,0:T(8,128)(2,1)}), bf16[16,256,128]{2,1,0:T(8,128)(2,1)S(1)}, u32[]{:S(2)}, u32[]{:S(2)}) async-start(bf16[16,256,128]{2,1,0:T(8,128)(2,1)} %bitcast.5), calls=%async_computation.1 | async-start | bytes 2097152 | tf_op jit(solution)/shard_map/all_to_all | solution.py:315
  75.6 2.2 %collective-permute-start.15 = (bf16[512,128]{1,0:T(8,128)(2,1)S(1)}, bf16[512,128]{1,0:T(8,128)(2,1)S(1)}, u32[]{:S(2)}, u32[]{:S(2)}) collective-permute-start(bf16[512,128]{1,0:T(8,128)(2,1)S(1)} %get-tuple-element.90), channel_id=1, source_target_pairs={{0,4},{4,0},{8,12},{12,8},{16,20},{20,16},{24,28},{28,24},{1,5},{5... | collective-permute-start | bytes 393224 | tf_op jit(solution)/shard_map/ppermute | solution.py:22
  76.1 15.7 %collective-permute-start.16 = (bf16[512,128]{1,0:T(8,128)(2,1)S(1)}, bf16[512,128]{1,0:T(8,128)(2,1)S(1)}, u32[]{:S(2)}, u32[]{:S(2)}) collective-permute-start(bf16[512,128]{1,0:T(8,128)(2,1)S(1)} %get-tuple-element.91), channel_id=1, source_target_pairs={{0,8},{4,12},{8,0},{12,4},{16,24},{20,28},{24,16},{28,20},{1,9},{5... | collective-permute-start | bytes 393224 | tf_op jit(solution)/shard_map/ppermute | solution.py:22
  77.8 16.6 %collective-permute-start.17 = (bf16[512,128]{1,0:T(8,128)(2,1)S(1)}, bf16[512,128]{1,0:T(8,128)(2,1)S(1)}, u32[]{:S(2)}, u32[]{:S(2)}) collective-permute-start(bf16[512,128]{1,0:T(8,128)(2,1)S(1)} %get-tuple-element.92), channel_id=1, source_target_pairs={{0,12},{4,8},{8,4},{12,0},{16,28},{20,24},{24,20},{28,16},{1,13},{... | collective-permute-start | bytes 393224 | tf_op jit(solution)/shard_map/ppermute | solution.py:22

commit v3 on v2

--- a/solution.py
+++ b/solution.py
@@ -12,6 +12,7 @@
 SCALE = DH**-0.5
 LOG2_E = 1.4426950408889634
 NT = (((1,), (1,)), ((), ()))
+TN = (((0,), (0,)), ((), ()))
 VMEM_BYTES = 16 << 20
 IN_VMEM = pl.BlockSpec(memory_space=pltpu.VMEM)
 IN_SMEM = pl.BlockSpec(memory_space=pltpu.SMEM)
@@ -48,43 +49,43 @@
     return [jax.ShapeDtypeStruct((blocks * BLK + extra, DH), jnp.bfloat16)] * count
 
 
-def natural(me_ref, i, n, by, parts):
+def natural(me_ref, i, n, by, near):
     k, j = (i, n) if by == "ctx" else (n, i)
-    return jnp.bitwise_xor(me_ref[0], k) * parts + jnp.bitwise_xor(me_ref[1], j)
-
-
-def pack(me_ref, *refs, arrays, others, by, parts):
+    return jnp.bitwise_xor(me_ref[1], j) * near + jnp.bitwise_xor(me_ref[0], k)
+
+
+def pack(me_ref, *refs, arrays, others, by, near):
     ins, outs = refs[:arrays], refs[arrays:]
     for i, out in enumerate(outs):
         for n in range(others):
-            lanes = head_lanes(natural(me_ref, i, n, by, parts))
+            lanes = head_lanes(natural(me_ref, i, n, by, near))
             for place, ref in enumerate(ins):
                 out[rows(place * others + n), :] = ref[:, lanes]
 
 
-def pack_with_index(me_ref, offsets_ref, pool_ref, picks_ref, *refs, parts, **kwargs):
-    pack(me_ref, *refs, by="ctx", parts=parts, **kwargs)
+def pack_with_index(me_ref, offsets_ref, pool_ref, picks_ref, *refs, parts, near, **kwargs):
+    pack(me_ref, *refs, by="ctx", near=near, **kwargs)
     row = lax.broadcasted_iota(jnp.int32, (INDEX_ROWS, DH), 0)
     lane = lax.broadcasted_iota(jnp.int32, (INDEX_ROWS, DH), 1)
     tile = jnp.zeros((INDEX_ROWS, DH), jnp.int32)
     for block in range(parts):
         local = [offsets_ref[block, n] for n in range(offsets_ref.shape[1])]
-        chosen = [me_ref[0] * parts + jnp.bitwise_and(block + offset, parts - 1) for offset in local]
+        chosen = [jnp.bitwise_and(block + offset, parts - 1) * near + me_ref[0] for offset in local]
         for bit in range(picks_ref.shape[1]):
-            far = jnp.bitwise_xor(me_ref[0], 1 << bit) * parts
+            far = jnp.bitwise_xor(me_ref[0], 1 << bit)
             for n in range(picks_ref.shape[2]):
-                chosen.append(far + pool_ref[me_ref[2], bit, picks_ref[block, bit, n]])
+                chosen.append(pool_ref[me_ref[2], bit, picks_ref[block, bit, n]] * near + far)
         for n, value in enumerate(chosen):
             tile = jnp.where((row == block) & (lane == n), value, tile)
     for out in refs[kwargs["arrays"] :]:
         out[out.shape[0] - INDEX_ROWS :, :] = tile.astype(jnp.float32).astype(out.dtype)
 
 
-def unpack(me_ref, *refs, by, parts):
+def unpack(me_ref, *refs, by, near):
     *ins, out = refs
     for i, ref in enumerate(ins):
         for n in range(ref.shape[0] // BLK):
-            out[:, head_lanes(natural(me_ref, i, n, by, parts))] = ref[rows(n), :]
+            out[:, head_lanes(natural(me_ref, i, n, by, near))] = ref[rows(n), :]
 
 
 def pack_natural(*refs):
@@ -116,23 +117,23 @@
         index_ref[k * INDEX_ROWS : (k + 1) * INDEX_ROWS, :] = tile.astype(jnp.float32).astype(jnp.int32)
 
 
-def gather(me_ref, table, refs, by, parts, place=0):
+def gather(me_ref, table, refs, by, near, place=0):
     others = table.shape[0] // len(refs)
     for i, ref in enumerate(refs):
         for n in range(others):
-            table[natural(me_ref, i, n, by, parts)] = ref[rows(place * others + n), :]
-
-
-def spread(me_ref, table, refs, by, parts):
+            table[natural(me_ref, i, n, by, near)] = ref[rows(place * others + n), :]
+
+
+def spread(me_ref, table, refs, by, near):
     others = table.shape[0] // len(refs)
     for i, ref in enumerate(refs):
         for n in range(others):
-            ref[rows(n), :] = table[natural(me_ref, i, n, by, parts)].astype(ref.dtype)
-
-
-def chosen_blocks(me_ref, index_ref, block, parts, key_count):
-    group = jnp.bitwise_xor(lax.div(block, parts), me_ref[0])
-    row = group * INDEX_ROWS + lax.rem(block, parts)
+            ref[rows(n), :] = table[natural(me_ref, i, n, by, near)].astype(ref.dtype)
+
+
+def chosen_blocks(me_ref, index_ref, block, near, key_count):
+    group = jnp.bitwise_xor(lax.rem(block, near), me_ref[0])
+    row = group * INDEX_ROWS + lax.div(block, near)
     return [index_ref[row, j] for j in range(key_count)]
 
 
@@ -153,12 +154,12 @@
             acc[block] += values[j * BLK : (j + 1) * BLK, half * DH : (half + 1) * DH]
 
 
-def for_pairs(me_ref, index_ref, count, parts, key_count, unroll, one):
+def for_pairs(me_ref, index_ref, count, near, key_count, unroll, one):
     def step(i, _):
         for slot in range(unroll):
             pair = i * unroll + slot
             blocks = (2 * pair, 2 * pair + 1)
-            one(pair, slot, blocks, [chosen_blocks(me_ref, index_ref, b, parts, key_count) for b in blocks])
+            one(pair, slot, blocks, [chosen_blocks(me_ref, index_ref, b, near, key_count) for b in blocks])
         return 0
 
     lax.fori_loop(0, count // unroll, step, 0)
@@ -180,15 +181,15 @@
         row_max = jnp.max(scores, axis=0, keepdims=True)
         exp_scores = jnp.exp2((scores - row_max) * (SCALE * LOG2_E))
         weights = exp_scores * (1.0 / jnp.sum(exp_scores, axis=0, keepdims=True))
-        w_ref[pair] = weights
+        w_ref[pair] = weights * SCALE
         half_ref[pair] = weights.astype(half_ref.dtype)
 
-    for_pairs(me_ref, index_ref, w_ref.shape[0], parts, key_count, unroll, one)
+    for_pairs(me_ref, index_ref, w_ref.shape[0], near, key_count, unroll, one)
 
 
 def dv_parts(me_ref, index_ref, half_ref, *refs, parts, near, key_count, unroll):
     g_refs, dv_refs, (acc, g_table, g_diag) = refs[:parts], refs[parts : 2 * parts], refs[2 * parts :]
-    gather(me_ref, g_table, g_refs, "head", parts)
+    gather(me_ref, g_table, g_refs, "head", near)
     for ref in (acc, g_diag):
         ref[...] = jnp.zeros_like(ref)
 
@@ -196,37 +197,35 @@
         set_diagonal(g_diag.at[slot], *(g_table[b] for b in blocks))
         add_pair(acc, chosen, jnp.dot(half_ref[pair], g_diag[slot], preferred_element_type=jnp.float32))
 
-    for_pairs(me_ref, index_ref, half_ref.shape[0], parts, key_count, unroll, one)
-    spread(me_ref, acc, dv_refs, "head", parts)
+    for_pairs(me_ref, index_ref, half_ref.shape[0], near, key_count, unroll, one)
+    spread(me_ref, acc, dv_refs, "head", near)
 
 
 def dq_and_dk(me_ref, index_ref, joined_ref, *refs, parts, near, key_count, unroll):
     g_refs, v_refs, refs = refs[:parts], refs[parts : 2 * parts], refs[2 * parts :]
-    w_ref, out_ref, acc, k_table, g_table, v_table, q_diag, g_diag = refs
-    gather(me_ref, g_table, g_refs, "head", parts)
-    gather(me_ref, v_table, v_refs, "head", parts)
+    w_ref, out_ref, acc, g_table, v_table, q_diag, g_diag = refs
+    gather(me_ref, g_table, g_refs, "head", near)
+    gather(me_ref, v_table, v_refs, "head", near)
     for ref in (acc, q_diag, g_diag):
         ref[...] = jnp.zeros_like(ref)
     query, key = (joined_block(joined_ref, near * parts, place) for place in range(2))
-    for block in range(k_table.shape[0]):
-        k_table[block] = key(block).T
 
     def one(pair, slot, blocks, chosen):
         set_diagonal(q_diag.at[slot], *map(query, blocks))
         set_diagonal(g_diag.at[slot], *(g_table[b] for b in blocks))
         values = pair_of(lambda b: v_table[b], *chosen)
         prob_grad = lax.dot_general(values, g_diag[slot], NT, preferred_element_type=jnp.float32)
-        weights = w_ref[pair]
-        row_delta = jnp.sum(weights * prob_grad, axis=0, keepdims=True)
-        score_grad = (SCALE * (weights * (prob_grad - row_delta))).astype(jnp.bfloat16)
+        scaled = w_ref[pair]
+        row_delta = jnp.sum(scaled * prob_grad, axis=0, keepdims=True) * (1 / SCALE)
+        score_grad = (scaled * (prob_grad - row_delta)).astype(jnp.bfloat16)
         add_pair(acc, chosen, jnp.dot(score_grad, q_diag[slot], preferred_element_type=jnp.float32))
+        keys = pair_of(key, *chosen)
+        grads = lax.dot_general(score_grad, keys, TN, preferred_element_type=jnp.float32)
         for half, block in enumerate(blocks):
-            turned = jnp.concatenate([k_table[b] for b in chosen[half]], axis=1)
-            own = score_grad[:, half * BLK : (half + 1) * BLK]
-            grad = jnp.dot(turned, own, preferred_element_type=jnp.float32).T
-            out_ref[rows(2 * block), :] = grad.astype(out_ref.dtype)
-
-    for_pairs(me_ref, index_ref, w_ref.shape[0], parts, key_count, unroll, one)
+            own = slice(half * BLK, (half + 1) * BLK)
+            out_ref[rows(2 * block), :] = grads[own, own].astype(out_ref.dtype)
+
+    for_pairs(me_ref, index_ref, w_ref.shape[0], near, key_count, unroll, one)
     for block in range(acc.shape[0]):
         out_ref[rows(2 * block + 1), :] = acc[block].astype(out_ref.dtype)
 
@@ -249,7 +248,7 @@
         return [x if j == 0 else swapped(x, "head", j) for j, x in enumerate(by_part)]
 
     members = [
-        [member * parts + part for member in range(first, first + near) for part in range(parts)]
+        [member * parts + part for part in range(parts) for member in range(first, first + near)]
         for first in range(0, lax.axis_size("ctx"), near)
     ]
     exchange = functools.partial(
@@ -261,12 +260,12 @@
     out_grads, value_vecs, local_offsets, partner_pool, partner_picks = later
     joined = exchange(joined)
     grad = local_call(
-        functools.partial(pack, arrays=1, others=parts, by="ctx", parts=parts), parts_of(parts, near), (me,), (out_grads,)
+        functools.partial(pack, arrays=1, others=parts, by="ctx", near=near), parts_of(parts, near), (me,), (out_grads,)
     )
     grad = local_call(functools.partial(regroup, count=near, places=[0]), parts_of(near, parts), (), over_ctx(grad))
     grad = over_head(grad)
     value = local_call(
-        functools.partial(pack_with_index, arrays=1, others=parts, parts=parts),
+        functools.partial(pack_with_index, arrays=1, others=parts, parts=parts, near=near),
         parts_of(parts, near, INDEX_ROWS),
         (me, local_offsets, partner_pool, partner_picks),
         (value_vecs,),
@@ -281,7 +280,7 @@
     value = over_head(value)
 
     pairs, keys = cluster // 2, key_count * BLK
-    unroll = 4 if pairs % 4 == 0 else 1
+    unroll = next(n for n in (8, 4, 2, 1) if pairs % n == 0)
     kwargs = dict(parts=parts, near=near, key_count=key_count, unroll=unroll)
     flops = 4 * cluster * keys * BLK * DH
     acc, table = (pltpu.VMEM((cluster, BLK, DH), dtype) for dtype in (jnp.float32, jnp.bfloat16))
@@ -308,7 +307,7 @@
         parts_of(2 * cluster, 1)[0],
         (me, index),
         (joined, *grad, *value, weights),
-        [acc] + [table] * 3 + [diagonal] * 2,
+        [acc] + [table] * 2 + [diagonal] * 2,
         flops * 3 // 2,
     )
     joined, dv = lax.optimization_barrier((joined, dv))
@@ -316,7 +315,7 @@
     dv = local_call(functools.partial(regroup, count=parts, places=[0]), parts_of(parts, near), (), dv)
     dv = over_ctx(dv)
     out = jax.ShapeDtypeStruct(queries.shape, queries.dtype)
-    value_grads = local_call(functools.partial(unpack, by="ctx", parts=parts), out, (me,), dv)
+    value_grads = local_call(functools.partial(unpack, by="ctx", near=near), out, (me,), dv)
     query_grads, key_grads = local_call(unpack_natural, [out] * 2, (), (joined,))
     return query_grads, key_grads, value_grads
 

time: 104 us -> 101 us (0.971); the launches traced: 104 us -> 99.1 us
  waiting for transfers between devices: 42.2 us -> 31.8 us
  starting transfers between devices: 32.6 us -> 39.8 us
  Pallas kernels: 21.7 us -> 20.3 us
    ppermute x18, starting transfers between devices: 20.6 us -> 27.4 us  [swapped(): lax.ppermute(value, axis, [(i, i ^ distance) for i in range(lax.axis_size...]
    ppermute x18, waiting for transfers between devices: 33.2 us -> 27 us  [swapped(): lax.ppermute(value, axis, [(i, i ^ distance) for i in range(lax.axis_size...]
    all_to_all x2, waiting for transfers between devices: 9.03 us -> 4.78 us  [whole_cluster(): joined = exchange(joined)]
    pallas_call x11, Pallas kernels: 21.7 us -> 20.3 us  [local_call(): pl.pallas_call(kernel, out_shape=out_shape, in_specs=[IN_SMEM] * len(scal...]
  transfers between devices with their start and end apart: 20 -> 20, of which waited for: 9 -> 8; matrix products, arithmetic and copies ran while one was open for 2% -> 2% of each run, Pallas kernels for 19% -> 18%
where the time goes in v3:
time: 101 us; the launch traced here: 99.1 us
  starting transfers between devices  39.8 us (39%)
  waiting for transfers between devices  31.8 us (31%)
  Pallas kernels  20.3 us (20%)
  local copies, waits for them, and re-layouts  6.47 us (6%)
    ppermute x18, starting transfers between devices, swapped(): lax.ppermute(value, axis, [(i, i ^ distance) for i in range(lax.axis_size...  27.4 us
    ppermute x18, waiting for transfers between devices, swapped(): lax.ppermute(value, axis, [(i, i ^ distance) for i in range(lax.axis_size...  27 us
    pallas_call x11, Pallas kernels, local_call(): pl.pallas_call(kernel, out_shape=out_shape, in_specs=[IN_SMEM] * len(scal...  20.3 us
    all_to_all x2, starting transfers between devices, whole_cluster(): joined = exchange(joined)  12.4 us
    all_to_all x2, waiting for transfers between devices, whole_cluster(): joined = exchange(joined)  4.78 us
    unnamed x8, local copies, waits for them, and re-layouts  4.16 us
    optimization_barrier x3, local copies, waits for them, and re-layouts, whole_cluster(): joined, later = lax.optimization_barrier((joined, later))  2.31 us
  transfers between devices with their start and end apart: 20, of which 8 were waited for; matrix products, arithmetic and copies ran while one was open for 2% of the time, Pallas kernels for 18%

profile of v3, /device:TPU:0, one launch (start us, length us, event | category | flops | bytes accessed | tf_op | source)
XLA Modules:
  0.0 99.1 jit_solution(17611631617113928874)
XLA Ops:
  0.6 1.0 %copy-done.2 = bf16[128,2048]{1,0:T(8,128)(2,1)S(1)} copy-done((bf16[128,2048]{1,0:T(8,128)(2,1)S(1)}, bf16[128,2048]{1,0:T(8,128)(2,1)}, u32[]{:S(2)}) %copy-start.2) | copy-done | bytes 524312
  1.7 1.0 %copy-done.3 = bf16[128,2048]{1,0:T(8,128)(2,1)S(1)} copy-done((bf16[128,2048]{1,0:T(8,128)(2,1)S(1)}, bf16[128,2048]{1,0:T(8,128)(2,1)}, u32[]{:S(2)}) %copy-start.3) | copy-done | bytes 524312
  2.7 1.2 %pack_natural.1 = bf16[4096,128]{1,0:T(8,128)(2,1)} custom-call(bf16[128,2048]{1,0:T(8,128)(2,1)S(1)} %copy-done.2, bf16[128,2048]{1,0:T(8,128)(2,1)S(1)} %copy-done.3), custom_call_target="tpu_custom_call" | custom-call | bytes 2097152 | tf_op jit(solution)/shard_map/pack_natural/pallas_call | solution.py:36
  3.9 7.4 %all-to-all-start = ((bf16[16,256,128]{2,1,0:T(8,128)(2,1)}), bf16[16,256,128]{2,1,0:T(8,128)(2,1)S(1)}, u32[]{:S(2)}, u32[]{:S(2)}) async-start(bf16[16,256,128]{2,1,0:T(8,128)(2,1)} %bitcast.3), calls=%async_computation | async-start | bytes 2097152 | tf_op jit(solution)/shard_map/all_to_all | solution.py:261
  11.2 0.1 pad_add_fusion.me_ref
  11.3 1.0 %copy-done = bf16[128,2048]{1,0:T(8,128)(2,1)S(1)} copy-done((bf16[128,2048]{1,0:T(8,128)(2,1)S(1)}, bf16[128,2048]{1,0:T(8,128)(2,1)}, u32[]{:S(2)}) %copy-start) | copy-done | bytes 524312
  12.4 0.7 pack.1
  13.1 0.5 collective-permute-start.3
  13.5 1.7 %collective-permute-start.4 = (bf16[512,128]{1,0:T(8,128)(2,1)S(1)}, bf16[512,128]{1,0:T(8,128)(2,1)S(1)}, u32[]{:S(2)}, u32[]{:S(2)}) collective-permute-start(bf16[512,128]{1,0:T(8,128)(2,1)S(1)} %get-tuple-element.66), channel_id=1, source_target_pairs={{0,8},{4,12},{8,0},{12,4},{16,24},{20,28},{24,16},{28,20},{1,9},{5... | collective-permute-start | bytes 393224 | tf_op jit(solution)/shard_map/ppermute | solution.py:23
  15.2 0.8 copy.11.pool_ref
  16.0 0.8 copy.12.picks_ref
  16.8 0.8 copy.10.offsets_ref
  17.5 1.0 %copy-done.1 = bf16[128,2048]{1,0:T(8,128)(2,1)S(1)} copy-done((bf16[128,2048]{1,0:T(8,128)(2,1)S(1)}, bf16[128,2048]{1,0:T(8,128)(2,1)}, u32[]{:S(2)}) %copy-start.1) | copy-done | bytes 524312
  18.6 1.0 pack_with_index.1
  19.5 0.5 collective-permute-start
  20.0 1.7 %collective-permute-start.1 = (bf16[528,128]{1,0:T(8,128)(2,1)S(1)}, bf16[528,128]{1,0:T(8,128)(2,1)S(1)}, u32[]{:S(2)}, u32[]{:S(2)}) collective-permute-start(bf16[528,128]{1,0:T(8,128)(2,1)S(1)} %get-tuple-element.54), channel_id=1, source_target_pairs={{0,8},{4,12},{8,0},{12,4},{16,24},{20,28},{24,16},{28,20},{1,9},{5... | collective-permute-start | bytes 405512 | tf_op jit(solution)/shard_map/ppermute | solution.py:23
  21.7 0.0 collective-permute-done.3.refs_1_
  21.7 0.0 collective-permute-start.2
  21.7 4.2 %collective-permute-done.4.refs_2_ = bf16[512,128]{1,0:T(8,128)(2,1)S(1)} collective-permute-done((bf16[512,128]{1,0:T(8,128)(2,1)S(1)}, bf16[512,128]{1,0:T(8,128)(2,1)S(1)}, u32[]{:S(2)}, u32[]{:S(2)}) %collective-permute-start.4) | collective-permute-done | bytes 131104 | tf_op jit(solution)/shard_map/ppermute | solution.py:23
  25.9 2.9 %collective-permute-done.5.refs_3_ = bf16[512,128]{1,0:T(8,128)(2,1)S(1)} collective-permute-done((bf16[512,128]{1,0:T(8,128)(2,1)S(1)}, bf16[512,128]{1,0:T(8,128)(2,1)S(1)}, u32[]{:S(2)}, u32[]{:S(2)}) %collective-permute-start.5) | collective-permute-done | bytes 131104 | tf_op jit(solution)/shard_map/ppermute | solution.py:23
  28.8 0.1 collective-permute-start.6
  28.9 4.4 %collective-permute-start.7 = (bf16[512,128]{1,0:T(8,128)(2,1)S(1)}, bf16[512,128]{1,0:T(8,128)(2,1)S(1)}, u32[]{:S(2)}, u32[]{:S(2)}) collective-permute-start(bf16[512,128]{1,0:T(8,128)(2,1)S(1)} %get-tuple-element.70), channel_id=1, source_target_pairs={{0,2},{1,3},{2,0},{3,1},{4,6},{5,7},{6,4},{7,5},{8,10},{9,11},{10,... | collective-permute-start | bytes 393224 | tf_op jit(solution)/shard_map/ppermute | solution.py:23
  33.3 0.0 collective-permute-done.refs_1_
  33.3 0.0 collective-permute-start.8
  33.3 3.2 %collective-permute-done.2.refs_3_ = bf16[528,128]{1,0:T(8,128)(2,1)S(1)} collective-permute-done((bf16[528,128]{1,0:T(8,128)(2,1)S(1)}, bf16[528,128]{1,0:T(8,128)(2,1)S(1)}, u32[]{:S(2)}, u32[]{:S(2)}) %collective-permute-start.2) | collective-permute-done | bytes 135200 | tf_op jit(solution)/shard_map/ppermute | solution.py:23
  36.6 0.0 all-to-all-done
  36.6 8.8 %collective-permute-start.10 = (bf16[512,128]{1,0:T(8,128)(2,1)S(1)}, bf16[512,128]{1,0:T(8,128)(2,1)S(1)}, u32[]{:S(2)}, u32[]{:S(2)}) collective-permute-start(bf16[512,128]{1,0:T(8,128)(2,1)S(1)} %get-tuple-element.74), channel_id=1, source_target_pairs={{0,2},{1,3},{2,0},{3,1},{4,6},{5,7},{6,4},{7,5},{8,10},{9,11},{10,... | collective-permute-start | bytes 393224 | tf_op jit(solution)/shard_map/ppermute | solution.py:23
  45.4 0.0 collective-permute-start.11
  45.4 0.0 collective-permute-done.6.refs_1_
  45.4 0.6 collective-permute-start.9
  46.0 4.2 %softmax_weights.1 = (f32[8,768,256]{2,1,0:T(8,128)S(1)}, bf16[8,768,256]{2,1,0:T(8,128)(2,1)S(1)}) custom-call(s32[3]{0:T(128)S(1)} %pad_add_fusion.me_ref, s32[64,128]{1,0:T(8,128)S(1)} %get-tuple-element.56.index_ref, bf16[4096,128]{1,0:T(8,128)(2,1)S(1)} %bitcast.7), custom_call_target="tpu_custom_call" | custom-call | flops 402653184 | bytes 10485760 | tf_op jit(solution)/shard_map/softmax_weights/pallas_call | solution.py:36
  50.2 1.0 %collective-permute-done.7.refs_2_ = bf16[512,128]{1,0:T(8,128)(2,1)S(1)} collective-permute-done((bf16[512,128]{1,0:T(8,128)(2,1)S(1)}, bf16[512,128]{1,0:T(8,128)(2,1)S(1)}, u32[]{:S(2)}, u32[]{:S(2)}) %collective-permute-start.7) | collective-permute-done | bytes 131104 | tf_op jit(solution)/shard_map/ppermute | solution.py:23
  51.2 0.0 collective-permute-done.8.refs_3_
  51.2 2.6 %dv_parts.1 = (bf16[512,128]{1,0:T(8,128)(2,1)S(1)}, bf16[512,128]{1,0:T(8,128)(2,1)S(1)}, bf16[512,128]{1,0:T(8,128)(2,1)S(1)}, bf16[512,128]{1,0:T(8,128)(2,1)S(1)}) custom-call(s32[3]{0:T(128)S(1)} %pad_add_fusion.me_ref, s32[64,128]{1,0:T(8,128)S(1)} %get-tuple-element.56.index_ref, bf16[8,768,256]{2,1,0:T(8,128)(2,1)S(1)} %get-tuple-element.77.half_ref, ...), custom_call_target="tpu_custom_call" | custom-call | flops 402653184 | bytes 4194304 | tf_op jit(solution)/shard_map/dv_parts/pallas_call | solution.py:36
  53.8 4.6 %collective-permute-start.12 = (bf16[512,128]{1,0:T(8,128)(2,1)S(1)}, bf16[512,128]{1,0:T(8,128)(2,1)S(1)}, u32[]{:S(2)}, u32[]{:S(2)}) collective-permute-start(bf16[512,128]{1,0:T(8,128)(2,1)S(1)} %get-tuple-element.79), channel_id=1, source_target_pairs={{0,1},{1,0},{2,3},{3,2},{4,5},{5,4},{6,7},{7,6},{8,9},{9,8},{10,11... | collective-permute-start | bytes 393224 | tf_op jit(solution)/shard_map/ppermute | solution.py:23
  58.4 0.1 collective-permute-start.13
  58.5 2.4 %collective-permute-start.14 = (bf16[512,128]{1,0:T(8,128)(2,1)S(1)}, bf16[512,128]{1,0:T(8,128)(2,1)S(1)}, u32[]{:S(2)}, u32[]{:S(2)}) collective-permute-start(bf16[512,128]{1,0:T(8,128)(2,1)S(1)} %get-tuple-element.81), channel_id=1, source_target_pairs={{0,3},{1,2},{2,1},{3,0},{4,7},{5,6},{6,5},{7,4},{8,11},{9,10},{10,... | collective-permute-start | bytes 393224 | tf_op jit(solution)/shard_map/ppermute | solution.py:23
  60.9 0.0 collective-permute-done.11.refs_7_
  60.9 7.8 %dq_and_dk.1 = bf16[4096,128]{1,0:T(8,128)(2,1)} custom-call(s32[3]{0:T(128)S(1)} %pad_add_fusion.me_ref, s32[64,128]{1,0:T(8,128)S(1)} %get-tuple-element.56.index_ref, bf16[4096,128]{1,0:T(8,128)(2,1)S(1)} %bitcast.8, bf16[512,128]{1,0:T(8,128)(2,1)S(1)} %get-tuple-element.68.refs_0_, bf16[512,128]{1,0:T(8,128)(2,1)S(1)} %collective-permute-done.6.refs_1_, ...), custom_call_target="tpu_custom_call" | custom-call | flops 1207959552 | bytes 9437184 | tf_op jit(solution)/shard_map/dq_and_dk/pallas_call | solution.py:36
  68.7 1.2 %collective-permute-done.13.refs_2_ = bf16[512,128]{1,0:T(8,128)(2,1)S(1)} collective-permute-done((bf16[512,128]{1,0:T(8,128)(2,1)S(1)}, bf16[512,128]{1,0:T(8,128)(2,1)S(1)}, u32[]{:S(2)}, u32[]{:S(2)}) %collective-permute-start.13) | collective-permute-done | bytes 131104 | tf_op jit(solution)/shard_map/ppermute | solution.py:23
  69.8 5.1 %all-to-all-start.1 = ((bf16[16,256,128]{2,1,0:T(8,128)(2,1)}), bf16[16,256,128]{2,1,0:T(8,128)(2,1)S(1)}, u32[]{:S(2)}, u32[]{:S(2)}) async-start(bf16[16,256,128]{2,1,0:T(8,128)(2,1)} %bitcast.5), calls=%async_computation.1 | async-start | bytes 2097152 | tf_op jit(solution)/shard_map/all_to_all | solution.py:314
  75.0 0.5 collective-permute-start.15
  75.4 1.7 %collective-permute-start.16 = (bf16[512,128]{1,0:T(8,128)(2,1)S(1)}, bf16[512,128]{1,0:T(8,128)(2,1)S(1)}, u32[]{:S(2)}, u32[]{:S(2)}) collective-permute-start(bf16[512,128]{1,0:T(8,128)(2,1)S(1)} %get-tuple-element.91), channel_id=1, source_target_pairs={{0,8},{4,12},{8,0},{12,4},{16,24},{20,28},{24,16},{28,20},{1,9},{5... | collective-permute-start | bytes 393224 | tf_op jit(solution)/shard_map/ppermute | solution.py:23
  77.1 12.5 %collective-permute-done.16.refs_2_ = bf16[512,128]{1,0:T(8,128)(2,1)S(1)} collective-permute-done((bf16[512,128]{1,0:T(8,128)(2,1)S(1)}, bf16[512,128]{1,0:T(8,128)(2,1)S(1)}, u32[]{:S(2)}, u32[]{:S(2)}) %collective-permute-start.16) | collective-permute-done | bytes 131104 | tf_op jit(solution)/shard_map/ppermute | solution.py:23
  89.6 2.0 %collective-permute-done.17.refs_3_ = bf16[512,128]{1,0:T(8,128)(2,1)S(1)} collective-permute-done((bf16[512,128]{1,0:T(8,128)(2,1)S(1)}, bf16[512,128]{1,0:T(8,128)(2,1)S(1)}, u32[]{:S(2)}, u32[]{:S(2)}) %collective-permute-start.17) | collective-permute-done | bytes 131104 | tf_op jit(solution)/shard_map/ppermute | solution.py:23
  91.6 1.5 %unpack.1 = bf16[128,2048]{1,0:T(8,128)(2,1)} custom-call(s32[3]{0:T(128)S(1)} %pad_add_fusion.me_ref, bf16[512,128]{1,0:T(8,128)(2,1)S(1)} %get-tuple-element.89.refs_0_, bf16[512,128]{1,0:T(8,128)(2,1)S(1)} %collective-permute-done.15.refs_1_, bf16[512,128]{1,0:T(8,128)(2,1)S(1)} %collective-permute-done.16.refs_2_, ...), custom_call_target="tpu_custom_call" | custom-call | bytes 1048576 | tf_op jit(solution)/shard_map/unpack/pallas_call | solution.py:36
  93.1 4.8 %all-to-all-done.1 = bf16[16,256,128]{2,1,0:T(8,128)(2,1)S(1)} async-done(((bf16[16,256,128]{2,1,0:T(8,128)(2,1)}), bf16[16,256,128]{2,1,0:T(8,128)(2,1)S(1)}, u32[]{:S(2)}, u32[]{:S(2)}) %all-to-all-start.1) | async-done | bytes 1048608 | tf_op jit(solution)/shard_map/all_to_all | solution.py:314
  97.9 1.3 %unpack_natural.1 = (bf16[128,2048]{1,0:T(8,128)(2,1)}, bf16[128,2048]{1,0:T(8,128)(2,1)}) custom-call(bf16[4096,128]{1,0:T(8,128)(2,1)S(1)} %bitcast.9), custom_call_target="tpu_custom_call" | custom-call | bytes 2097152 | tf_op jit(solution)/shard_map/unpack_natural/pallas_call | solution.py:36
  (15 shorter events, 0.1 us)
Async XLA Ops:
  0.6 1.0 %copy-start.2 = (bf16[128,2048]{1,0:T(8,128)(2,1)S(1)}, bf16[128,2048]{1,0:T(8,128)(2,1)}, u32[]{:S(2)}) copy-start(bf16[128,2048]{1,0:T(8,128)(2,1)} %refs_0_.1) | copy-start | bytes 1572868
  1.7 1.0 %copy-start.3 = (bf16[128,2048]{1,0:T(8,128)(2,1)S(1)}, bf16[128,2048]{1,0:T(8,128)(2,1)}, u32[]{:S(2)}) copy-start(bf16[128,2048]{1,0:T(8,128)(2,1)} %refs_1_.1) | copy-start | bytes 1572868
  3.9 32.7 %all-to-all-start = ((bf16[16,256,128]{2,1,0:T(8,128)(2,1)}), bf16[16,256,128]{2,1,0:T(8,128)(2,1)S(1)}, u32[]{:S(2)}, u32[]{:S(2)}) async-start(bf16[16,256,128]{2,1,0:T(8,128)(2,1)} %bitcast.3), calls=%async_computation | async-start | bytes 2097152 | tf_op jit(solution)/shard_map/all_to_all | solution.py:261
  11.3 1.0 %copy-start = (bf16[128,2048]{1,0:T(8,128)(2,1)S(1)}, bf16[128,2048]{1,0:T(8,128)(2,1)}, u32[]{:S(2)}) copy-start(bf16[128,2048]{1,0:T(8,128)(2,1)} %refs_0_.3) | copy-start | bytes 1572868
  13.1 8.7 %collective-permute-start.3 = (bf16[512,128]{1,0:T(8,128)(2,1)S(1)}, bf16[512,128]{1,0:T(8,128)(2,1)S(1)}, u32[]{:S(2)}, u32[]{:S(2)}) collective-permute-start(bf16[512,128]{1,0:T(8,128)(2,1)S(1)} %get-tuple-element.65), channel_id=1, source_target_pairs={{0,4},{4,0},{8,12},{12,8},{16,20},{20,16},{24,28},{28,24},{1,5},{5... | collective-permute-start | bytes 393224 | tf_op jit(solution)/shard_map/ppermute | solution.py:23
  13.5 12.4 %collective-permute-start.4 = (bf16[512,128]{1,0:T(8,128)(2,1)S(1)}, bf16[512,128]{1,0:T(8,128)(2,1)S(1)}, u32[]{:S(2)}, u32[]{:S(2)}) collective-permute-start(bf16[512,128]{1,0:T(8,128)(2,1)S(1)} %get-tuple-element.66), channel_id=1, source_target_pairs={{0,8},{4,12},{8,0},{12,4},{16,24},{20,28},{24,16},{28,20},{1,9},{5... | collective-permute-start | bytes 393224 | tf_op jit(solution)/shard_map/ppermute | solution.py:23
  15.2 13.6 %collective-permute-start.5 = (bf16[512,128]{1,0:T(8,128)(2,1)S(1)}, bf16[512,128]{1,0:T(8,128)(2,1)S(1)}, u32[]{:S(2)}, u32[]{:S(2)}) collective-permute-start(bf16[512,128]{1,0:T(8,128)(2,1)S(1)} %get-tuple-element.67), channel_id=1, source_target_pairs={{0,12},{4,8},{8,4},{12,0},{16,28},{20,24},{24,20},{28,16},{1,13},{... | collective-permute-start | bytes 393224 | tf_op jit(solution)/shard_map/ppermute | solution.py:23
  17.5 1.0 %copy-start.1 = (bf16[128,2048]{1,0:T(8,128)(2,1)S(1)}, bf16[128,2048]{1,0:T(8,128)(2,1)}, u32[]{:S(2)}) copy-start(bf16[128,2048]{1,0:T(8,128)(2,1)} %refs_0_.2) | copy-start | bytes 1572868
  19.5 13.7 %collective-permute-start = (bf16[528,128]{1,0:T(8,128)(2,1)S(1)}, bf16[528,128]{1,0:T(8,128)(2,1)S(1)}, u32[]{:S(2)}, u32[]{:S(2)}) collective-permute-start(bf16[528,128]{1,0:T(8,128)(2,1)S(1)} %get-tuple-element.53), channel_id=1, source_target_pairs={{0,4},{4,0},{8,12},{12,8},{16,20},{20,16},{24,28},{28,24},{1,5},{5... | collective-permute-start | bytes 405512 | tf_op jit(solution)/shard_map/ppermute | solution.py:23
  20.0 13.3 %collective-permute-start.1 = (bf16[528,128]{1,0:T(8,128)(2,1)S(1)}, bf16[528,128]{1,0:T(8,128)(2,1)S(1)}, u32[]{:S(2)}, u32[]{:S(2)}) collective-permute-start(bf16[528,128]{1,0:T(8,128)(2,1)S(1)} %get-tuple-element.54), channel_id=1, source_target_pairs={{0,8},{4,12},{8,0},{12,4},{16,24},{20,28},{24,16},{28,20},{1,9},{5... | collective-permute-start | bytes 405512 | tf_op jit(solution)/shard_map/ppermute | solution.py:23
  21.7 14.8 %collective-permute-start.2 = (bf16[528,128]{1,0:T(8,128)(2,1)S(1)}, bf16[528,128]{1,0:T(8,128)(2,1)S(1)}, u32[]{:S(2)}, u32[]{:S(2)}) collective-permute-start(bf16[528,128]{1,0:T(8,128)(2,1)S(1)} %get-tuple-element.55), channel_id=1, source_target_pairs={{0,12},{4,8},{8,4},{12,0},{16,28},{20,24},{24,20},{28,16},{1,13},{... | collective-permute-start | bytes 405512 | tf_op jit(solution)/shard_map/ppermute | solution.py:23
  28.8 16.6 %collective-permute-start.6 = (bf16[512,128]{1,0:T(8,128)(2,1)S(1)}, bf16[512,128]{1,0:T(8,128)(2,1)S(1)}, u32[]{:S(2)}, u32[]{:S(2)}) collective-permute-start(bf16[512,128]{1,0:T(8,128)(2,1)S(1)} %get-tuple-element.69), channel_id=1, source_target_pairs={{0,1},{1,0},{2,3},{3,2},{4,5},{5,4},{6,7},{7,6},{8,9},{9,8},{10,11... | collective-permute-start | bytes 393224 | tf_op jit(solution)/shard_map/ppermute | solution.py:23
  28.9 22.3 %collective-permute-start.7 = (bf16[512,128]{1,0:T(8,128)(2,1)S(1)}, bf16[512,128]{1,0:T(8,128)(2,1)S(1)}, u32[]{:S(2)}, u32[]{:S(2)}) collective-permute-start(bf16[512,128]{1,0:T(8,128)(2,1)S(1)} %get-tuple-element.70), channel_id=1, source_target_pairs={{0,2},{1,3},{2,0},{3,1},{4,6},{5,7},{6,4},{7,5},{8,10},{9,11},{10,... | collective-permute-start | bytes 393224 | tf_op jit(solution)/shard_map/ppermute | solution.py:23
  33.3 17.9 %collective-permute-start.8 = (bf16[512,128]{1,0:T(8,128)(2,1)S(1)}, bf16[512,128]{1,0:T(8,128)(2,1)S(1)}, u32[]{:S(2)}, u32[]{:S(2)}) collective-permute-start(bf16[512,128]{1,0:T(8,128)(2,1)S(1)} %get-tuple-element.71), channel_id=1, source_target_pairs={{0,3},{1,2},{2,1},{3,0},{4,7},{5,6},{6,5},{7,4},{8,11},{9,10},{10,... | collective-permute-start | bytes 393224 | tf_op jit(solution)/shard_map/ppermute | solution.py:23
  36.6 21.9 %collective-permute-start.10 = (bf16[512,128]{1,0:T(8,128)(2,1)S(1)}, bf16[512,128]{1,0:T(8,128)(2,1)S(1)}, u32[]{:S(2)}, u32[]{:S(2)}) collective-permute-start(bf16[512,128]{1,0:T(8,128)(2,1)S(1)} %get-tuple-element.74), channel_id=1, source_target_pairs={{0,2},{1,3},{2,0},{3,1},{4,6},{5,7},{6,4},{7,5},{8,10},{9,11},{10,... | collective-permute-start | bytes 393224 | tf_op jit(solution)/shard_map/ppermute | solution.py:23
  45.4 15.5 %collective-permute-start.11 = (bf16[512,128]{1,0:T(8,128)(2,1)S(1)}, bf16[512,128]{1,0:T(8,128)(2,1)S(1)}, u32[]{:S(2)}, u32[]{:S(2)}) collective-permute-start(bf16[512,128]{1,0:T(8,128)(2,1)S(1)} %get-tuple-element.75), channel_id=1, source_target_pairs={{0,3},{1,2},{2,1},{3,0},{4,7},{5,6},{6,5},{7,4},{8,11},{9,10},{10,... | collective-permute-start | bytes 393224 | tf_op jit(solution)/shard_map/ppermute | solution.py:23
  45.4 15.5 %collective-permute-start.9 = (bf16[512,128]{1,0:T(8,128)(2,1)S(1)}, bf16[512,128]{1,0:T(8,128)(2,1)S(1)}, u32[]{:S(2)}, u32[]{:S(2)}) collective-permute-start(bf16[512,128]{1,0:T(8,128)(2,1)S(1)} %get-tuple-element.73), channel_id=1, source_target_pairs={{0,1},{1,0},{2,3},{3,2},{4,5},{5,4},{6,7},{7,6},{8,9},{9,8},{10,11... | collective-permute-start | bytes 393224 | tf_op jit(solution)/shard_map/ppermute | solution.py:23
  53.8 14.9 %collective-permute-start.12 = (bf16[512,128]{1,0:T(8,128)(2,1)S(1)}, bf16[512,128]{1,0:T(8,128)(2,1)S(1)}, u32[]{:S(2)}, u32[]{:S(2)}) collective-permute-start(bf16[512,128]{1,0:T(8,128)(2,1)S(1)} %get-tuple-element.79), channel_id=1, source_target_pairs={{0,1},{1,0},{2,3},{3,2},{4,5},{5,4},{6,7},{7,6},{8,9},{9,8},{10,11... | collective-permute-start | bytes 393224 | tf_op jit(solution)/shard_map/ppermute | solution.py:23
  58.4 11.4 %collective-permute-start.13 = (bf16[512,128]{1,0:T(8,128)(2,1)S(1)}, bf16[512,128]{1,0:T(8,128)(2,1)S(1)}, u32[]{:S(2)}, u32[]{:S(2)}) collective-permute-start(bf16[512,128]{1,0:T(8,128)(2,1)S(1)} %get-tuple-element.80), channel_id=1, source_target_pairs={{0,2},{1,3},{2,0},{3,1},{4,6},{5,7},{6,4},{7,5},{8,10},{9,11},{10,... | collective-permute-start | bytes 393224 | tf_op jit(solution)/shard_map/ppermute | solution.py:23
  58.5 11.3 %collective-permute-start.14 = (bf16[512,128]{1,0:T(8,128)(2,1)S(1)}, bf16[512,128]{1,0:T(8,128)(2,1)S(1)}, u32[]{:S(2)}, u32[]{:S(2)}) collective-permute-start(bf16[512,128]{1,0:T(8,128)(2,1)S(1)} %get-tuple-element.81), channel_id=1, source_target_pairs={{0,3},{1,2},{2,1},{3,0},{4,7},{5,6},{6,5},{7,4},{8,11},{9,10},{10,... | collective-permute-start | bytes 393224 | tf_op jit(solution)/shard_map/ppermute | solution.py:23
  69.8 28.0 %all-to-all-start.1 = ((bf16[16,256,128]{2,1,0:T(8,128)(2,1)}), bf16[16,256,128]{2,1,0:T(8,128)(2,1)S(1)}, u32[]{:S(2)}, u32[]{:S(2)}) async-start(bf16[16,256,128]{2,1,0:T(8,128)(2,1)} %bitcast.5), calls=%async_computation.1 | async-start | bytes 2097152 | tf_op jit(solution)/shard_map/all_to_all | solution.py:314
  75.0 2.2 %collective-permute-start.15 = (bf16[512,128]{1,0:T(8,128)(2,1)S(1)}, bf16[512,128]{1,0:T(8,128)(2,1)S(1)}, u32[]{:S(2)}, u32[]{:S(2)}) collective-permute-start(bf16[512,128]{1,0:T(8,128)(2,1)S(1)} %get-tuple-element.90), channel_id=1, source_target_pairs={{0,4},{4,0},{8,12},{12,8},{16,20},{20,16},{24,28},{28,24},{1,5},{5... | collective-permute-start | bytes 393224 | tf_op jit(solution)/shard_map/ppermute | solution.py:23
  75.4 14.2 %collective-permute-start.16 = (bf16[512,128]{1,0:T(8,128)(2,1)S(1)}, bf16[512,128]{1,0:T(8,128)(2,1)S(1)}, u32[]{:S(2)}, u32[]{:S(2)}) collective-permute-start(bf16[512,128]{1,0:T(8,128)(2,1)S(1)} %get-tuple-element.91), channel_id=1, source_target_pairs={{0,8},{4,12},{8,0},{12,4},{16,24},{20,28},{24,16},{28,20},{1,9},{5... | collective-permute-start | bytes 393224 | tf_op jit(solution)/shard_map/ppermute | solution.py:23
  77.1 14.5 %collective-permute-start.17 = (bf16[512,128]{1,0:T(8,128)(2,1)S(1)}, bf16[512,128]{1,0:T(8,128)(2,1)S(1)}, u32[]{:S(2)}, u32[]{:S(2)}) collective-permute-start(bf16[512,128]{1,0:T(8,128)(2,1)S(1)} %get-tuple-element.92), channel_id=1, source_target_pairs={{0,12},{4,8},{8,4},{12,0},{16,28},{20,24},{24,20},{28,16},{1,13},{... | collective-permute-start | bytes 393224 | tf_op jit(solution)/shard_map/ppermute | solution.py:23

commit v4 on v3

--- a/solution.py
+++ b/solution.py
@@ -16,6 +16,7 @@
 VMEM_BYTES = 16 << 20
 IN_VMEM = pl.BlockSpec(memory_space=pltpu.VMEM)
 IN_SMEM = pl.BlockSpec(memory_space=pltpu.SMEM)
+IN_HBM = pl.BlockSpec(memory_space=pl.ANY)
 INDEX_ROWS = 16
 
 
@@ -31,15 +32,15 @@
     return pl.ds(pl.multiple_of(head * DH, DH), DH)
 
 
-def local_call(kernel, out_shape, scalars, arrays, scratch=(), flops=0):
+def local_call(kernel, out_shape, scalars, arrays, scratch=(), flops=0, arrays_in=IN_VMEM, vmem_bytes=VMEM_BYTES):
     moved = sum(x.size * x.dtype.itemsize for x in (*arrays, *jax.tree.leaves(out_shape)))
     return pl.pallas_call(
         kernel,
         out_shape=out_shape,
-        in_specs=[IN_SMEM] * len(scalars) + [IN_VMEM] * len(arrays),
+        in_specs=[IN_SMEM] * len(scalars) + [arrays_in] * len(arrays),
         out_specs=jax.tree.map(lambda _: IN_VMEM, out_shape),
         scratch_shapes=list(scratch),
-        compiler_params=pltpu.CompilerParams(vmem_limit_bytes=VMEM_BYTES),
+        compiler_params=pltpu.CompilerParams(vmem_limit_bytes=vmem_bytes),
         cost_estimate=pl.CostEstimate(flops=flops, bytes_accessed=moved, transcendentals=0),
         name=getattr(kernel, "func", kernel).__name__,
     )(*scalars, *arrays)
@@ -89,10 +90,17 @@
 
 
 def pack_natural(*refs):
-    *ins, out = refs
+    *ins, out, copied = refs
+    copies = []
     for head in range(ins[0].shape[1] // DH):
         for place, ref in enumerate(ins):
-            out[rows(head * len(ins) + place), :] = ref[:, head * DH : (head + 1) * DH]
+            target = head * len(ins) + place
+            source = ref.at[:, head * DH : (head + 1) * DH]
+            copies.append(pltpu.make_async_copy(source, out.at[rows(target), :], copied.at[target]))
+    for copy in copies:
+        copy.start()
+    for copy in copies:
+        copy.wait()
 
 
 def unpack_natural(ref, *outs):
@@ -254,7 +262,15 @@
     exchange = functools.partial(
         lax.all_to_all, axis_name=("ctx", "head"), split_axis=0, concat_axis=0, tiled=True, axis_index_groups=members
     )
-    joined = local_call(pack_natural, parts_of(2 * cluster, 1)[0], (), (queries, key_vecs))
+    joined = local_call(
+        pack_natural,
+        parts_of(2 * cluster, 1)[0],
+        (),
+        (queries, key_vecs),
+        [pltpu.SemaphoreType.DMA((2 * cluster,))],
+        arrays_in=IN_HBM,
+        vmem_bytes=58 << 20,
+    )
     later = (out_grads, value_vecs, local_offsets, partner_pool, partner_picks)
     joined, later = lax.optimization_barrier((joined, later))
     out_grads, value_vecs, local_offsets, partner_pool, partner_picks = later
@@ -277,6 +293,8 @@
         over_ctx(value),
     )
     joined, value = lax.optimization_barrier((joined, value))
+    middle, last = parts // 2, parts - 1
+    value[middle], grad[last] = lax.optimization_barrier((value[middle], grad[last]))
     value = over_head(value)
 
     pairs, keys = cluster // 2, key_count * BLK

time: 101 us -> 99.5 us (0.985)
  local copies, waits for them, and re-layouts: 6.47 us -> 4.39 us
  Pallas kernels: 20.3 us -> 21.6 us
    unnamed x8 -> x4, local copies, waits for them, and re-layouts: 4.16 us -> 2.08 us
    pallas_call x11, Pallas kernels: 20.3 us -> 21.6 us  [local_call(): pl.pallas_call(kernel, out_shape=out_shape, in_specs=[IN_SMEM] * len(scal...]
where the time goes in v4:
time: 99.5 us; the launch traced here: 97.9 us
  starting transfers between devices  40.1 us (40%)
  waiting for transfers between devices  30.9 us (31%)
  Pallas kernels  21.6 us (22%)
  local copies, waits for them, and re-layouts  4.39 us (4%)
    ppermute x18, starting transfers between devices, swapped(): lax.ppermute(value, axis, [(i, i ^ distance) for i in range(lax.axis_size...  28 us
    ppermute x18, waiting for transfers between devices, swapped(): lax.ppermute(value, axis, [(i, i ^ distance) for i in range(lax.axis_size...  26.1 us
    pallas_call x11, Pallas kernels, local_call(): pl.pallas_call(kernel, out_shape=out_shape, in_specs=[IN_SMEM] * len(scal...  21.6 us
    all_to_all x2, starting transfers between devices, whole_cluster(): joined = exchange(joined)  12.1 us
    all_to_all x2, waiting for transfers between devices, whole_cluster(): joined = exchange(joined)  4.78 us
    optimization_barrier x3, local copies, waits for them, and re-layouts, whole_cluster(): joined, later = lax.optimization_barrier((joined, later))  2.31 us
    unnamed x4, local copies, waits for them, and re-layouts  2.08 us
  transfers between devices with their start and end apart: 20, of which 8 were waited for; matrix products, arithmetic and copies ran while one was open for 2% of the time, Pallas kernels for 18%

profile of v4, /device:TPU:0, one launch (start us, length us, event | category | flops | bytes accessed | tf_op | source)
XLA Modules:
  0.0 97.9 jit_solution(5459437773259602568)
XLA Ops:
  0.6 2.5 %pack_natural.1 = bf16[4096,128]{1,0:T(8,128)(2,1)} custom-call(bf16[128,2048]{1,0:T(8,128)(2,1)} %refs_0_.1, bf16[128,2048]{1,0:T(8,128)(2,1)} %refs_1_.1), custom_call_target="tpu_custom_call" | custom-call | bytes 2097152 | tf_op jit(solution)/shard_map/pack_natural/pallas_call | solution.py:37
  3.1 7.4 %all-to-all-start = ((bf16[16,256,128]{2,1,0:T(8,128)(2,1)}), bf16[16,256,128]{2,1,0:T(8,128)(2,1)S(1)}, u32[]{:S(2)}, u32[]{:S(2)}) async-start(bf16[16,256,128]{2,1,0:T(8,128)(2,1)} %bitcast.10), calls=%async_computation | async-start | bytes 2097152 | tf_op jit(solution)/shard_map/all_to_all | solution.py:277
  10.5 0.1 pad_add_fusion.me_ref
  10.6 1.0 %copy-done = bf16[128,2048]{1,0:T(8,128)(2,1)S(1)} copy-done((bf16[128,2048]{1,0:T(8,128)(2,1)S(1)}, bf16[128,2048]{1,0:T(8,128)(2,1)}, u32[]{:S(2)}) %copy-start) | copy-done | bytes 524312
  11.6 0.7 pack.1
  12.3 0.5 collective-permute-start.3
  12.8 1.7 %collective-permute-start.4 = (bf16[512,128]{1,0:T(8,128)(2,1)S(1)}, bf16[512,128]{1,0:T(8,128)(2,1)S(1)}, u32[]{:S(2)}, u32[]{:S(2)}) collective-permute-start(bf16[512,128]{1,0:T(8,128)(2,1)S(1)} %get-tuple-element.68), channel_id=1, source_target_pairs={{0,8},{4,12},{8,0},{12,4},{16,24},{20,28},{24,16},{28,20},{1,9},{5... | collective-permute-start | bytes 393224 | tf_op jit(solution)/shard_map/ppermute | solution.py:24
  14.4 0.0 collective-permute-start.5
  14.4 0.8 copy.11.pool_ref
  15.2 0.8 copy.12.picks_ref
  16.0 0.8 copy.10.offsets_ref
  16.8 1.0 %copy-done.1 = bf16[128,2048]{1,0:T(8,128)(2,1)S(1)} copy-done((bf16[128,2048]{1,0:T(8,128)(2,1)S(1)}, bf16[128,2048]{1,0:T(8,128)(2,1)}, u32[]{:S(2)}) %copy-start.1) | copy-done | bytes 524312
  17.8 1.0 pack_with_index.1
  18.8 0.5 collective-permute-start
  19.3 1.7 %collective-permute-start.1 = (bf16[528,128]{1,0:T(8,128)(2,1)S(1)}, bf16[528,128]{1,0:T(8,128)(2,1)S(1)}, u32[]{:S(2)}, u32[]{:S(2)}) collective-permute-start(bf16[528,128]{1,0:T(8,128)(2,1)S(1)} %get-tuple-element.56), channel_id=1, source_target_pairs={{0,8},{4,12},{8,0},{12,4},{16,24},{20,28},{24,16},{28,20},{1,9},{5... | collective-permute-start | bytes 405512 | tf_op jit(solution)/shard_map/ppermute | solution.py:24
  21.0 0.0 collective-permute-done.3.refs_1_
  21.0 0.0 collective-permute-start.2
  21.0 4.2 %collective-permute-done.4.refs_2_ = bf16[512,128]{1,0:T(8,128)(2,1)S(1)} collective-permute-done((bf16[512,128]{1,0:T(8,128)(2,1)S(1)}, bf16[512,128]{1,0:T(8,128)(2,1)S(1)}, u32[]{:S(2)}, u32[]{:S(2)}) %collective-permute-start.4) | collective-permute-done | bytes 131104 | tf_op jit(solution)/shard_map/ppermute | solution.py:24
  25.1 2.9 %collective-permute-done.5.refs_3_ = bf16[512,128]{1,0:T(8,128)(2,1)S(1)} collective-permute-done((bf16[512,128]{1,0:T(8,128)(2,1)S(1)}, bf16[512,128]{1,0:T(8,128)(2,1)S(1)}, u32[]{:S(2)}, u32[]{:S(2)}) %collective-permute-start.5) | collective-permute-done | bytes 131104 | tf_op jit(solution)/shard_map/ppermute | solution.py:24
  28.1 3.9 %collective-permute-start.8 = (bf16[512,128]{1,0:T(8,128)(2,1)S(1)}, bf16[512,128]{1,0:T(8,128)(2,1)S(1)}, u32[]{:S(2)}, u32[]{:S(2)}) collective-permute-start(bf16[512,128]{1,0:T(8,128)(2,1)S(1)} %get-tuple-element.74), channel_id=1, source_target_pairs={{0,3},{1,2},{2,1},{3,0},{4,7},{5,6},{6,5},{7,4},{8,11},{9,10},{10,... | collective-permute-start | bytes 393224 | tf_op jit(solution)/shard_map/ppermute | solution.py:24
  31.9 0.0 collective-permute-start.6
  31.9 0.6 collective-permute-start.7
  32.6 0.0 collective-permute-done.1.refs_2_
  32.6 3.2 %collective-permute-done.2.refs_3_ = bf16[528,128]{1,0:T(8,128)(2,1)S(1)} collective-permute-done((bf16[528,128]{1,0:T(8,128)(2,1)S(1)}, bf16[528,128]{1,0:T(8,128)(2,1)S(1)}, u32[]{:S(2)}, u32[]{:S(2)}) %collective-permute-start.2) | collective-permute-done | bytes 135200 | tf_op jit(solution)/shard_map/ppermute | solution.py:24
  35.8 0.0 all-to-all-done
  35.8 0.6 collective-permute-done.8.refs_3_
  36.4 10.1 %collective-permute-start.10 = (bf16[512,128]{1,0:T(8,128)(2,1)S(1)}, bf16[512,128]{1,0:T(8,128)(2,1)S(1)}, u32[]{:S(2)}, u32[]{:S(2)}) collective-permute-start(bf16[512,128]{1,0:T(8,128)(2,1)S(1)} %get-tuple-element.78), channel_id=1, source_target_pairs={{0,2},{1,3},{2,0},{3,1},{4,6},{5,7},{6,4},{7,5},{8,10},{9,11},{10,... | collective-permute-start | bytes 393224 | tf_op jit(solution)/shard_map/ppermute | solution.py:24
  46.6 2.3 %collective-permute-start.11 = (bf16[512,128]{1,0:T(8,128)(2,1)S(1)}, bf16[512,128]{1,0:T(8,128)(2,1)S(1)}, u32[]{:S(2)}, u32[]{:S(2)}) collective-permute-start(bf16[512,128]{1,0:T(8,128)(2,1)S(1)} %get-tuple-element.79), channel_id=1, source_target_pairs={{0,3},{1,2},{2,1},{3,0},{4,7},{5,6},{6,5},{7,4},{8,11},{9,10},{10,... | collective-permute-start | bytes 393224 | tf_op jit(solution)/shard_map/ppermute | solution.py:24
  48.9 4.3 %softmax_weights.1 = (f32[8,768,256]{2,1,0:T(8,128)S(1)}, bf16[8,768,256]{2,1,0:T(8,128)(2,1)S(1)}) custom-call(s32[3]{0:T(128)S(1)} %pad_add_fusion.me_ref, s32[64,128]{1,0:T(8,128)S(1)} %get-tuple-element.58.index_ref, bf16[4096,128]{1,0:T(8,128)(2,1)S(1)} %bitcast.7), custom_call_target="tpu_custom_call" | custom-call | flops 402653184 | bytes 10485760 | tf_op jit(solution)/shard_map/softmax_weights/pallas_call | solution.py:37
  53.1 0.0 collective-permute-done.6.refs_1_
  53.2 2.6 %dv_parts.1 = (bf16[512,128]{1,0:T(8,128)(2,1)S(1)}, bf16[512,128]{1,0:T(8,128)(2,1)S(1)}, bf16[512,128]{1,0:T(8,128)(2,1)S(1)}, bf16[512,128]{1,0:T(8,128)(2,1)S(1)}) custom-call(s32[3]{0:T(128)S(1)} %pad_add_fusion.me_ref, s32[64,128]{1,0:T(8,128)S(1)} %get-tuple-element.58.index_ref, bf16[8,768,256]{2,1,0:T(8,128)(2,1)S(1)} %get-tuple-element.81.half_ref, ...), custom_call_target="tpu_custom_call" | custom-call | flops 402653184 | bytes 4194304 | tf_op jit(solution)/shard_map/dv_parts/pallas_call | solution.py:37
  55.8 2.1 %collective-permute-start.12 = (bf16[512,128]{1,0:T(8,128)(2,1)S(1)}, bf16[512,128]{1,0:T(8,128)(2,1)S(1)}, u32[]{:S(2)}, u32[]{:S(2)}) collective-permute-start(bf16[512,128]{1,0:T(8,128)(2,1)S(1)} %get-tuple-element.83), channel_id=1, source_target_pairs={{0,1},{1,0},{2,3},{3,2},{4,5},{5,4},{6,7},{7,6},{8,9},{9,8},{10,11... | collective-permute-start | bytes 393224 | tf_op jit(solution)/shard_map/ppermute | solution.py:24
  57.9 0.1 collective-permute-start.13
  58.0 2.3 %collective-permute-start.14 = (bf16[512,128]{1,0:T(8,128)(2,1)S(1)}, bf16[512,128]{1,0:T(8,128)(2,1)S(1)}, u32[]{:S(2)}, u32[]{:S(2)}) collective-permute-start(bf16[512,128]{1,0:T(8,128)(2,1)S(1)} %get-tuple-element.85), channel_id=1, source_target_pairs={{0,3},{1,2},{2,1},{3,0},{4,7},{5,6},{6,5},{7,4},{8,11},{9,10},{10,... | collective-permute-start | bytes 393224 | tf_op jit(solution)/shard_map/ppermute | solution.py:24
  60.3 0.0 collective-permute-done.11.refs_7_
  60.3 7.8 %dq_and_dk.1 = bf16[4096,128]{1,0:T(8,128)(2,1)} custom-call(s32[3]{0:T(128)S(1)} %pad_add_fusion.me_ref, s32[64,128]{1,0:T(8,128)S(1)} %get-tuple-element.58.index_ref, bf16[4096,128]{1,0:T(8,128)(2,1)S(1)} %bitcast.8, bf16[512,128]{1,0:T(8,128)(2,1)S(1)} %get-tuple-element.70.refs_0_, bf16[512,128]{1,0:T(8,128)(2,1)S(1)} %collective-permute-done.6.refs_1_, ...), custom_call_target="tpu_custom_call" | custom-call | flops 1207959552 | bytes 9437184 | tf_op jit(solution)/shard_map/dq_and_dk/pallas_call | solution.py:37
  68.1 0.0 collective-permute-done.12.refs_1_
  68.1 0.8 collective-permute-done.13.refs_2_
  68.9 4.7 %all-to-all-start.1 = ((bf16[16,256,128]{2,1,0:T(8,128)(2,1)}), bf16[16,256,128]{2,1,0:T(8,128)(2,1)S(1)}, u32[]{:S(2)}, u32[]{:S(2)}) async-start(bf16[16,256,128]{2,1,0:T(8,128)(2,1)} %bitcast.5), calls=%async_computation.1 | async-start | bytes 2097152 | tf_op jit(solution)/shard_map/all_to_all | solution.py:332
  73.7 0.5 collective-permute-start.15
  74.2 1.7 %collective-permute-start.16 = (bf16[512,128]{1,0:T(8,128)(2,1)S(1)}, bf16[512,128]{1,0:T(8,128)(2,1)S(1)}, u32[]{:S(2)}, u32[]{:S(2)}) collective-permute-start(bf16[512,128]{1,0:T(8,128)(2,1)S(1)} %get-tuple-element.95), channel_id=1, source_target_pairs={{0,8},{4,12},{8,0},{12,4},{16,24},{20,28},{24,16},{28,20},{1,9},{5... | collective-permute-start | bytes 393224 | tf_op jit(solution)/shard_map/ppermute | solution.py:24
  75.9 0.0 collective-permute-start.17
  75.9 0.0 collective-permute-done.15.refs_1_
  75.9 12.5 %collective-permute-done.16.refs_2_ = bf16[512,128]{1,0:T(8,128)(2,1)S(1)} collective-permute-done((bf16[512,128]{1,0:T(8,128)(2,1)S(1)}, bf16[512,128]{1,0:T(8,128)(2,1)S(1)}, u32[]{:S(2)}, u32[]{:S(2)}) %collective-permute-start.16) | collective-permute-done | bytes 131104 | tf_op jit(solution)/shard_map/ppermute | solution.py:24
  88.3 2.0 %collective-permute-done.17.refs_3_ = bf16[512,128]{1,0:T(8,128)(2,1)S(1)} collective-permute-done((bf16[512,128]{1,0:T(8,128)(2,1)S(1)}, bf16[512,128]{1,0:T(8,128)(2,1)S(1)}, u32[]{:S(2)}, u32[]{:S(2)}) %collective-permute-start.17) | collective-permute-done | bytes 131104 | tf_op jit(solution)/shard_map/ppermute | solution.py:24
  90.4 1.5 %unpack.1 = bf16[128,2048]{1,0:T(8,128)(2,1)} custom-call(s32[3]{0:T(128)S(1)} %pad_add_fusion.me_ref, bf16[512,128]{1,0:T(8,128)(2,1)S(1)} %get-tuple-element.93.refs_0_, bf16[512,128]{1,0:T(8,128)(2,1)S(1)} %collective-permute-done.15.refs_1_, bf16[512,128]{1,0:T(8,128)(2,1)S(1)} %collective-permute-done.16.refs_2_, ...), custom_call_target="tpu_custom_call" | custom-call | bytes 1048576 | tf_op jit(solution)/shard_map/unpack/pallas_call | solution.py:37
  91.8 4.8 %all-to-all-done.1 = bf16[16,256,128]{2,1,0:T(8,128)(2,1)S(1)} async-done(((bf16[16,256,128]{2,1,0:T(8,128)(2,1)}), bf16[16,256,128]{2,1,0:T(8,128)(2,1)S(1)}, u32[]{:S(2)}, u32[]{:S(2)}) %all-to-all-start.1) | async-done | bytes 1048608 | tf_op jit(solution)/shard_map/all_to_all | solution.py:332
  96.6 1.3 %unpack_natural.1 = (bf16[128,2048]{1,0:T(8,128)(2,1)}, bf16[128,2048]{1,0:T(8,128)(2,1)}) custom-call(bf16[4096,128]{1,0:T(8,128)(2,1)S(1)} %bitcast.9), custom_call_target="tpu_custom_call" | custom-call | bytes 2097152 | tf_op jit(solution)/shard_map/unpack_natural/pallas_call | solution.py:37
  (11 shorter events, 0.1 us)
Async XLA Ops:
  3.1 32.7 %all-to-all-start = ((bf16[16,256,128]{2,1,0:T(8,128)(2,1)}), bf16[16,256,128]{2,1,0:T(8,128)(2,1)S(1)}, u32[]{:S(2)}, u32[]{:S(2)}) async-start(bf16[16,256,128]{2,1,0:T(8,128)(2,1)} %bitcast.10), calls=%async_computation | async-start | bytes 2097152 | tf_op jit(solution)/shard_map/all_to_all | solution.py:277
  10.6 1.0 %copy-start = (bf16[128,2048]{1,0:T(8,128)(2,1)S(1)}, bf16[128,2048]{1,0:T(8,128)(2,1)}, u32[]{:S(2)}) copy-start(bf16[128,2048]{1,0:T(8,128)(2,1)} %refs_0_.3) | copy-start | bytes 1572868
  12.3 8.7 %collective-permute-start.3 = (bf16[512,128]{1,0:T(8,128)(2,1)S(1)}, bf16[512,128]{1,0:T(8,128)(2,1)S(1)}, u32[]{:S(2)}, u32[]{:S(2)}) collective-permute-start(bf16[512,128]{1,0:T(8,128)(2,1)S(1)} %get-tuple-element.67), channel_id=1, source_target_pairs={{0,4},{4,0},{8,12},{12,8},{16,20},{20,16},{24,28},{28,24},{1,5},{5... | collective-permute-start | bytes 393224 | tf_op jit(solution)/shard_map/ppermute | solution.py:24
  12.8 12.4 %collective-permute-start.4 = (bf16[512,128]{1,0:T(8,128)(2,1)S(1)}, bf16[512,128]{1,0:T(8,128)(2,1)S(1)}, u32[]{:S(2)}, u32[]{:S(2)}) collective-permute-start(bf16[512,128]{1,0:T(8,128)(2,1)S(1)} %get-tuple-element.68), channel_id=1, source_target_pairs={{0,8},{4,12},{8,0},{12,4},{16,24},{20,28},{24,16},{28,20},{1,9},{5... | collective-permute-start | bytes 393224 | tf_op jit(solution)/shard_map/ppermute | solution.py:24
  14.4 13.6 %collective-permute-start.5 = (bf16[512,128]{1,0:T(8,128)(2,1)S(1)}, bf16[512,128]{1,0:T(8,128)(2,1)S(1)}, u32[]{:S(2)}, u32[]{:S(2)}) collective-permute-start(bf16[512,128]{1,0:T(8,128)(2,1)S(1)} %get-tuple-element.69), channel_id=1, source_target_pairs={{0,12},{4,8},{8,4},{12,0},{16,28},{20,24},{24,20},{28,16},{1,13},{... | collective-permute-start | bytes 393224 | tf_op jit(solution)/shard_map/ppermute | solution.py:24
  16.8 1.0 %copy-start.1 = (bf16[128,2048]{1,0:T(8,128)(2,1)S(1)}, bf16[128,2048]{1,0:T(8,128)(2,1)}, u32[]{:S(2)}) copy-start(bf16[128,2048]{1,0:T(8,128)(2,1)} %refs_0_.2) | copy-start | bytes 1572868
  18.8 13.2 %collective-permute-start = (bf16[528,128]{1,0:T(8,128)(2,1)S(1)}, bf16[528,128]{1,0:T(8,128)(2,1)S(1)}, u32[]{:S(2)}, u32[]{:S(2)}) collective-permute-start(bf16[528,128]{1,0:T(8,128)(2,1)S(1)} %get-tuple-element.55), channel_id=1, source_target_pairs={{0,4},{4,0},{8,12},{12,8},{16,20},{20,16},{24,28},{28,24},{1,5},{5... | collective-permute-start | bytes 405512 | tf_op jit(solution)/shard_map/ppermute | solution.py:24
  19.3 13.3 %collective-permute-start.1 = (bf16[528,128]{1,0:T(8,128)(2,1)S(1)}, bf16[528,128]{1,0:T(8,128)(2,1)S(1)}, u32[]{:S(2)}, u32[]{:S(2)}) collective-permute-start(bf16[528,128]{1,0:T(8,128)(2,1)S(1)} %get-tuple-element.56), channel_id=1, source_target_pairs={{0,8},{4,12},{8,0},{12,4},{16,24},{20,28},{24,16},{28,20},{1,9},{5... | collective-permute-start | bytes 405512 | tf_op jit(solution)/shard_map/ppermute | solution.py:24
  21.0 14.8 %collective-permute-start.2 = (bf16[528,128]{1,0:T(8,128)(2,1)S(1)}, bf16[528,128]{1,0:T(8,128)(2,1)S(1)}, u32[]{:S(2)}, u32[]{:S(2)}) collective-permute-start(bf16[528,128]{1,0:T(8,128)(2,1)S(1)} %get-tuple-element.57), channel_id=1, source_target_pairs={{0,12},{4,8},{8,4},{12,0},{16,28},{20,24},{24,20},{28,16},{1,13},{... | collective-permute-start | bytes 405512 | tf_op jit(solution)/shard_map/ppermute | solution.py:24
  28.1 8.4 %collective-permute-start.8 = (bf16[512,128]{1,0:T(8,128)(2,1)S(1)}, bf16[512,128]{1,0:T(8,128)(2,1)S(1)}, u32[]{:S(2)}, u32[]{:S(2)}) collective-permute-start(bf16[512,128]{1,0:T(8,128)(2,1)S(1)} %get-tuple-element.74), channel_id=1, source_target_pairs={{0,3},{1,2},{2,1},{3,0},{4,7},{5,6},{6,5},{7,4},{8,11},{9,10},{10,... | collective-permute-start | bytes 393224 | tf_op jit(solution)/shard_map/ppermute | solution.py:24
  31.9 21.2 %collective-permute-start.6 = (bf16[512,128]{1,0:T(8,128)(2,1)S(1)}, bf16[512,128]{1,0:T(8,128)(2,1)S(1)}, u32[]{:S(2)}, u32[]{:S(2)}) collective-permute-start(bf16[512,128]{1,0:T(8,128)(2,1)S(1)} %get-tuple-element.71), channel_id=1, source_target_pairs={{0,1},{1,0},{2,3},{3,2},{4,5},{5,4},{6,7},{7,6},{8,9},{9,8},{10,11... | collective-permute-start | bytes 393224 | tf_op jit(solution)/shard_map/ppermute | solution.py:24
  31.9 21.2 %collective-permute-start.7 = (bf16[512,128]{1,0:T(8,128)(2,1)S(1)}, bf16[512,128]{1,0:T(8,128)(2,1)S(1)}, u32[]{:S(2)}, u32[]{:S(2)}) collective-permute-start(bf16[512,128]{1,0:T(8,128)(2,1)S(1)} %get-tuple-element.72), channel_id=1, source_target_pairs={{0,2},{1,3},{2,0},{3,1},{4,6},{5,7},{6,4},{7,5},{8,10},{9,11},{10,... | collective-permute-start | bytes 393224 | tf_op jit(solution)/shard_map/ppermute | solution.py:24
  36.4 21.6 %collective-permute-start.10 = (bf16[512,128]{1,0:T(8,128)(2,1)S(1)}, bf16[512,128]{1,0:T(8,128)(2,1)S(1)}, u32[]{:S(2)}, u32[]{:S(2)}) collective-permute-start(bf16[512,128]{1,0:T(8,128)(2,1)S(1)} %get-tuple-element.78), channel_id=1, source_target_pairs={{0,2},{1,3},{2,0},{3,1},{4,6},{5,7},{6,4},{7,5},{8,10},{9,11},{10,... | collective-permute-start | bytes 393224 | tf_op jit(solution)/shard_map/ppermute | solution.py:24
  46.6 13.8 %collective-permute-start.11 = (bf16[512,128]{1,0:T(8,128)(2,1)S(1)}, bf16[512,128]{1,0:T(8,128)(2,1)S(1)}, u32[]{:S(2)}, u32[]{:S(2)}) collective-permute-start(bf16[512,128]{1,0:T(8,128)(2,1)S(1)} %get-tuple-element.79), channel_id=1, source_target_pairs={{0,3},{1,2},{2,1},{3,0},{4,7},{5,6},{6,5},{7,4},{8,11},{9,10},{10,... | collective-permute-start | bytes 393224 | tf_op jit(solution)/shard_map/ppermute | solution.py:24
  48.8 11.5 %collective-permute-start.9 = (bf16[512,128]{1,0:T(8,128)(2,1)S(1)}, bf16[512,128]{1,0:T(8,128)(2,1)S(1)}, u32[]{:S(2)}, u32[]{:S(2)}) collective-permute-start(bf16[512,128]{1,0:T(8,128)(2,1)S(1)} %get-tuple-element.77), channel_id=1, source_target_pairs={{0,1},{1,0},{2,3},{3,2},{4,5},{5,4},{6,7},{7,6},{8,9},{9,8},{10,11... | collective-permute-start | bytes 393224 | tf_op jit(solution)/shard_map/ppermute | solution.py:24
  55.8 12.3 %collective-permute-start.12 = (bf16[512,128]{1,0:T(8,128)(2,1)S(1)}, bf16[512,128]{1,0:T(8,128)(2,1)S(1)}, u32[]{:S(2)}, u32[]{:S(2)}) collective-permute-start(bf16[512,128]{1,0:T(8,128)(2,1)S(1)} %get-tuple-element.83), channel_id=1, source_target_pairs={{0,1},{1,0},{2,3},{3,2},{4,5},{5,4},{6,7},{7,6},{8,9},{9,8},{10,11... | collective-permute-start | bytes 393224 | tf_op jit(solution)/shard_map/ppermute | solution.py:24
  57.9 11.0 %collective-permute-start.13 = (bf16[512,128]{1,0:T(8,128)(2,1)S(1)}, bf16[512,128]{1,0:T(8,128)(2,1)S(1)}, u32[]{:S(2)}, u32[]{:S(2)}) collective-permute-start(bf16[512,128]{1,0:T(8,128)(2,1)S(1)} %get-tuple-element.84), channel_id=1, source_target_pairs={{0,2},{1,3},{2,0},{3,1},{4,6},{5,7},{6,4},{7,5},{8,10},{9,11},{10,... | collective-permute-start | bytes 393224 | tf_op jit(solution)/shard_map/ppermute | solution.py:24
  58.0 10.9 %collective-permute-start.14 = (bf16[512,128]{1,0:T(8,128)(2,1)S(1)}, bf16[512,128]{1,0:T(8,128)(2,1)S(1)}, u32[]{:S(2)}, u32[]{:S(2)}) collective-permute-start(bf16[512,128]{1,0:T(8,128)(2,1)S(1)} %get-tuple-element.85), channel_id=1, source_target_pairs={{0,3},{1,2},{2,1},{3,0},{4,7},{5,6},{6,5},{7,4},{8,11},{9,10},{10,... | collective-permute-start | bytes 393224 | tf_op jit(solution)/shard_map/ppermute | solution.py:24
  68.9 27.7 %all-to-all-start.1 = ((bf16[16,256,128]{2,1,0:T(8,128)(2,1)}), bf16[16,256,128]{2,1,0:T(8,128)(2,1)S(1)}, u32[]{:S(2)}, u32[]{:S(2)}) async-start(bf16[16,256,128]{2,1,0:T(8,128)(2,1)} %bitcast.5), calls=%async_computation.1 | async-start | bytes 2097152 | tf_op jit(solution)/shard_map/all_to_all | solution.py:332
  73.7 2.2 %collective-permute-start.15 = (bf16[512,128]{1,0:T(8,128)(2,1)S(1)}, bf16[512,128]{1,0:T(8,128)(2,1)S(1)}, u32[]{:S(2)}, u32[]{:S(2)}) collective-permute-start(bf16[512,128]{1,0:T(8,128)(2,1)S(1)} %get-tuple-element.94), channel_id=1, source_target_pairs={{0,4},{4,0},{8,12},{12,8},{16,20},{20,16},{24,28},{28,24},{1,5},{5... | collective-permute-start | bytes 393224 | tf_op jit(solution)/shard_map/ppermute | solution.py:24
  74.2 14.2 %collective-permute-start.16 = (bf16[512,128]{1,0:T(8,128)(2,1)S(1)}, bf16[512,128]{1,0:T(8,128)(2,1)S(1)}, u32[]{:S(2)}, u32[]{:S(2)}) collective-permute-start(bf16[512,128]{1,0:T(8,128)(2,1)S(1)} %get-tuple-element.95), channel_id=1, source_target_pairs={{0,8},{4,12},{8,0},{12,4},{16,24},{20,28},{24,16},{28,20},{1,9},{5... | collective-permute-start | bytes 393224 | tf_op jit(solution)/shard_map/ppermute | solution.py:24
  75.9 14.5 %collective-permute-start.17 = (bf16[512,128]{1,0:T(8,128)(2,1)S(1)}, bf16[512,128]{1,0:T(8,128)(2,1)S(1)}, u32[]{:S(2)}, u32[]{:S(2)}) collective-permute-start(bf16[512,128]{1,0:T(8,128)(2,1)S(1)} %get-tuple-element.96), channel_id=1, source_target_pairs={{0,12},{4,8},{8,4},{12,0},{16,28},{20,24},{24,20},{28,16},{1,13},{... | collective-permute-start | bytes 393224 | tf_op jit(solution)/shard_map/ppermute | solution.py:24

commit v5 on v4

--- a/solution.py
+++ b/solution.py
@@ -32,13 +32,13 @@
     return pl.ds(pl.multiple_of(head * DH, DH), DH)
 
 
-def local_call(kernel, out_shape, scalars, arrays, scratch=(), flops=0, arrays_in=IN_VMEM, vmem_bytes=VMEM_BYTES):
+def local_call(kernel, out_shape, scalars, arrays, scratch=(), flops=0, arrays_in=IN_VMEM, outs_in=IN_VMEM, vmem_bytes=VMEM_BYTES):
     moved = sum(x.size * x.dtype.itemsize for x in (*arrays, *jax.tree.leaves(out_shape)))
     return pl.pallas_call(
         kernel,
         out_shape=out_shape,
         in_specs=[IN_SMEM] * len(scalars) + [arrays_in] * len(arrays),
-        out_specs=jax.tree.map(lambda _: IN_VMEM, out_shape),
+        out_specs=jax.tree.map(lambda _: outs_in, out_shape),
         scratch_shapes=list(scratch),
         compiler_params=pltpu.CompilerParams(vmem_limit_bytes=vmem_bytes),
         cost_estimate=pl.CostEstimate(flops=flops, bytes_accessed=moved, transcendentals=0),
@@ -103,10 +103,18 @@
         copy.wait()
 
 
-def unpack_natural(ref, *outs):
+def unpack_natural(ref, *refs):
+    *outs, copied = refs
+    copies = []
     for head in range(outs[0].shape[1] // DH):
         for place, out in enumerate(outs):
-            out[:, head * DH : (head + 1) * DH] = ref[rows(head * len(outs) + place), :]
+            source = head * len(outs) + place
+            target = out.at[:, head * DH : (head + 1) * DH]
+            copies.append(pltpu.make_async_copy(ref.at[rows(source), :], target, copied.at[source]))
+    for copy in copies:
+        copy.start()
+    for copy in copies:
+        copy.wait()
 
 
 def regroup(*refs, count, places):
@@ -334,7 +342,9 @@
     dv = over_ctx(dv)
     out = jax.ShapeDtypeStruct(queries.shape, queries.dtype)
     value_grads = local_call(functools.partial(unpack, by="ctx", near=near), out, (me,), dv)
-    query_grads, key_grads = local_call(unpack_natural, [out] * 2, (), (joined,))
+    query_grads, key_grads = local_call(
+        unpack_natural, [out] * 2, (), (joined,), [pltpu.SemaphoreType.DMA((2 * cluster,))], outs_in=IN_HBM
+    )
     return query_grads, key_grads, value_grads
 
 

time: 99.5 us -> 99.5 us (level)
  no operation moved by 1% of the time
where the time goes in v5:
time: 99.5 us; the launch traced here: 97.8 us
  starting transfers between devices  40.1 us (40%)
  waiting for transfers between devices  30.9 us (31%)
  Pallas kernels  21.6 us (22%)
  local copies, waits for them, and re-layouts  4.39 us (4%)
    ppermute x18, starting transfers between devices, swapped(): lax.ppermute(value, axis, [(i, i ^ distance) for i in range(lax.axis_size...  28 us
    ppermute x18, waiting for transfers between devices, swapped(): lax.ppermute(value, axis, [(i, i ^ distance) for i in range(lax.axis_size...  26.1 us
    pallas_call x11, Pallas kernels, local_call(): pl.pallas_call(kernel, out_shape=out_shape, in_specs=[IN_SMEM] * len(scal...  21.6 us
    all_to_all x2, starting transfers between devices, whole_cluster(): joined = exchange(joined)  12.1 us
    all_to_all x2, waiting for transfers between devices, whole_cluster(): joined = exchange(joined)  4.78 us
    optimization_barrier x3, local copies, waits for them, and re-layouts, whole_cluster(): joined, later = lax.optimization_barrier((joined, later))  2.31 us
    unnamed x4, local copies, waits for them, and re-layouts  2.08 us
  transfers between devices with their start and end apart: 20, of which 8 were waited for; matrix products, arithmetic and copies ran while one was open for 2% of the time, Pallas kernels for 18%

profile of v5, /device:TPU:0, one launch (start us, length us, event | category | flops | bytes accessed | tf_op | source)
XLA Modules:
  0.0 97.8 jit_solution(6154208513551595638)
XLA Ops:
  0.6 2.5 %pack_natural.1 = bf16[4096,128]{1,0:T(8,128)(2,1)} custom-call(bf16[128,2048]{1,0:T(8,128)(2,1)} %refs_0_.1, bf16[128,2048]{1,0:T(8,128)(2,1)} %refs_1_.1), custom_call_target="tpu_custom_call" | custom-call | bytes 2097152 | tf_op jit(solution)/shard_map/pack_natural/pallas_call | solution.py:37
  3.1 7.4 %all-to-all-start = ((bf16[16,256,128]{2,1,0:T(8,128)(2,1)}), bf16[16,256,128]{2,1,0:T(8,128)(2,1)S(1)}, u32[]{:S(2)}, u32[]{:S(2)}) async-start(bf16[16,256,128]{2,1,0:T(8,128)(2,1)} %bitcast.10), calls=%async_computation | async-start | bytes 2097152 | tf_op jit(solution)/shard_map/all_to_all | solution.py:285
  10.5 0.1 pad_add_fusion.me_ref
  10.6 1.0 %copy-done = bf16[128,2048]{1,0:T(8,128)(2,1)S(1)} copy-done((bf16[128,2048]{1,0:T(8,128)(2,1)S(1)}, bf16[128,2048]{1,0:T(8,128)(2,1)}, u32[]{:S(2)}) %copy-start) | copy-done | bytes 524312
  11.6 0.7 pack.1
  12.3 0.5 collective-permute-start.3
  12.8 1.7 %collective-permute-start.4 = (bf16[512,128]{1,0:T(8,128)(2,1)S(1)}, bf16[512,128]{1,0:T(8,128)(2,1)S(1)}, u32[]{:S(2)}, u32[]{:S(2)}) collective-permute-start(bf16[512,128]{1,0:T(8,128)(2,1)S(1)} %get-tuple-element.68), channel_id=1, source_target_pairs={{0,8},{4,12},{8,0},{12,4},{16,24},{20,28},{24,16},{28,20},{1,9},{5... | collective-permute-start | bytes 393224 | tf_op jit(solution)/shard_map/ppermute | solution.py:24
  14.4 0.0 collective-permute-start.5
  14.4 0.8 copy.11.pool_ref
  15.2 0.8 copy.12.picks_ref
  16.0 0.8 copy.10.offsets_ref
  16.8 1.0 %copy-done.1 = bf16[128,2048]{1,0:T(8,128)(2,1)S(1)} copy-done((bf16[128,2048]{1,0:T(8,128)(2,1)S(1)}, bf16[128,2048]{1,0:T(8,128)(2,1)}, u32[]{:S(2)}) %copy-start.1) | copy-done | bytes 524312
  17.8 1.0 pack_with_index.1
  18.8 0.5 collective-permute-start
  19.3 1.7 %collective-permute-start.1 = (bf16[528,128]{1,0:T(8,128)(2,1)S(1)}, bf16[528,128]{1,0:T(8,128)(2,1)S(1)}, u32[]{:S(2)}, u32[]{:S(2)}) collective-permute-start(bf16[528,128]{1,0:T(8,128)(2,1)S(1)} %get-tuple-element.56), channel_id=1, source_target_pairs={{0,8},{4,12},{8,0},{12,4},{16,24},{20,28},{24,16},{28,20},{1,9},{5... | collective-permute-start | bytes 405512 | tf_op jit(solution)/shard_map/ppermute | solution.py:24
  21.0 0.0 collective-permute-done.3.refs_1_
  21.0 0.0 collective-permute-start.2
  21.0 4.2 %collective-permute-done.4.refs_2_ = bf16[512,128]{1,0:T(8,128)(2,1)S(1)} collective-permute-done((bf16[512,128]{1,0:T(8,128)(2,1)S(1)}, bf16[512,128]{1,0:T(8,128)(2,1)S(1)}, u32[]{:S(2)}, u32[]{:S(2)}) %collective-permute-start.4) | collective-permute-done | bytes 131104 | tf_op jit(solution)/shard_map/ppermute | solution.py:24
  25.1 2.9 %collective-permute-done.5.refs_3_ = bf16[512,128]{1,0:T(8,128)(2,1)S(1)} collective-permute-done((bf16[512,128]{1,0:T(8,128)(2,1)S(1)}, bf16[512,128]{1,0:T(8,128)(2,1)S(1)}, u32[]{:S(2)}, u32[]{:S(2)}) %collective-permute-start.5) | collective-permute-done | bytes 131104 | tf_op jit(solution)/shard_map/ppermute | solution.py:24
  28.1 3.9 %collective-permute-start.8 = (bf16[512,128]{1,0:T(8,128)(2,1)S(1)}, bf16[512,128]{1,0:T(8,128)(2,1)S(1)}, u32[]{:S(2)}, u32[]{:S(2)}) collective-permute-start(bf16[512,128]{1,0:T(8,128)(2,1)S(1)} %get-tuple-element.74), channel_id=1, source_target_pairs={{0,3},{1,2},{2,1},{3,0},{4,7},{5,6},{6,5},{7,4},{8,11},{9,10},{10,... | collective-permute-start | bytes 393224 | tf_op jit(solution)/shard_map/ppermute | solution.py:24
  31.9 0.0 collective-permute-done.refs_1_
  31.9 0.6 collective-permute-start.7
  32.6 3.2 %collective-permute-done.2.refs_3_ = bf16[528,128]{1,0:T(8,128)(2,1)S(1)} collective-permute-done((bf16[528,128]{1,0:T(8,128)(2,1)S(1)}, bf16[528,128]{1,0:T(8,128)(2,1)S(1)}, u32[]{:S(2)}, u32[]{:S(2)}) %collective-permute-start.2) | collective-permute-done | bytes 135200 | tf_op jit(solution)/shard_map/ppermute | solution.py:24
  35.8 0.6 collective-permute-done.8.refs_3_
  36.4 10.1 %collective-permute-start.10 = (bf16[512,128]{1,0:T(8,128)(2,1)S(1)}, bf16[512,128]{1,0:T(8,128)(2,1)S(1)}, u32[]{:S(2)}, u32[]{:S(2)}) collective-permute-start(bf16[512,128]{1,0:T(8,128)(2,1)S(1)} %get-tuple-element.78), channel_id=1, source_target_pairs={{0,2},{1,3},{2,0},{3,1},{4,6},{5,7},{6,4},{7,5},{8,10},{9,11},{10,... | collective-permute-start | bytes 393224 | tf_op jit(solution)/shard_map/ppermute | solution.py:24
  46.6 2.3 %collective-permute-start.11 = (bf16[512,128]{1,0:T(8,128)(2,1)S(1)}, bf16[512,128]{1,0:T(8,128)(2,1)S(1)}, u32[]{:S(2)}, u32[]{:S(2)}) collective-permute-start(bf16[512,128]{1,0:T(8,128)(2,1)S(1)} %get-tuple-element.79), channel_id=1, source_target_pairs={{0,3},{1,2},{2,1},{3,0},{4,7},{5,6},{6,5},{7,4},{8,11},{9,10},{10,... | collective-permute-start | bytes 393224 | tf_op jit(solution)/shard_map/ppermute | solution.py:24
  48.8 0.0 collective-permute-start.9
  48.9 4.3 %softmax_weights.1 = (f32[8,768,256]{2,1,0:T(8,128)S(1)}, bf16[8,768,256]{2,1,0:T(8,128)(2,1)S(1)}) custom-call(s32[3]{0:T(128)S(1)} %pad_add_fusion.me_ref, s32[64,128]{1,0:T(8,128)S(1)} %get-tuple-element.58.index_ref, bf16[4096,128]{1,0:T(8,128)(2,1)S(1)} %bitcast.7), custom_call_target="tpu_custom_call" | custom-call | flops 402653184 | bytes 10485760 | tf_op jit(solution)/shard_map/softmax_weights/pallas_call | solution.py:37
  53.1 0.0 collective-permute-done.6.refs_1_
  53.1 0.0 collective-permute-done.7.refs_2_
  53.2 2.6 %dv_parts.1 = (bf16[512,128]{1,0:T(8,128)(2,1)S(1)}, bf16[512,128]{1,0:T(8,128)(2,1)S(1)}, bf16[512,128]{1,0:T(8,128)(2,1)S(1)}, bf16[512,128]{1,0:T(8,128)(2,1)S(1)}) custom-call(s32[3]{0:T(128)S(1)} %pad_add_fusion.me_ref, s32[64,128]{1,0:T(8,128)S(1)} %get-tuple-element.58.index_ref, bf16[8,768,256]{2,1,0:T(8,128)(2,1)S(1)} %get-tuple-element.81.half_ref, ...), custom_call_target="tpu_custom_call" | custom-call | flops 402653184 | bytes 4194304 | tf_op jit(solution)/shard_map/dv_parts/pallas_call | solution.py:37
  55.8 2.1 %collective-permute-start.12 = (bf16[512,128]{1,0:T(8,128)(2,1)S(1)}, bf16[512,128]{1,0:T(8,128)(2,1)S(1)}, u32[]{:S(2)}, u32[]{:S(2)}) collective-permute-start(bf16[512,128]{1,0:T(8,128)(2,1)S(1)} %get-tuple-element.83), channel_id=1, source_target_pairs={{0,1},{1,0},{2,3},{3,2},{4,5},{5,4},{6,7},{7,6},{8,9},{9,8},{10,11... | collective-permute-start | bytes 393224 | tf_op jit(solution)/shard_map/ppermute | solution.py:24
  57.9 0.1 collective-permute-start.13
  58.0 0.0 collective-permute-done.10.refs_6_
  58.0 2.3 %collective-permute-start.14 = (bf16[512,128]{1,0:T(8,128)(2,1)S(1)}, bf16[512,128]{1,0:T(8,128)(2,1)S(1)}, u32[]{:S(2)}, u32[]{:S(2)}) collective-permute-start(bf16[512,128]{1,0:T(8,128)(2,1)S(1)} %get-tuple-element.85), channel_id=1, source_target_pairs={{0,3},{1,2},{2,1},{3,0},{4,7},{5,6},{6,5},{7,4},{8,11},{9,10},{10,... | collective-permute-start | bytes 393224 | tf_op jit(solution)/shard_map/ppermute | solution.py:24
  60.3 0.0 collective-permute-done.9.refs_5_
  60.3 7.8 %dq_and_dk.1 = bf16[4096,128]{1,0:T(8,128)(2,1)} custom-call(s32[3]{0:T(128)S(1)} %pad_add_fusion.me_ref, s32[64,128]{1,0:T(8,128)S(1)} %get-tuple-element.58.index_ref, bf16[4096,128]{1,0:T(8,128)(2,1)S(1)} %bitcast.8, bf16[512,128]{1,0:T(8,128)(2,1)S(1)} %get-tuple-element.70.refs_0_, bf16[512,128]{1,0:T(8,128)(2,1)S(1)} %collective-permute-done.6.refs_1_, ...), custom_call_target="tpu_custom_call" | custom-call | flops 1207959552 | bytes 9437184 | tf_op jit(solution)/shard_map/dq_and_dk/pallas_call | solution.py:37
  68.1 0.0 collective-permute-done.12.refs_1_
  68.1 0.8 collective-permute-done.13.refs_2_
  68.9 0.0 collective-permute-done.14.refs_3_
  68.9 4.7 %all-to-all-start.1 = ((bf16[16,256,128]{2,1,0:T(8,128)(2,1)}), bf16[16,256,128]{2,1,0:T(8,128)(2,1)S(1)}, u32[]{:S(2)}, u32[]{:S(2)}) async-start(bf16[16,256,128]{2,1,0:T(8,128)(2,1)} %bitcast.5), calls=%async_computation.1 | async-start | bytes 2097152 | tf_op jit(solution)/shard_map/all_to_all | solution.py:340
  73.7 0.5 collective-permute-start.15
  74.2 1.7 %collective-permute-start.16 = (bf16[512,128]{1,0:T(8,128)(2,1)S(1)}, bf16[512,128]{1,0:T(8,128)(2,1)S(1)}, u32[]{:S(2)}, u32[]{:S(2)}) collective-permute-start(bf16[512,128]{1,0:T(8,128)(2,1)S(1)} %get-tuple-element.95), channel_id=1, source_target_pairs={{0,8},{4,12},{8,0},{12,4},{16,24},{20,28},{24,16},{28,20},{1,9},{5... | collective-permute-start | bytes 393224 | tf_op jit(solution)/shard_map/ppermute | solution.py:24
  75.9 12.5 %collective-permute-done.16.refs_2_ = bf16[512,128]{1,0:T(8,128)(2,1)S(1)} collective-permute-done((bf16[512,128]{1,0:T(8,128)(2,1)S(1)}, bf16[512,128]{1,0:T(8,128)(2,1)S(1)}, u32[]{:S(2)}, u32[]{:S(2)}) %collective-permute-start.16) | collective-permute-done | bytes 131104 | tf_op jit(solution)/shard_map/ppermute | solution.py:24
  88.3 2.0 %collective-permute-done.17.refs_3_ = bf16[512,128]{1,0:T(8,128)(2,1)S(1)} collective-permute-done((bf16[512,128]{1,0:T(8,128)(2,1)S(1)}, bf16[512,128]{1,0:T(8,128)(2,1)S(1)}, u32[]{:S(2)}, u32[]{:S(2)}) %collective-permute-start.17) | collective-permute-done | bytes 131104 | tf_op jit(solution)/shard_map/ppermute | solution.py:24
  90.4 1.5 %unpack.1 = bf16[128,2048]{1,0:T(8,128)(2,1)} custom-call(s32[3]{0:T(128)S(1)} %pad_add_fusion.me_ref, bf16[512,128]{1,0:T(8,128)(2,1)S(1)} %get-tuple-element.93.refs_0_, bf16[512,128]{1,0:T(8,128)(2,1)S(1)} %collective-permute-done.15.refs_1_, bf16[512,128]{1,0:T(8,128)(2,1)S(1)} %collective-permute-done.16.refs_2_, ...), custom_call_target="tpu_custom_call" | custom-call | bytes 1048576 | tf_op jit(solution)/shard_map/unpack/pallas_call | solution.py:37
  91.8 4.8 %all-to-all-done.1 = bf16[16,256,128]{2,1,0:T(8,128)(2,1)S(1)} async-done(((bf16[16,256,128]{2,1,0:T(8,128)(2,1)}), bf16[16,256,128]{2,1,0:T(8,128)(2,1)S(1)}, u32[]{:S(2)}, u32[]{:S(2)}) %all-to-all-start.1) | async-done | bytes 1048608 | tf_op jit(solution)/shard_map/all_to_all | solution.py:340
  96.6 1.2 %unpack_natural.1 = (bf16[128,2048]{1,0:T(8,128)(2,1)}, bf16[128,2048]{1,0:T(8,128)(2,1)}) custom-call(bf16[4096,128]{1,0:T(8,128)(2,1)S(1)} %bitcast.9), custom_call_target="tpu_custom_call" | custom-call | bytes 2097152 | tf_op jit(solution)/shard_map/unpack_natural/pallas_call | solution.py:37
  (11 shorter events, 0.1 us)
Async XLA Ops:
  3.1 32.7 %all-to-all-start = ((bf16[16,256,128]{2,1,0:T(8,128)(2,1)}), bf16[16,256,128]{2,1,0:T(8,128)(2,1)S(1)}, u32[]{:S(2)}, u32[]{:S(2)}) async-start(bf16[16,256,128]{2,1,0:T(8,128)(2,1)} %bitcast.10), calls=%async_computation | async-start | bytes 2097152 | tf_op jit(solution)/shard_map/all_to_all | solution.py:285
  10.6 1.0 %copy-start = (bf16[128,2048]{1,0:T(8,128)(2,1)S(1)}, bf16[128,2048]{1,0:T(8,128)(2,1)}, u32[]{:S(2)}) copy-start(bf16[128,2048]{1,0:T(8,128)(2,1)} %refs_0_.3) | copy-start | bytes 1572868
  12.3 8.7 %collective-permute-start.3 = (bf16[512,128]{1,0:T(8,128)(2,1)S(1)}, bf16[512,128]{1,0:T(8,128)(2,1)S(1)}, u32[]{:S(2)}, u32[]{:S(2)}) collective-permute-start(bf16[512,128]{1,0:T(8,128)(2,1)S(1)} %get-tuple-element.67), channel_id=1, source_target_pairs={{0,4},{4,0},{8,12},{12,8},{16,20},{20,16},{24,28},{28,24},{1,5},{5... | collective-permute-start | bytes 393224 | tf_op jit(solution)/shard_map/ppermute | solution.py:24
  12.8 12.4 %collective-permute-start.4 = (bf16[512,128]{1,0:T(8,128)(2,1)S(1)}, bf16[512,128]{1,0:T(8,128)(2,1)S(1)}, u32[]{:S(2)}, u32[]{:S(2)}) collective-permute-start(bf16[512,128]{1,0:T(8,128)(2,1)S(1)} %get-tuple-element.68), channel_id=1, source_target_pairs={{0,8},{4,12},{8,0},{12,4},{16,24},{20,28},{24,16},{28,20},{1,9},{5... | collective-permute-start | bytes 393224 | tf_op jit(solution)/shard_map/ppermute | solution.py:24
  14.4 13.6 %collective-permute-start.5 = (bf16[512,128]{1,0:T(8,128)(2,1)S(1)}, bf16[512,128]{1,0:T(8,128)(2,1)S(1)}, u32[]{:S(2)}, u32[]{:S(2)}) collective-permute-start(bf16[512,128]{1,0:T(8,128)(2,1)S(1)} %get-tuple-element.69), channel_id=1, source_target_pairs={{0,12},{4,8},{8,4},{12,0},{16,28},{20,24},{24,20},{28,16},{1,13},{... | collective-permute-start | bytes 393224 | tf_op jit(solution)/shard_map/ppermute | solution.py:24
  16.8 1.0 %copy-start.1 = (bf16[128,2048]{1,0:T(8,128)(2,1)S(1)}, bf16[128,2048]{1,0:T(8,128)(2,1)}, u32[]{:S(2)}) copy-start(bf16[128,2048]{1,0:T(8,128)(2,1)} %refs_0_.2) | copy-start | bytes 1572868
  18.8 13.2 %collective-permute-start = (bf16[528,128]{1,0:T(8,128)(2,1)S(1)}, bf16[528,128]{1,0:T(8,128)(2,1)S(1)}, u32[]{:S(2)}, u32[]{:S(2)}) collective-permute-start(bf16[528,128]{1,0:T(8,128)(2,1)S(1)} %get-tuple-element.55), channel_id=1, source_target_pairs={{0,4},{4,0},{8,12},{12,8},{16,20},{20,16},{24,28},{28,24},{1,5},{5... | collective-permute-start | bytes 405512 | tf_op jit(solution)/shard_map/ppermute | solution.py:24
  19.3 13.3 %collective-permute-start.1 = (bf16[528,128]{1,0:T(8,128)(2,1)S(1)}, bf16[528,128]{1,0:T(8,128)(2,1)S(1)}, u32[]{:S(2)}, u32[]{:S(2)}) collective-permute-start(bf16[528,128]{1,0:T(8,128)(2,1)S(1)} %get-tuple-element.56), channel_id=1, source_target_pairs={{0,8},{4,12},{8,0},{12,4},{16,24},{20,28},{24,16},{28,20},{1,9},{5... | collective-permute-start | bytes 405512 | tf_op jit(solution)/shard_map/ppermute | solution.py:24
  21.0 14.8 %collective-permute-start.2 = (bf16[528,128]{1,0:T(8,128)(2,1)S(1)}, bf16[528,128]{1,0:T(8,128)(2,1)S(1)}, u32[]{:S(2)}, u32[]{:S(2)}) collective-permute-start(bf16[528,128]{1,0:T(8,128)(2,1)S(1)} %get-tuple-element.57), channel_id=1, source_target_pairs={{0,12},{4,8},{8,4},{12,0},{16,28},{20,24},{24,20},{28,16},{1,13},{... | collective-permute-start | bytes 405512 | tf_op jit(solution)/shard_map/ppermute | solution.py:24
  28.1 8.4 %collective-permute-start.8 = (bf16[512,128]{1,0:T(8,128)(2,1)S(1)}, bf16[512,128]{1,0:T(8,128)(2,1)S(1)}, u32[]{:S(2)}, u32[]{:S(2)}) collective-permute-start(bf16[512,128]{1,0:T(8,128)(2,1)S(1)} %get-tuple-element.74), channel_id=1, source_target_pairs={{0,3},{1,2},{2,1},{3,0},{4,7},{5,6},{6,5},{7,4},{8,11},{9,10},{10,... | collective-permute-start | bytes 393224 | tf_op jit(solution)/shard_map/ppermute | solution.py:24
  31.9 21.2 %collective-permute-start.6 = (bf16[512,128]{1,0:T(8,128)(2,1)S(1)}, bf16[512,128]{1,0:T(8,128)(2,1)S(1)}, u32[]{:S(2)}, u32[]{:S(2)}) collective-permute-start(bf16[512,128]{1,0:T(8,128)(2,1)S(1)} %get-tuple-element.71), channel_id=1, source_target_pairs={{0,1},{1,0},{2,3},{3,2},{4,5},{5,4},{6,7},{7,6},{8,9},{9,8},{10,11... | collective-permute-start | bytes 393224 | tf_op jit(solution)/shard_map/ppermute | solution.py:24
  31.9 21.2 %collective-permute-start.7 = (bf16[512,128]{1,0:T(8,128)(2,1)S(1)}, bf16[512,128]{1,0:T(8,128)(2,1)S(1)}, u32[]{:S(2)}, u32[]{:S(2)}) collective-permute-start(bf16[512,128]{1,0:T(8,128)(2,1)S(1)} %get-tuple-element.72), channel_id=1, source_target_pairs={{0,2},{1,3},{2,0},{3,1},{4,6},{5,7},{6,4},{7,5},{8,10},{9,11},{10,... | collective-permute-start | bytes 393224 | tf_op jit(solution)/shard_map/ppermute | solution.py:24
  36.4 21.6 %collective-permute-start.10 = (bf16[512,128]{1,0:T(8,128)(2,1)S(1)}, bf16[512,128]{1,0:T(8,128)(2,1)S(1)}, u32[]{:S(2)}, u32[]{:S(2)}) collective-permute-start(bf16[512,128]{1,0:T(8,128)(2,1)S(1)} %get-tuple-element.78), channel_id=1, source_target_pairs={{0,2},{1,3},{2,0},{3,1},{4,6},{5,7},{6,4},{7,5},{8,10},{9,11},{10,... | collective-permute-start | bytes 393224 | tf_op jit(solution)/shard_map/ppermute | solution.py:24
  46.6 13.8 %collective-permute-start.11 = (bf16[512,128]{1,0:T(8,128)(2,1)S(1)}, bf16[512,128]{1,0:T(8,128)(2,1)S(1)}, u32[]{:S(2)}, u32[]{:S(2)}) collective-permute-start(bf16[512,128]{1,0:T(8,128)(2,1)S(1)} %get-tuple-element.79), channel_id=1, source_target_pairs={{0,3},{1,2},{2,1},{3,0},{4,7},{5,6},{6,5},{7,4},{8,11},{9,10},{10,... | collective-permute-start | bytes 393224 | tf_op jit(solution)/shard_map/ppermute | solution.py:24
  48.8 11.5 %collective-permute-start.9 = (bf16[512,128]{1,0:T(8,128)(2,1)S(1)}, bf16[512,128]{1,0:T(8,128)(2,1)S(1)}, u32[]{:S(2)}, u32[]{:S(2)}) collective-permute-start(bf16[512,128]{1,0:T(8,128)(2,1)S(1)} %get-tuple-element.77), channel_id=1, source_target_pairs={{0,1},{1,0},{2,3},{3,2},{4,5},{5,4},{6,7},{7,6},{8,9},{9,8},{10,11... | collective-permute-start | bytes 393224 | tf_op jit(solution)/shard_map/ppermute | solution.py:24
  55.8 12.3 %collective-permute-start.12 = (bf16[512,128]{1,0:T(8,128)(2,1)S(1)}, bf16[512,128]{1,0:T(8,128)(2,1)S(1)}, u32[]{:S(2)}, u32[]{:S(2)}) collective-permute-start(bf16[512,128]{1,0:T(8,128)(2,1)S(1)} %get-tuple-element.83), channel_id=1, source_target_pairs={{0,1},{1,0},{2,3},{3,2},{4,5},{5,4},{6,7},{7,6},{8,9},{9,8},{10,11... | collective-permute-start | bytes 393224 | tf_op jit(solution)/shard_map/ppermute | solution.py:24
  57.9 11.0 %collective-permute-start.13 = (bf16[512,128]{1,0:T(8,128)(2,1)S(1)}, bf16[512,128]{1,0:T(8,128)(2,1)S(1)}, u32[]{:S(2)}, u32[]{:S(2)}) collective-permute-start(bf16[512,128]{1,0:T(8,128)(2,1)S(1)} %get-tuple-element.84), channel_id=1, source_target_pairs={{0,2},{1,3},{2,0},{3,1},{4,6},{5,7},{6,4},{7,5},{8,10},{9,11},{10,... | collective-permute-start | bytes 393224 | tf_op jit(solution)/shard_map/ppermute | solution.py:24
  58.0 10.9 %collective-permute-start.14 = (bf16[512,128]{1,0:T(8,128)(2,1)S(1)}, bf16[512,128]{1,0:T(8,128)(2,1)S(1)}, u32[]{:S(2)}, u32[]{:S(2)}) collective-permute-start(bf16[512,128]{1,0:T(8,128)(2,1)S(1)} %get-tuple-element.85), channel_id=1, source_target_pairs={{0,3},{1,2},{2,1},{3,0},{4,7},{5,6},{6,5},{7,4},{8,11},{9,10},{10,... | collective-permute-start | bytes 393224 | tf_op jit(solution)/shard_map/ppermute | solution.py:24
  68.9 27.7 %all-to-all-start.1 = ((bf16[16,256,128]{2,1,0:T(8,128)(2,1)}), bf16[16,256,128]{2,1,0:T(8,128)(2,1)S(1)}, u32[]{:S(2)}, u32[]{:S(2)}) async-start(bf16[16,256,128]{2,1,0:T(8,128)(2,1)} %bitcast.5), calls=%async_computation.1 | async-start | bytes 2097152 | tf_op jit(solution)/shard_map/all_to_all | solution.py:340
  73.7 2.2 %collective-permute-start.15 = (bf16[512,128]{1,0:T(8,128)(2,1)S(1)}, bf16[512,128]{1,0:T(8,128)(2,1)S(1)}, u32[]{:S(2)}, u32[]{:S(2)}) collective-permute-start(bf16[512,128]{1,0:T(8,128)(2,1)S(1)} %get-tuple-element.94), channel_id=1, source_target_pairs={{0,4},{4,0},{8,12},{12,8},{16,20},{20,16},{24,28},{28,24},{1,5},{5... | collective-permute-start | bytes 393224 | tf_op jit(solution)/shard_map/ppermute | solution.py:24
  74.2 14.2 %collective-permute-start.16 = (bf16[512,128]{1,0:T(8,128)(2,1)S(1)}, bf16[512,128]{1,0:T(8,128)(2,1)S(1)}, u32[]{:S(2)}, u32[]{:S(2)}) collective-permute-start(bf16[512,128]{1,0:T(8,128)(2,1)S(1)} %get-tuple-element.95), channel_id=1, source_target_pairs={{0,8},{4,12},{8,0},{12,4},{16,24},{20,28},{24,16},{28,20},{1,9},{5... | collective-permute-start | bytes 393224 | tf_op jit(solution)/shard_map/ppermute | solution.py:24
  75.9 14.5 %collective-permute-start.17 = (bf16[512,128]{1,0:T(8,128)(2,1)S(1)}, bf16[512,128]{1,0:T(8,128)(2,1)S(1)}, u32[]{:S(2)}, u32[]{:S(2)}) collective-permute-start(bf16[512,128]{1,0:T(8,128)(2,1)S(1)} %get-tuple-element.96), channel_id=1, source_target_pairs={{0,12},{4,8},{8,4},{12,0},{16,28},{20,24},{24,20},{28,16},{1,13},{... | collective-permute-start | bytes 393224 | tf_op jit(solution)/shard_map/ppermute | solution.py:24

commit v6 on v4

--- a/solution.py
+++ b/solution.py
@@ -292,7 +292,6 @@
         (),
         over_ctx(value),
     )
-    joined, value = lax.optimization_barrier((joined, value))
     middle, last = parts // 2, parts - 1
     value[middle], grad[last] = lax.optimization_barrier((value[middle], grad[last]))
     value = over_head(value)

time: 99.5 us -> 99.7 us (level)
  starting transfers between devices: 40.1 us -> 41.4 us
  waiting for transfers between devices: 30.9 us -> 29.7 us
    ppermute x18, waiting for transfers between devices: 26.1 us -> 25 us  [swapped(): lax.ppermute(value, axis, [(i, i ^ distance) for i in range(lax.axis_size...]
    ppermute x18, starting transfers between devices: 28 us -> 29 us  [swapped(): lax.ppermute(value, axis, [(i, i ^ distance) for i in range(lax.axis_size...]
  transfers between devices with their start and end apart: 20 -> 20, of which waited for: 8 -> 7; matrix products, arithmetic and copies ran while one was open for 2% -> 2% of each run, Pallas kernels for 18% -> 18%
where the time goes in v6:
time: 99.7 us; the launch traced here: 98 us
  starting transfers between devices  41.4 us (42%)
  waiting for transfers between devices  29.7 us (30%)
  Pallas kernels  21.7 us (22%)
  local copies, waits for them, and re-layouts  4.39 us (4%)
    ppermute x18, starting transfers between devices, swapped(): lax.ppermute(value, axis, [(i, i ^ distance) for i in range(lax.axis_size...  29 us
    ppermute x18, waiting for transfers between devices, swapped(): lax.ppermute(value, axis, [(i, i ^ distance) for i in range(lax.axis_size...  25 us
    pallas_call x11, Pallas kernels, local_call(): pl.pallas_call(kernel, out_shape=out_shape, in_specs=[IN_SMEM] * len(scal...  21.7 us
    all_to_all x2, starting transfers between devices, whole_cluster(): joined = exchange(joined)  12.4 us
    all_to_all x2, waiting for transfers between devices, whole_cluster(): joined = exchange(joined)  4.78 us
    optimization_barrier x3, local copies, waits for them, and re-layouts, whole_cluster(): joined, later = lax.optimization_barrier((joined, later))  2.31 us
    unnamed x4, local copies, waits for them, and re-layouts  2.08 us
  transfers between devices with their start and end apart: 20, of which 7 were waited for; matrix products, arithmetic and copies ran while one was open for 2% of the time, Pallas kernels for 18%

profile of v6, /device:TPU:0, one launch (start us, length us, event | category | flops | bytes accessed | tf_op | source)
XLA Modules:
  0.0 98.0 jit_solution(5665728595588714530)
XLA Ops:
  0.6 2.5 %pack_natural.1 = bf16[4096,128]{1,0:T(8,128)(2,1)} custom-call(bf16[128,2048]{1,0:T(8,128)(2,1)} %refs_0_.1, bf16[128,2048]{1,0:T(8,128)(2,1)} %refs_1_.1), custom_call_target="tpu_custom_call" | custom-call | bytes 2097152 | tf_op jit(solution)/shard_map/pack_natural/pallas_call | solution.py:37
  3.1 7.4 %all-to-all-start = ((bf16[16,256,128]{2,1,0:T(8,128)(2,1)}), bf16[16,256,128]{2,1,0:T(8,128)(2,1)S(1)}, u32[]{:S(2)}, u32[]{:S(2)}) async-start(bf16[16,256,128]{2,1,0:T(8,128)(2,1)} %bitcast.10), calls=%async_computation | async-start | bytes 2097152 | tf_op jit(solution)/shard_map/all_to_all | solution.py:277
  10.5 0.1 pad_add_fusion.me_ref
  10.6 1.0 %copy-done = bf16[128,2048]{1,0:T(8,128)(2,1)S(1)} copy-done((bf16[128,2048]{1,0:T(8,128)(2,1)S(1)}, bf16[128,2048]{1,0:T(8,128)(2,1)}, u32[]{:S(2)}) %copy-start) | copy-done | bytes 524312
  11.6 0.7 pack.1
  12.3 0.5 collective-permute-start.3
  12.8 1.7 %collective-permute-start.4 = (bf16[512,128]{1,0:T(8,128)(2,1)S(1)}, bf16[512,128]{1,0:T(8,128)(2,1)S(1)}, u32[]{:S(2)}, u32[]{:S(2)}) collective-permute-start(bf16[512,128]{1,0:T(8,128)(2,1)S(1)} %get-tuple-element.58), channel_id=1, source_target_pairs={{0,8},{4,12},{8,0},{12,4},{16,24},{20,28},{24,16},{28,20},{1,9},{5... | collective-permute-start | bytes 393224 | tf_op jit(solution)/shard_map/ppermute | solution.py:24
  14.4 0.8 copy.11.pool_ref
  15.2 0.8 copy.12.picks_ref
  16.0 0.8 copy.10.offsets_ref
  16.8 1.0 %copy-done.1 = bf16[128,2048]{1,0:T(8,128)(2,1)S(1)} copy-done((bf16[128,2048]{1,0:T(8,128)(2,1)S(1)}, bf16[128,2048]{1,0:T(8,128)(2,1)}, u32[]{:S(2)}) %copy-start.1) | copy-done | bytes 524312
  17.8 1.0 pack_with_index.1
  18.8 0.5 collective-permute-start
  19.3 1.7 %collective-permute-start.1 = (bf16[528,128]{1,0:T(8,128)(2,1)S(1)}, bf16[528,128]{1,0:T(8,128)(2,1)S(1)}, u32[]{:S(2)}, u32[]{:S(2)}) collective-permute-start(bf16[528,128]{1,0:T(8,128)(2,1)S(1)} %get-tuple-element.51), channel_id=1, source_target_pairs={{0,8},{4,12},{8,0},{12,4},{16,24},{20,28},{24,16},{28,20},{1,9},{5... | collective-permute-start | bytes 405512 | tf_op jit(solution)/shard_map/ppermute | solution.py:24
  21.0 4.2 %collective-permute-done.4.refs_2_ = bf16[512,128]{1,0:T(8,128)(2,1)S(1)} collective-permute-done((bf16[512,128]{1,0:T(8,128)(2,1)S(1)}, bf16[512,128]{1,0:T(8,128)(2,1)S(1)}, u32[]{:S(2)}, u32[]{:S(2)}) %collective-permute-start.4) | collective-permute-done | bytes 131104 | tf_op jit(solution)/shard_map/ppermute | solution.py:24
  25.1 2.9 %collective-permute-done.5.refs_3_ = bf16[512,128]{1,0:T(8,128)(2,1)S(1)} collective-permute-done((bf16[512,128]{1,0:T(8,128)(2,1)S(1)}, bf16[512,128]{1,0:T(8,128)(2,1)S(1)}, u32[]{:S(2)}, u32[]{:S(2)}) %collective-permute-start.5) | collective-permute-done | bytes 131104 | tf_op jit(solution)/shard_map/ppermute | solution.py:24
  28.1 3.9 %collective-permute-start.8 = (bf16[512,128]{1,0:T(8,128)(2,1)S(1)}, bf16[512,128]{1,0:T(8,128)(2,1)S(1)}, u32[]{:S(2)}, u32[]{:S(2)}) collective-permute-start(bf16[512,128]{1,0:T(8,128)(2,1)S(1)} %get-tuple-element.64), channel_id=1, source_target_pairs={{0,3},{1,2},{2,1},{3,0},{4,7},{5,6},{6,5},{7,4},{8,11},{9,10},{10,... | collective-permute-start | bytes 393224 | tf_op jit(solution)/shard_map/ppermute | solution.py:24
  31.9 0.0 collective-permute-start.6
  31.9 0.0 collective-permute-done.refs_1_
  31.9 0.6 collective-permute-start.7
  32.6 0.0 collective-permute-done.1.refs_2_
  32.6 3.2 %collective-permute-done.2.refs_3_ = bf16[528,128]{1,0:T(8,128)(2,1)S(1)} collective-permute-done((bf16[528,128]{1,0:T(8,128)(2,1)S(1)}, bf16[528,128]{1,0:T(8,128)(2,1)S(1)}, u32[]{:S(2)}, u32[]{:S(2)}) %collective-permute-start.2) | collective-permute-done | bytes 135200 | tf_op jit(solution)/shard_map/ppermute | solution.py:24
  35.8 3.1 %collective-permute-start.11 = (bf16[512,128]{1,0:T(8,128)(2,1)S(1)}, bf16[512,128]{1,0:T(8,128)(2,1)S(1)}, u32[]{:S(2)}, u32[]{:S(2)}) collective-permute-start(bf16[512,128]{1,0:T(8,128)(2,1)S(1)} %get-tuple-element.69), channel_id=1, source_target_pairs={{0,3},{1,2},{2,1},{3,0},{4,7},{5,6},{6,5},{7,4},{8,11},{9,10},{10,... | collective-permute-start | bytes 393224 | tf_op jit(solution)/shard_map/ppermute | solution.py:24
  38.9 0.0 collective-permute-start.9
  38.9 0.0 collective-permute-done.8.refs_3_
  38.9 10.5 %collective-permute-start.10 = (bf16[512,128]{1,0:T(8,128)(2,1)S(1)}, bf16[512,128]{1,0:T(8,128)(2,1)S(1)}, u32[]{:S(2)}, u32[]{:S(2)}) collective-permute-start(bf16[512,128]{1,0:T(8,128)(2,1)S(1)} %get-tuple-element.68), channel_id=1, source_target_pairs={{0,2},{1,3},{2,0},{3,1},{4,6},{5,7},{6,4},{7,5},{8,10},{9,11},{10,... | collective-permute-start | bytes 393224 | tf_op jit(solution)/shard_map/ppermute | solution.py:24
  49.4 0.0 all-to-all-done
  49.4 4.3 %softmax_weights.1 = (f32[8,768,256]{2,1,0:T(8,128)S(1)}, bf16[8,768,256]{2,1,0:T(8,128)(2,1)S(1)}) custom-call(s32[3]{0:T(128)S(1)} %pad_add_fusion.me_ref, s32[64,128]{1,0:T(8,128)S(1)} %get-tuple-element.53.index_ref, bf16[4096,128]{1,0:T(8,128)(2,1)S(1)} %bitcast.7), custom_call_target="tpu_custom_call" | custom-call | flops 402653184 | bytes 10485760 | tf_op jit(solution)/shard_map/softmax_weights/pallas_call | solution.py:37
  53.7 0.0 collective-permute-done.7.refs_2_
  53.7 2.6 %dv_parts.1 = (bf16[512,128]{1,0:T(8,128)(2,1)S(1)}, bf16[512,128]{1,0:T(8,128)(2,1)S(1)}, bf16[512,128]{1,0:T(8,128)(2,1)S(1)}, bf16[512,128]{1,0:T(8,128)(2,1)S(1)}) custom-call(s32[3]{0:T(128)S(1)} %pad_add_fusion.me_ref, s32[64,128]{1,0:T(8,128)S(1)} %get-tuple-element.53.index_ref, bf16[8,768,256]{2,1,0:T(8,128)(2,1)S(1)} %get-tuple-element.71.half_ref, ...), custom_call_target="tpu_custom_call" | custom-call | flops 402653184 | bytes 4194304 | tf_op jit(solution)/shard_map/dv_parts/pallas_call | solution.py:37
  56.3 0.1 collective-permute-start.12
  56.4 2.8 %collective-permute-start.13 = (bf16[512,128]{1,0:T(8,128)(2,1)S(1)}, bf16[512,128]{1,0:T(8,128)(2,1)S(1)}, u32[]{:S(2)}, u32[]{:S(2)}) collective-permute-start(bf16[512,128]{1,0:T(8,128)(2,1)S(1)} %get-tuple-element.74), channel_id=1, source_target_pairs={{0,2},{1,3},{2,0},{3,1},{4,6},{5,7},{6,4},{7,5},{8,10},{9,11},{10,... | collective-permute-start | bytes 393224 | tf_op jit(solution)/shard_map/ppermute | solution.py:24
  59.2 0.0 collective-permute-done.11.refs_7_
  59.2 1.5 %collective-permute-start.14 = (bf16[512,128]{1,0:T(8,128)(2,1)S(1)}, bf16[512,128]{1,0:T(8,128)(2,1)S(1)}, u32[]{:S(2)}, u32[]{:S(2)}) collective-permute-start(bf16[512,128]{1,0:T(8,128)(2,1)S(1)} %get-tuple-element.75), channel_id=1, source_target_pairs={{0,3},{1,2},{2,1},{3,0},{4,7},{5,6},{6,5},{7,4},{8,11},{9,10},{10,... | collective-permute-start | bytes 393224 | tf_op jit(solution)/shard_map/ppermute | solution.py:24
  60.8 7.8 %dq_and_dk.1 = bf16[4096,128]{1,0:T(8,128)(2,1)} custom-call(s32[3]{0:T(128)S(1)} %pad_add_fusion.me_ref, s32[64,128]{1,0:T(8,128)S(1)} %get-tuple-element.53.index_ref, bf16[4096,128]{1,0:T(8,128)(2,1)S(1)} %bitcast.8, bf16[512,128]{1,0:T(8,128)(2,1)S(1)} %get-tuple-element.60.refs_0_, bf16[512,128]{1,0:T(8,128)(2,1)S(1)} %collective-permute-done.6.refs_1_, ...), custom_call_target="tpu_custom_call" | custom-call | flops 1207959552 | bytes 9437184 | tf_op jit(solution)/shard_map/dq_and_dk/pallas_call | solution.py:37
  68.6 0.0 collective-permute-done.12.refs_1_
  68.6 0.2 collective-permute-done.13.refs_2_
  68.8 0.0 collective-permute-done.14.refs_3_
  68.8 5.0 %all-to-all-start.1 = ((bf16[16,256,128]{2,1,0:T(8,128)(2,1)}), bf16[16,256,128]{2,1,0:T(8,128)(2,1)S(1)}, u32[]{:S(2)}, u32[]{:S(2)}) async-start(bf16[16,256,128]{2,1,0:T(8,128)(2,1)} %bitcast.5), calls=%async_computation.1 | async-start | bytes 2097152 | tf_op jit(solution)/shard_map/all_to_all | solution.py:331
  73.9 0.5 collective-permute-start.15
  74.3 1.7 %collective-permute-start.16 = (bf16[512,128]{1,0:T(8,128)(2,1)S(1)}, bf16[512,128]{1,0:T(8,128)(2,1)S(1)}, u32[]{:S(2)}, u32[]{:S(2)}) collective-permute-start(bf16[512,128]{1,0:T(8,128)(2,1)S(1)} %get-tuple-element.85), channel_id=1, source_target_pairs={{0,8},{4,12},{8,0},{12,4},{16,24},{20,28},{24,16},{28,20},{1,9},{5... | collective-permute-start | bytes 393224 | tf_op jit(solution)/shard_map/ppermute | solution.py:24
  76.0 0.0 collective-permute-start.17
  76.0 0.0 collective-permute-done.15.refs_1_
  76.0 12.5 %collective-permute-done.16.refs_2_ = bf16[512,128]{1,0:T(8,128)(2,1)S(1)} collective-permute-done((bf16[512,128]{1,0:T(8,128)(2,1)S(1)}, bf16[512,128]{1,0:T(8,128)(2,1)S(1)}, u32[]{:S(2)}, u32[]{:S(2)}) %collective-permute-start.16) | collective-permute-done | bytes 131104 | tf_op jit(solution)/shard_map/ppermute | solution.py:24
  88.5 2.0 %collective-permute-done.17.refs_3_ = bf16[512,128]{1,0:T(8,128)(2,1)S(1)} collective-permute-done((bf16[512,128]{1,0:T(8,128)(2,1)S(1)}, bf16[512,128]{1,0:T(8,128)(2,1)S(1)}, u32[]{:S(2)}, u32[]{:S(2)}) %collective-permute-start.17) | collective-permute-done | bytes 131104 | tf_op jit(solution)/shard_map/ppermute | solution.py:24
  90.5 1.5 %unpack.1 = bf16[128,2048]{1,0:T(8,128)(2,1)} custom-call(s32[3]{0:T(128)S(1)} %pad_add_fusion.me_ref, bf16[512,128]{1,0:T(8,128)(2,1)S(1)} %get-tuple-element.83.refs_0_, bf16[512,128]{1,0:T(8,128)(2,1)S(1)} %collective-permute-done.15.refs_1_, bf16[512,128]{1,0:T(8,128)(2,1)S(1)} %collective-permute-done.16.refs_2_, ...), custom_call_target="tpu_custom_call" | custom-call | bytes 1048576 | tf_op jit(solution)/shard_map/unpack/pallas_call | solution.py:37
  92.0 4.8 %all-to-all-done.1 = bf16[16,256,128]{2,1,0:T(8,128)(2,1)S(1)} async-done(((bf16[16,256,128]{2,1,0:T(8,128)(2,1)}), bf16[16,256,128]{2,1,0:T(8,128)(2,1)S(1)}, u32[]{:S(2)}, u32[]{:S(2)}) %all-to-all-start.1) | async-done | bytes 1048608 | tf_op jit(solution)/shard_map/all_to_all | solution.py:331
  96.8 1.3 %unpack_natural.1 = (bf16[128,2048]{1,0:T(8,128)(2,1)}, bf16[128,2048]{1,0:T(8,128)(2,1)}) custom-call(bf16[4096,128]{1,0:T(8,128)(2,1)S(1)} %bitcast.9), custom_call_target="tpu_custom_call" | custom-call | bytes 2097152 | tf_op jit(solution)/shard_map/unpack_natural/pallas_call | solution.py:37
  (11 shorter events, 0.1 us)
Async XLA Ops:
  3.1 46.3 %all-to-all-start = ((bf16[16,256,128]{2,1,0:T(8,128)(2,1)}), bf16[16,256,128]{2,1,0:T(8,128)(2,1)S(1)}, u32[]{:S(2)}, u32[]{:S(2)}) async-start(bf16[16,256,128]{2,1,0:T(8,128)(2,1)} %bitcast.10), calls=%async_computation | async-start | bytes 2097152 | tf_op jit(solution)/shard_map/all_to_all | solution.py:277
  10.6 1.0 %copy-start = (bf16[128,2048]{1,0:T(8,128)(2,1)S(1)}, bf16[128,2048]{1,0:T(8,128)(2,1)}, u32[]{:S(2)}) copy-start(bf16[128,2048]{1,0:T(8,128)(2,1)} %refs_0_.3) | copy-start | bytes 1572868
  12.3 8.7 %collective-permute-start.3 = (bf16[512,128]{1,0:T(8,128)(2,1)S(1)}, bf16[512,128]{1,0:T(8,128)(2,1)S(1)}, u32[]{:S(2)}, u32[]{:S(2)}) collective-permute-start(bf16[512,128]{1,0:T(8,128)(2,1)S(1)} %get-tuple-element.57), channel_id=1, source_target_pairs={{0,4},{4,0},{8,12},{12,8},{16,20},{20,16},{24,28},{28,24},{1,5},{5... | collective-permute-start | bytes 393224 | tf_op jit(solution)/shard_map/ppermute | solution.py:24
  12.8 12.4 %collective-permute-start.4 = (bf16[512,128]{1,0:T(8,128)(2,1)S(1)}, bf16[512,128]{1,0:T(8,128)(2,1)S(1)}, u32[]{:S(2)}, u32[]{:S(2)}) collective-permute-start(bf16[512,128]{1,0:T(8,128)(2,1)S(1)} %get-tuple-element.58), channel_id=1, source_target_pairs={{0,8},{4,12},{8,0},{12,4},{16,24},{20,28},{24,16},{28,20},{1,9},{5... | collective-permute-start | bytes 393224 | tf_op jit(solution)/shard_map/ppermute | solution.py:24
  14.4 13.6 %collective-permute-start.5 = (bf16[512,128]{1,0:T(8,128)(2,1)S(1)}, bf16[512,128]{1,0:T(8,128)(2,1)S(1)}, u32[]{:S(2)}, u32[]{:S(2)}) collective-permute-start(bf16[512,128]{1,0:T(8,128)(2,1)S(1)} %get-tuple-element.59), channel_id=1, source_target_pairs={{0,12},{4,8},{8,4},{12,0},{16,28},{20,24},{24,20},{28,16},{1,13},{... | collective-permute-start | bytes 393224 | tf_op jit(solution)/shard_map/ppermute | solution.py:24
  16.8 1.0 %copy-start.1 = (bf16[128,2048]{1,0:T(8,128)(2,1)S(1)}, bf16[128,2048]{1,0:T(8,128)(2,1)}, u32[]{:S(2)}) copy-start(bf16[128,2048]{1,0:T(8,128)(2,1)} %refs_0_.2) | copy-start | bytes 1572868
  18.8 13.2 %collective-permute-start = (bf16[528,128]{1,0:T(8,128)(2,1)S(1)}, bf16[528,128]{1,0:T(8,128)(2,1)S(1)}, u32[]{:S(2)}, u32[]{:S(2)}) collective-permute-start(bf16[528,128]{1,0:T(8,128)(2,1)S(1)} %get-tuple-element.50), channel_id=1, source_target_pairs={{0,4},{4,0},{8,12},{12,8},{16,20},{20,16},{24,28},{28,24},{1,5},{5... | collective-permute-start | bytes 405512 | tf_op jit(solution)/shard_map/ppermute | solution.py:24
  19.3 13.3 %collective-permute-start.1 = (bf16[528,128]{1,0:T(8,128)(2,1)S(1)}, bf16[528,128]{1,0:T(8,128)(2,1)S(1)}, u32[]{:S(2)}, u32[]{:S(2)}) collective-permute-start(bf16[528,128]{1,0:T(8,128)(2,1)S(1)} %get-tuple-element.51), channel_id=1, source_target_pairs={{0,8},{4,12},{8,0},{12,4},{16,24},{20,28},{24,16},{28,20},{1,9},{5... | collective-permute-start | bytes 405512 | tf_op jit(solution)/shard_map/ppermute | solution.py:24
  21.0 14.8 %collective-permute-start.2 = (bf16[528,128]{1,0:T(8,128)(2,1)S(1)}, bf16[528,128]{1,0:T(8,128)(2,1)S(1)}, u32[]{:S(2)}, u32[]{:S(2)}) collective-permute-start(bf16[528,128]{1,0:T(8,128)(2,1)S(1)} %get-tuple-element.52), channel_id=1, source_target_pairs={{0,12},{4,8},{8,4},{12,0},{16,28},{20,24},{24,20},{28,16},{1,13},{... | collective-permute-start | bytes 405512 | tf_op jit(solution)/shard_map/ppermute | solution.py:24
  28.1 10.8 %collective-permute-start.8 = (bf16[512,128]{1,0:T(8,128)(2,1)S(1)}, bf16[512,128]{1,0:T(8,128)(2,1)S(1)}, u32[]{:S(2)}, u32[]{:S(2)}) collective-permute-start(bf16[512,128]{1,0:T(8,128)(2,1)S(1)} %get-tuple-element.64), channel_id=1, source_target_pairs={{0,3},{1,2},{2,1},{3,0},{4,7},{5,6},{6,5},{7,4},{8,11},{9,10},{10,... | collective-permute-start | bytes 393224 | tf_op jit(solution)/shard_map/ppermute | solution.py:24
  31.9 21.7 %collective-permute-start.6 = (bf16[512,128]{1,0:T(8,128)(2,1)S(1)}, bf16[512,128]{1,0:T(8,128)(2,1)S(1)}, u32[]{:S(2)}, u32[]{:S(2)}) collective-permute-start(bf16[512,128]{1,0:T(8,128)(2,1)S(1)} %get-tuple-element.61), channel_id=1, source_target_pairs={{0,1},{1,0},{2,3},{3,2},{4,5},{5,4},{6,7},{7,6},{8,9},{9,8},{10,11... | collective-permute-start | bytes 393224 | tf_op jit(solution)/shard_map/ppermute | solution.py:24
  31.9 21.7 %collective-permute-start.7 = (bf16[512,128]{1,0:T(8,128)(2,1)S(1)}, bf16[512,128]{1,0:T(8,128)(2,1)S(1)}, u32[]{:S(2)}, u32[]{:S(2)}) collective-permute-start(bf16[512,128]{1,0:T(8,128)(2,1)S(1)} %get-tuple-element.62), channel_id=1, source_target_pairs={{0,2},{1,3},{2,0},{3,1},{4,6},{5,7},{6,4},{7,5},{8,10},{9,11},{10,... | collective-permute-start | bytes 393224 | tf_op jit(solution)/shard_map/ppermute | solution.py:24
  35.8 23.4 %collective-permute-start.11 = (bf16[512,128]{1,0:T(8,128)(2,1)S(1)}, bf16[512,128]{1,0:T(8,128)(2,1)S(1)}, u32[]{:S(2)}, u32[]{:S(2)}) collective-permute-start(bf16[512,128]{1,0:T(8,128)(2,1)S(1)} %get-tuple-element.69), channel_id=1, source_target_pairs={{0,3},{1,2},{2,1},{3,0},{4,7},{5,6},{6,5},{7,4},{8,11},{9,10},{10,... | collective-permute-start | bytes 393224 | tf_op jit(solution)/shard_map/ppermute | solution.py:24
  38.9 21.9 %collective-permute-start.9 = (bf16[512,128]{1,0:T(8,128)(2,1)S(1)}, bf16[512,128]{1,0:T(8,128)(2,1)S(1)}, u32[]{:S(2)}, u32[]{:S(2)}) collective-permute-start(bf16[512,128]{1,0:T(8,128)(2,1)S(1)} %get-tuple-element.67), channel_id=1, source_target_pairs={{0,1},{1,0},{2,3},{3,2},{4,5},{5,4},{6,7},{7,6},{8,9},{9,8},{10,11... | collective-permute-start | bytes 393224 | tf_op jit(solution)/shard_map/ppermute | solution.py:24
  38.9 21.9 %collective-permute-start.10 = (bf16[512,128]{1,0:T(8,128)(2,1)S(1)}, bf16[512,128]{1,0:T(8,128)(2,1)S(1)}, u32[]{:S(2)}, u32[]{:S(2)}) collective-permute-start(bf16[512,128]{1,0:T(8,128)(2,1)S(1)} %get-tuple-element.68), channel_id=1, source_target_pairs={{0,2},{1,3},{2,0},{3,1},{4,6},{5,7},{6,4},{7,5},{8,10},{9,11},{10,... | collective-permute-start | bytes 393224 | tf_op jit(solution)/shard_map/ppermute | solution.py:24
  56.3 12.3 %collective-permute-start.12 = (bf16[512,128]{1,0:T(8,128)(2,1)S(1)}, bf16[512,128]{1,0:T(8,128)(2,1)S(1)}, u32[]{:S(2)}, u32[]{:S(2)}) collective-permute-start(bf16[512,128]{1,0:T(8,128)(2,1)S(1)} %get-tuple-element.73), channel_id=1, source_target_pairs={{0,1},{1,0},{2,3},{3,2},{4,5},{5,4},{6,7},{7,6},{8,9},{9,8},{10,11... | collective-permute-start | bytes 393224 | tf_op jit(solution)/shard_map/ppermute | solution.py:24
  56.4 12.4 %collective-permute-start.13 = (bf16[512,128]{1,0:T(8,128)(2,1)S(1)}, bf16[512,128]{1,0:T(8,128)(2,1)S(1)}, u32[]{:S(2)}, u32[]{:S(2)}) collective-permute-start(bf16[512,128]{1,0:T(8,128)(2,1)S(1)} %get-tuple-element.74), channel_id=1, source_target_pairs={{0,2},{1,3},{2,0},{3,1},{4,6},{5,7},{6,4},{7,5},{8,10},{9,11},{10,... | collective-permute-start | bytes 393224 | tf_op jit(solution)/shard_map/ppermute | solution.py:24
  59.2 9.6 %collective-permute-start.14 = (bf16[512,128]{1,0:T(8,128)(2,1)S(1)}, bf16[512,128]{1,0:T(8,128)(2,1)S(1)}, u32[]{:S(2)}, u32[]{:S(2)}) collective-permute-start(bf16[512,128]{1,0:T(8,128)(2,1)S(1)} %get-tuple-element.75), channel_id=1, source_target_pairs={{0,3},{1,2},{2,1},{3,0},{4,7},{5,6},{6,5},{7,4},{8,11},{9,10},{10,... | collective-permute-start | bytes 393224 | tf_op jit(solution)/shard_map/ppermute | solution.py:24
  68.8 28.0 %all-to-all-start.1 = ((bf16[16,256,128]{2,1,0:T(8,128)(2,1)}), bf16[16,256,128]{2,1,0:T(8,128)(2,1)S(1)}, u32[]{:S(2)}, u32[]{:S(2)}) async-start(bf16[16,256,128]{2,1,0:T(8,128)(2,1)} %bitcast.5), calls=%async_computation.1 | async-start | bytes 2097152 | tf_op jit(solution)/shard_map/all_to_all | solution.py:331
  73.9 2.2 %collective-permute-start.15 = (bf16[512,128]{1,0:T(8,128)(2,1)S(1)}, bf16[512,128]{1,0:T(8,128)(2,1)S(1)}, u32[]{:S(2)}, u32[]{:S(2)}) collective-permute-start(bf16[512,128]{1,0:T(8,128)(2,1)S(1)} %get-tuple-element.84), channel_id=1, source_target_pairs={{0,4},{4,0},{8,12},{12,8},{16,20},{20,16},{24,28},{28,24},{1,5},{5... | collective-permute-start | bytes 393224 | tf_op jit(solution)/shard_map/ppermute | solution.py:24
  74.3 14.2 %collective-permute-start.16 = (bf16[512,128]{1,0:T(8,128)(2,1)S(1)}, bf16[512,128]{1,0:T(8,128)(2,1)S(1)}, u32[]{:S(2)}, u32[]{:S(2)}) collective-permute-start(bf16[512,128]{1,0:T(8,128)(2,1)S(1)} %get-tuple-element.85), channel_id=1, source_target_pairs={{0,8},{4,12},{8,0},{12,4},{16,24},{20,28},{24,16},{28,20},{1,9},{5... | collective-permute-start | bytes 393224 | tf_op jit(solution)/shard_map/ppermute | solution.py:24
  76.0 14.5 %collective-permute-start.17 = (bf16[512,128]{1,0:T(8,128)(2,1)S(1)}, bf16[512,128]{1,0:T(8,128)(2,1)S(1)}, u32[]{:S(2)}, u32[]{:S(2)}) collective-permute-start(bf16[512,128]{1,0:T(8,128)(2,1)S(1)} %get-tuple-element.86), channel_id=1, source_target_pairs={{0,12},{4,8},{8,4},{12,0},{16,28},{20,24},{24,20},{28,16},{1,13},{... | collective-permute-start | bytes 393224 | tf_op jit(solution)/shard_map/ppermute | solution.py:24
